TPU v7x, 128 devices: a whole 4x4x4 slice. The times are simulated.
128 devices in a mesh: batch: 128 (over y, z, x, core).
Axes of the slice: x: 4, y: 4, z: 4, core: 2. Of those that a mesh axis runs over, the one named last changes fastest.
Arguments:
- tokens: bfloat16 [65536, 256], P('batch'), may hold values from -5 to 5
- labels: int32 [65536, 2], P('batch'), may hold values from 0 to 1
- lengths: int32 [512], replicated, may hold values from 1 to 200, 65536 in all
- codes_one: bfloat16 [256, 32], replicated, may hold values from -0.375 to 0.375
- mixing_one: bfloat16 [256, 8], replicated, may hold values from -0.1875 to 0.1875
- inner_one: bfloat16 [256, 4096], replicated, may hold values from -0.375 to 0.375
- inner_bias_one: bfloat16 [4096], replicated, may hold values from -1.5 to 1.5
- outer_one: bfloat16 [16, 256, 256], replicated, may hold values from -1.5 to 1.5
- outer_bias_one: bfloat16 [16, 256], replicated, may hold values from -3 to 3
- codes_two: bfloat16 [256, 32], replicated, may hold values from -0.75 to 0.75
- mixing_two: bfloat16 [256, 8], replicated, may hold values from -0.375 to 0.375
- inner_two: bfloat16 [256, 4096], replicated, may hold values from -0.75 to 0.75
- inner_bias_two: bfloat16 [4096], replicated, may hold values from -1.5 to 1.5
- outer_two: bfloat16 [16, 256, 256], replicated, may hold values from -1.5 to 1.5
- outer_bias_two: bfloat16 [16, 256], replicated, may hold values from -3 to 3
- tower_inner: bfloat16 [2, 256, 128], replicated, may hold values from -0.75 to 0.75
- tower_inner_bias: bfloat16 [2, 128], replicated, may hold values from -1.5 to 1.5
- tower_outer: bfloat16 [2, 128], replicated, may hold values from -1 to 1
- tower_outer_bias: bfloat16 [2], replicated, may hold values from 1 to 2
Outputs:
- predictions: float32 [65536, 2], P('batch')
- grad_tokens: float32 [65536, 256], P('batch')
- grad_codes_one: float32 [256, 32], replicated
- grad_mixing_one: float32 [256, 8], replicated
- grad_inner_one: float32 [256, 4096], replicated
- grad_inner_bias_one: float32 [4096], replicated
- grad_outer_one: float32 [16, 256, 256], replicated
- grad_outer_bias_one: float32 [16, 256], replicated
- grad_codes_two: float32 [256, 32], replicated
- grad_mixing_two: float32 [256, 8], replicated
- grad_inner_two: float32 [256, 4096], replicated
- grad_inner_bias_two: float32 [4096], replicated
- grad_outer_two: float32 [16, 256, 256], replicated
- grad_outer_bias_two: float32 [16, 256], replicated
- grad_tower_inner: float32 [2, 256, 128], replicated
- grad_tower_inner_bias: float32 [2, 128], replicated
- grad_tower_outer: float32 [2, 128], replicated
- grad_tower_outer_bias: float32 [2], replicated
Inputs may be any that keep to these rules, and one draw needn't show every extreme that they name: Session lengths sum to 65536; the longest session has exactly 200 rows.
All inputs are finite; a program needn't handle non-finite values.
Results may differ from a plain program's by a relative error of at most 0.012.
The roundings to bfloat16 on the way count: a program that leaves them out, or rounds other values in their place, can miss the bound.
Values sent between devices are 32-bit elements; how exact they have to be, the bound alone decides.
No kernel may reach another device: no remote copies, remote signals or barrier semaphores. Data moves between devices by JAX's collectives and lax.ppermute only.
A program may use at most 256 MiB of HBM per device.

v0:
```python
import jax
import jax.numpy as jnp
from jax import lax
from jax.sharding import PartitionSpec as P

EXPERTS = 16
SEL = 4
BITS = 4


highest = lax.Precision.HIGHEST
smooth_gamma = 10.0


def smooth_gates(code_logits, mixing):
    half_span = 0.5 * smooth_gamma
    clipped = jnp.clip(code_logits, -half_span, half_span)
    step_val = -2.0 / smooth_gamma**3 * clipped**3 + 1.5 / smooth_gamma * clipped + 0.5
    shaped = step_val.reshape(code_logits.shape[:-1] + (SEL, BITS, 1))
    expert_ids = jnp.arange(EXPERTS, dtype=jnp.int32)
    bit_ids = jnp.arange(BITS, dtype=jnp.int32)
    bit_table = (expert_ids[None, :] // (2**bit_ids)[:, None] % 2).astype(jnp.float32)
    factors = bit_table * shaped + (1.0 - bit_table) * (1.0 - shaped)
    select_prob = jnp.prod(factors, axis=-2)
    mix_weights = jax.nn.softmax(mixing, axis=-1)
    return jnp.sum(mix_weights[..., None] * select_prob, axis=-2)


def gelu_back(pre_act, upstream):
    _, back_fn = jax.vjp(jax.nn.gelu, pre_act)
    return back_fn(upstream)[0]


def gates_back(code_logits, mixing, grad_gates):
    _, back_fn = jax.vjp(smooth_gates, code_logits, mixing)
    grad_code, grad_mix = back_fn(grad_gates)
    return (grad_code.astype(jnp.bfloat16), grad_mix.astype(jnp.bfloat16))


def experts_forward(inputs, inner, inner_bias, outer, outer_bias):
    num_rows = inputs.shape[0]
    pre_act = jnp.dot(inputs, inner, preferred_element_type=jnp.float32) + inner_bias.astype(
        jnp.float32
    )
    hidden = (
        jax.nn.gelu(pre_act).astype(jnp.bfloat16).reshape(num_rows, outer.shape[0], outer.shape[1])
    )
    expert_out = jnp.einsum(
        "nej,ejd->ned", hidden, outer, preferred_element_type=jnp.float32
    ) + outer_bias.astype(jnp.float32)
    return (pre_act, hidden, expert_out)


def experts_backward(inputs, inner, outer, pre_act, hidden, grad_out):
    num_rows = inputs.shape[0]
    grad_outer_bias = jnp.sum(grad_out.astype(jnp.float32), axis=0)
    grad_outer = jnp.einsum("nej,ned->ejd", hidden, grad_out, preferred_element_type=jnp.float32)
    grad_hidden = jnp.einsum(
        "ned,ejd->nej", grad_out, outer, preferred_element_type=jnp.float32
    ).reshape(num_rows, -1)
    grad_pre = gelu_back(pre_act, grad_hidden).astype(jnp.bfloat16)
    grad_inner_bias = jnp.sum(grad_pre.astype(jnp.float32), axis=0)
    grad_inner = jnp.dot(inputs.T, grad_pre, preferred_element_type=jnp.float32)
    grad_inputs = jnp.dot(grad_pre, inner.T, preferred_element_type=jnp.float32)
    return (grad_inner, grad_inner_bias, grad_outer, grad_outer_bias, grad_inputs)


def on_device(
    tokens,
    labels,
    lengths,
    codes_one,
    mixing_one,
    inner_one,
    inner_bias_one,
    outer_one,
    outer_bias_one,
    codes_two,
    mixing_two,
    inner_two,
    inner_bias_two,
    outer_two,
    outer_bias_two,
    tower_inner,
    tower_inner_bias,
    tower_outer,
    tower_outer_bias,
):
    local_rows, model_width = tokens.shape
    num_tasks = labels.shape[1]
    labels_f = labels.astype(jnp.float32)
    positives = lax.psum(jnp.sum(labels_f, axis=0), "batch")
    all_rows = local_rows * lax.axis_size("batch")
    pos_ratio = (all_rows - positives) / positives
    row_ids = lax.axis_index("batch") * local_rows + jnp.arange(local_rows, dtype=jnp.int32)
    session_ends = jnp.cumsum(lengths)
    session_starts = session_ends - lengths
    inside = (
        (row_ids[:, None] >= session_starts[None, :]) & (row_ids[:, None] < session_ends[None, :])
    ).astype(jnp.float32)
    row_length = jnp.dot(inside, lengths.astype(jnp.float32), precision=highest)
    row_weight = all_rows / lengths.shape[0] / row_length
    pre_one, hid_one, out_one = experts_forward(
        tokens, inner_one, inner_bias_one, outer_one, outer_bias_one
    )
    code_one = jnp.dot(tokens, codes_one, preferred_element_type=jnp.float32).reshape(
        local_rows, num_tasks, -1
    )
    mix_one = jnp.dot(tokens, mixing_one, preferred_element_type=jnp.float32).reshape(
        local_rows, num_tasks, -1
    )
    gate_one = smooth_gates(code_one, mix_one)
    y_one = jnp.einsum("nte,ned->ntd", gate_one, out_one, precision=highest)
    u_two = y_one.astype(jnp.bfloat16)
    flat_two = u_two.reshape(local_rows * num_tasks, model_width)
    pre_two, hid_two, out_flat = experts_forward(
        flat_two, inner_two, inner_bias_two, outer_two, outer_bias_two
    )
    out_two = out_flat.reshape(local_rows, num_tasks, out_flat.shape[1], model_width)
    codes_split = codes_two.reshape(model_width, num_tasks, -1)
    mixing_split = mixing_two.reshape(model_width, num_tasks, -1)
    code_two = jnp.einsum("ntd,dtc->ntc", u_two, codes_split, preferred_element_type=jnp.float32)
    mix_two = jnp.einsum("ntd,dtc->ntc", u_two, mixing_split, preferred_element_type=jnp.float32)
    gate_two = smooth_gates(code_two, mix_two)
    y_two = jnp.einsum("nte,nted->ntd", gate_two, out_two, precision=highest)
    tower_in = y_two.astype(jnp.bfloat16)
    tower_pre = jnp.einsum(
        "ntd,tdh->nth", tower_in, tower_inner, preferred_element_type=jnp.float32
    ) + tower_inner_bias.astype(jnp.float32)
    tower_hid = jax.nn.gelu(tower_pre).astype(jnp.bfloat16)
    logit = jnp.einsum(
        "nth,th->nt", tower_hid, tower_outer, preferred_element_type=jnp.float32
    ) + tower_outer_bias.astype(jnp.float32)
    predictions = jax.nn.sigmoid(logit)
    grad_logit = row_weight[:, None] * (
        -pos_ratio * labels_f * jax.nn.sigmoid(-logit) + (1.0 - labels_f) * predictions
    )
    grad_logit = grad_logit.astype(jnp.bfloat16)
    grad_tower_outer_bias = jnp.sum(grad_logit.astype(jnp.float32), axis=0)
    grad_tower_outer = jnp.einsum(
        "nt,nth->th", grad_logit, tower_hid, preferred_element_type=jnp.float32
    )
    grad_tower_hid = jnp.einsum(
        "nt,th->nth", grad_logit, tower_outer, preferred_element_type=jnp.float32
    )
    grad_tower_pre = gelu_back(tower_pre, grad_tower_hid).astype(jnp.bfloat16)
    grad_tower_inner_bias = jnp.sum(grad_tower_pre.astype(jnp.float32), axis=0)
    grad_tower_inner = jnp.einsum(
        "ntd,nth->tdh", tower_in, grad_tower_pre, preferred_element_type=jnp.float32
    )
    grad_y_two = jnp.einsum(
        "nth,tdh->ntd", grad_tower_pre, tower_inner, preferred_element_type=jnp.float32
    )
    grad_out_two = (gate_two[..., None] * grad_y_two[:, :, None, :]).astype(jnp.bfloat16)
    grad_gate_two = jnp.einsum("nted,ntd->nte", out_two, grad_y_two, precision=highest)
    grad_code_two, grad_mix_two = gates_back(code_two, mix_two, grad_gate_two)
    grad_codes_two = jnp.einsum(
        "ntd,ntc->dtc", u_two, grad_code_two, preferred_element_type=jnp.float32
    ).reshape(model_width, -1)
    grad_mixing_two = jnp.einsum(
        "ntd,ntc->dtc", u_two, grad_mix_two, preferred_element_type=jnp.float32
    ).reshape(model_width, -1)
    grad_inner_two, grad_inner_bias_two, grad_outer_two, grad_outer_bias_two, grad_flat = (
        experts_backward(
            flat_two,
            inner_two,
            outer_two,
            pre_two,
            hid_two,
            grad_out_two.reshape(local_rows * num_tasks, out_flat.shape[1], model_width),
        )
    )
    grad_y_one = (
        grad_flat.reshape(local_rows, num_tasks, model_width)
        + jnp.einsum("ntc,dtc->ntd", grad_code_two, codes_split, preferred_element_type=jnp.float32)
        + jnp.einsum("ntc,dtc->ntd", grad_mix_two, mixing_split, preferred_element_type=jnp.float32)
    )
    upper_list = (
        grad_codes_two,
        grad_mixing_two,
        grad_inner_two,
        grad_inner_bias_two,
        grad_outer_two,
        grad_outer_bias_two,
        grad_tower_inner,
        grad_tower_inner_bias,
        grad_tower_outer,
        grad_tower_outer_bias,
    )
    grad_out_one = jnp.einsum("nte,ntd->ned", gate_one, grad_y_one, precision=highest).astype(
        jnp.bfloat16
    )
    grad_gate_one = jnp.einsum("ned,ntd->nte", out_one, grad_y_one, precision=highest)
    grad_code_one, grad_mix_one = gates_back(code_one, mix_one, grad_gate_one)
    code_flat = grad_code_one.reshape(local_rows, -1)
    mix_flat = grad_mix_one.reshape(local_rows, -1)
    grad_codes_one = jnp.dot(tokens.T, code_flat, preferred_element_type=jnp.float32)
    grad_mixing_one = jnp.dot(tokens.T, mix_flat, preferred_element_type=jnp.float32)
    grad_inner_one, grad_inner_bias_one, grad_outer_one, grad_outer_bias_one, grad_inputs = (
        experts_backward(tokens, inner_one, outer_one, pre_one, hid_one, grad_out_one)
    )
    grad_tokens = (
        grad_inputs
        + jnp.dot(code_flat, codes_one.T, preferred_element_type=jnp.float32)
        + jnp.dot(mix_flat, mixing_one.T, preferred_element_type=jnp.float32)
    )
    summed_all = lax.psum(
        (
            grad_codes_one,
            grad_mixing_one,
            grad_inner_one,
            grad_inner_bias_one,
            grad_outer_one,
            grad_outer_bias_one,
            grad_codes_two,
            grad_mixing_two,
            grad_inner_two,
            grad_inner_bias_two,
            grad_outer_two,
            grad_outer_bias_two,
            grad_tower_inner,
            grad_tower_inner_bias,
            grad_tower_outer,
            grad_tower_outer_bias,
        ),
        "batch",
    )
    lower_list = summed_all[:6]
    upper_list = summed_all[6:]
    return (
        predictions,
        grad_tokens,
        lower_list[0],
        lower_list[1],
        lower_list[2],
        lower_list[3],
        lower_list[4],
        lower_list[5],
        upper_list[0],
        upper_list[1],
        upper_list[2],
        upper_list[3],
        upper_list[4],
        upper_list[5],
        upper_list[6],
        upper_list[7],
        upper_list[8],
        upper_list[9],
    )


def solution(mesh):
    in_specs = (
        P("batch", None),
        P("batch", None),
        P(),
        P(),
        P(),
        P(),
        P(),
        P(),
        P(),
        P(),
        P(),
        P(),
        P(),
        P(),
        P(),
        P(),
        P(),
        P(),
        P(),
    )
    out_specs = (
        P("batch", None),
        P("batch", None),
        P(),
        P(),
        P(),
        P(),
        P(),
        P(),
        P(),
        P(),
        P(),
        P(),
        P(),
        P(),
        P(),
        P(),
        P(),
        P(),
    )
    return jax.shard_map(
        on_device, mesh=mesh, in_specs=in_specs, out_specs=out_specs, check_vma=False
    )
```

profile of v0, /device:TPU:1, one launch (start us, length us, event | category | flops | bytes accessed | tf_op | source)
XLA Modules:
  0.0 748.7 jit_solution(8580921904209702386)
XLA Ops:
  7.7 1.9 broadcast_clamp_fusion
  13.2 9.6 %multiply_convert_fusion.4 = (bf16[512,4096]{1,0:T(8,128)(2,1)}, f32[512,4096]{1,0:T(8,128)}) fusion(f32[4096]{0:T(1024)S(1)} %convert_element_type.119, bf16[512,256]{1,0:T(8,128)(2,1)} %param.24, bf16[256,4096]{1,0:T(8,128)(2,1)} %param.29), kind=kOutput, calls=%fused_computation.36 | convolution fusion | flops 1094713344 | bytes 14958592 | tf_op jit(solution)/shard_map/dot_general | solution.py:42
  22.9 6.6 copy.153
  29.5 4.3 add_bitcast_fusion.1
  33.8 3.2 copy-done.1
  37.0 8.1 %fusion.33 = bf16[512,2,256]{2,1,0:T(2,128)(2,1)S(1)} fusion(f32[512,2,16]{2,1,0:T(2,128)S(1)} %copy.102, f32[512,16,256]{2,0,1:T(8,128)S(1)} %add_bitcast_fusion.1), kind=kOutput, calls=%fused_computation.51 | convolution fusion | flops 50593792 | bytes 8978432 | tf_op jit(solution)/shard_map/nte,ned->ntd/dot_general | solution.py:113
  48.1 2.7 copy.151
  53.8 11.5 %multiply_convert_fusion.1 = (bf16[1024,4096]{1,0:T(8,128)(2,1)}, f32[1024,4096]{1,0:T(8,128)}) fusion(f32[4096]{0:T(1024)S(1)} %convert_element_type.123, bf16[1024,256]{1,0:T(8,128)(2,1)S(1)} %reshape.357, bf16[256,4096]{1,0:T(8,128)(2,1)S(1)} %copy-done), kind=kOutput, calls=%fused_computation.17 | convolution fusion | flops 2189426688 | bytes 27803648 | tf_op jit(solution)/shard_map/dot_general | solution.py:42
  65.4 12.4 %copy.154 = bf16[1024,4096]{0,1:T(8,128)(2,1)} copy(bf16[1024,4096]{1,0:T(8,128)(2,1)} %get-tuple-element.138) | data formatting | bytes 16777216 | tf_op jit(solution)/shard_map/reshape | solution.py:46
  77.8 12.4 %add_bitcast_fusion = f32[1024,16,256]{2,0,1:T(8,128)} fusion(bf16[1024,16,256]{0,2,1:T(8,128)(2,1)} %bitcast.201, bf16[16,256,256]{2,1,0:T(8,128)(2,1)} %param.37, f32[16,256]{1,0:T(8,128)S(1)} %convert_element_type.125), kind=kOutput, calls=%fused_computation.16 | convolution fusion | flops 2151677952 | bytes 27279360 | tf_op jit(solution)/shard_map/nej,ejd->ned/dot_general | solution.py:48
  90.2 20.1 %reshape.359 = f32[512,2,16,256]{3,1,0,2:T(2,128)} reshape(f32[1024,16,256]{2,0,1:T(8,128)} %add_bitcast_fusion) | data formatting | bytes 33554432 | tf_op jit(solution)/shard_map/reshape | solution.py:119
  110.5 12.2 %multiply_reduce_fusion = bf16[512,2,256]{2,1,0:T(2,128)(2,1)S(1)} fusion(f32[512,2,16,256]{3,1,0,2:T(2,128)} %reshape.359, f32[512,2,16]{1,0,2:T(8,128)} %copy.151), kind=kLoop, calls=%fused_computation.12 | loop fusion | flops 8126464 | bytes 17367040
  123.5 68.7 %psum.119 = f32[2]{0:T(128)S(1)} all-reduce(f32[2]{0:T(128)S(1)} %convert_reduce_fusion.6), channel_id=1, replica_groups=mesh['batch'=128] {'batch'}, use_global_device_ids=true, to_apply=%region_11.13 | all-reduce | flops 2 | bytes 16 | tf_op jit(solution)/shard_map/psum | solution.py:92
  198.6 21.5 %fusion.8 = f32[512,2,1,16]{3,2,1,0:T(1,128)} fusion(f32[512,2,16,256]{3,1,0,2:T(2,128)} %reshape.359, f32[512,2,256,1]{2,0,1,3:T(8,128)S(1)} %bitcast.206), kind=kOutput, calls=%fused_computation.10 | convolution fusion | flops 50331648 | bytes 17891328 | tf_op jit(solution)/shard_map/nted,ntd->nte/dot_general | solution.py:155
  221.5 1.9 multiply_multiply_fusion.9
  227.4 1.5 slice_multiply_fusion.5
  228.9 2.1 multiply_reduce_fusion.4
  233.3 1.8 copy.110
  235.1 1.9 mul.777
  238.2 8.6 %fusion.11 = f32[16,1024,256]{1,2,0:T(8,128)} fusion(bf16[16,256,256]{2,1,0:T(8,128)(2,1)} %param.37, f32[1024,256]{1,0:T(8,128)S(1)} %mul.777, f32[1024,16]{0,1:T(8,128)S(1)} %copy.109), kind=kOutput, calls=%fused_computation.19 | convolution fusion | flops 2155872256 | bytes 19988480 | tf_op jit(solution)/shard_map/ned,ejd->nej/dot_general | solution.py:58
  246.8 17.5 %copy.149 = f32[1024,4096]{1,0:T(8,128)} copy(f32[1024,4096]{0,1:T(8,128)} %bitcast.196) | data formatting | bytes 33554432 | tf_op jit(solution)/shard_map/reshape | solution.py:60
  264.3 16.9 %convert_reduce_fusion.1 = (f32[4096]{0:T(1024)}, bf16[1024,4096]{1,0:T(8,128)(2,1)S(1)}) fusion(f32[1024,4096]{1,0:T(8,128)} %copy.149, f32[1024,4096]{1,0:T(8,128)} %get-tuple-element.139, f32[4096]{0:T(1024)} %copy-done.38), kind=kLoop, calls=%fused_computation.14 | loop fusion | flops 96464896 | bytes 41975808 | tf_op jit(solution)/shard_map/reduce_sum | solution.py:62
  281.2 3.2 copy-done.3
  284.5 3.3 fusion.113
  287.8 2.8 reshape.363
  292.5 1.6 fusion.32
  295.2 10.4 %convert_reduce_fusion.2 = (f32[16,256]{1,0:T(8,128)}, bf16[512,16,256]{2,1,0:T(8,128)(2,1)S(1)}) fusion(f32[512,2,16]{2,1,0:T(2,128)} %copy-done.11, f32[512,2,256]{2,0,1:T(8,128)S(1)} %fusion.31), kind=kOutput, calls=%fused_computation.29 | convolution fusion | flops 56619008 | bytes 5324800 | tf_op jit(solution)/shard_map/nte,ntd->ned/dot_general | solution.py:190
  305.6 6.6 fusion.29
  312.2 3.9 fusion.27
  316.1 4.6 fusion.115
  320.7 4.6 fusion.10
  326.2 9.0 %copy.150 = f32[512,4096]{1,0:T(8,128)} copy(f32[512,4096]{0,1:T(8,128)} %bitcast.205) | data formatting | bytes 16777216 | tf_op jit(solution)/shard_map/reshape | solution.py:60
  335.2 10.3 %convert_reduce_fusion.3 = (f32[4096]{0:T(1024)}, bf16[512,4096]{1,0:T(8,128)(2,1)S(1)}) fusion(f32[512,4096]{1,0:T(8,128)} %copy.150, f32[512,4096]{1,0:T(8,128)} %get-tuple-element.137, f32[4096]{0:T(1024)S(1)} %copy-done.37), kind=kLoop, calls=%fused_computation.30 | loop fusion | flops 48230400 | bytes 21004288 | tf_op jit(solution)/shard_map/reduce_sum | solution.py:62
  345.6 2.0 copy-done.4
  347.6 3.3 convolution_bitcast_fusion
  351.1 16.6 %fusion.23 = f32[512,2,16]{2,1,0:T(2,128)} fusion(f32[512,16,256]{2,0,1:T(8,128)} %copy-done.1, f32[512,2,256]{2,0,1:T(8,128)} %copy-done.6), kind=kOutput, calls=%fused_computation.37 | convolution fusion | flops 50331648 | bytes 9502720 | tf_op jit(solution)/shard_map/ned,ntd->nte/dot_general | solution.py:193
  377.2 1.5 copy.127
  387.8 1.7 fusion.90
  391.0 1.9 fusion.57
  392.9 3.1 convert_reduce_fusion
  396.0 4.3 fusion.114
  401.7 167.0 %all-reduce.15.cloned.1.call-done = (f32[256,4096]{0,1:T(8,128)}, f32[16,256,256]{2,1,0:T(8,128)}, f32[256,4096]{1,0:T(8,128)}, f32[16,256,256]{2,1,0:T(8,128)}, f32[2,256,128]{2,1,0:T(8,128)}) async-done(((f32[256,4096]{0,1:T(8,128)}, f32[16,256,256]{2,1,0:T(8,128)}, f32[256,4096]{1,0:T(8,128)}, f32[16,256,256]{2,1,0:T(8,128)}, f32[2,256,128]{2,1,0:T(8,128)}), (f32[256,4096]{0,1:T(8,128)}, ...) | async-done | bytes 17039376 | tf_op jit(solution)/shard_map/psum | solution.py:207
  568.6 5.6 copy.134
  574.2 149.1 %all-reduce.13.cloned.1.call-done = (f32[256,32]{0,1:T(8,128)}, f32[256,8]{0,1:T(8,128)}, f32[4096]{0:T(1024)}, f32[16,256]{1,0:T(8,128)}, f32[256,32]{0,1:T(8,1...) async-done(((f32[256,32]{0,1:T(8,128)}, f32[256,8]{0,1:T(8,128)}, ...) | async-done | bytes 149528 | tf_op jit(solution)/shard_map/psum | solution.py:207
  723.3 1.5 copy.215
  727.5 4.7 copy.218
  734.1 2.0 copy.222
  736.7 2.0 copy.224
  (235 shorter events, 59.5 us)
Async XLA Ops:
  7.2 46.7 %copy-start = (bf16[256,4096]{1,0:T(8,128)(2,1)S(1)}, bf16[256,4096]{1,0:T(8,128)(2,1)}, u32[]{:S(2)}) copy-start(bf16[256,4096]{1,0:T(8,128)(2,1)} %param.35) | copy-start | bytes 6291460
  7.2 561.4 %all-reduce.15.cloned.1.call-start = ((), (), s32[]{:S(2)}) async-start(), calls=%async_computation.1 | async-start | bytes 34078720 | tf_op jit(solution)/shard_map/psum | solution.py:207
  7.5 39.5 %copy-start.31 = (f32[4,16]{1,0:T(4,128)}, f32[4,16]{1,0:T(4,128)S(1)}, u32[]{:S(2)}) copy-start(f32[4,16]{1,0:T(4,128)S(1)} %broadcast_subtract_fusion.2) | copy-start | bytes 772
  7.7 39.3 %copy-start.33 = (f32[4,16]{1,0:T(4,128)}, f32[4,16]{1,0:T(4,128)S(1)}, u32[]{:S(2)}) copy-start(f32[4,16]{1,0:T(4,128)S(1)} %fusion.93) | copy-start | bytes 772
  10.8 12.1 %copy-start.28 = (f32[512,8]{0,1:T(8,128)}, f32[512,8]{0,1:T(8,128)S(1)}, u32[]{:S(2)}) copy-start(f32[512,8]{0,1:T(8,128)S(1)} %fusion.111) | copy-start | bytes 49156
  10.8 12.1 %copy-start.20 = (f32[512,2,4]{0,2,1:T(4,128)}, f32[512,2,4]{0,2,1:T(4,128)S(1)}, u32[]{:S(2)}) copy-start(f32[512,2,4]{0,2,1:T(4,128)S(1)} %reshape.353) | copy-start | bytes 49156
  10.8 12.0 %copy-start.30 = (f32[512,2]{0,1:T(2,128)}, f32[512,2]{0,1:T(2,128)S(1)}, u32[]{:S(2)}) copy-start(f32[512,2]{0,1:T(2,128)S(1)} %reduce_max.16) | copy-start | bytes 12292
  10.9 12.0 %copy-start.39 = (f32[512,2]{0,1:T(2,128)}, f32[512,2]{0,1:T(2,128)S(1)}, u32[]{:S(2)}) copy-start(f32[512,2]{0,1:T(2,128)S(1)} %fusion.86) | copy-start | bytes 12292
  11.8 22.0 %copy-start.11 = (f32[512,2,16]{2,1,0:T(2,128)}, f32[512,2,16]{2,1,0:T(2,128)S(1)}, u32[]{:S(2)}) copy-start(f32[512,2,16]{2,1,0:T(2,128)S(1)} %copy.102) | copy-start | bytes 196612
  13.2 9.6 %copy-start.36 = (f32[4096]{0:T(1024)}, f32[4096]{0:T(1024)S(1)}, u32[]{:S(2)}) copy-start(f32[4096]{0:T(1024)S(1)} %convert_element_type.119) | copy-start | bytes 49156
  37.0 8.4 %copy-start.43 = (bf16[256,32]{0,1:T(8,128)(2,1)S(1)}, bf16[256,32]{0,1:T(8,128)(2,1)}, u32[]{:S(2)}) copy-start(bf16[256,32]{0,1:T(8,128)(2,1)} %param.33) | copy-start | bytes 49156
  37.0 10.1 %copy-start.54 = (bf16[256,8]{0,1:T(8,128)(2,1)S(1)}, bf16[256,8]{0,1:T(8,128)(2,1)}, u32[]{:S(2)}) copy-start(bf16[256,8]{0,1:T(8,128)(2,1)} %param.34) | copy-start | bytes 12292
  45.2 20.2 %copy-start.9 = (bf16[512,2,256]{2,1,0:T(2,128)(2,1)}, bf16[512,2,256]{2,1,0:T(2,128)(2,1)S(1)}, u32[]{:S(2)}) copy-start(bf16[512,2,256]{2,1,0:T(2,128)(2,1)S(1)} %fusion.33) | copy-start | bytes 1572868
  45.4 20.0 %copy-start.14 = (bf16[1024,256]{1,0:T(8,128)(2,1)}, bf16[1024,256]{1,0:T(8,128)(2,1)S(1)}, u32[]{:S(2)}) copy-start(bf16[1024,256]{1,0:T(8,128)(2,1)S(1)} %reshape.357) | copy-start | bytes 1572868
  53.8 11.5 %copy-start.38 = (f32[4096]{0:T(1024)}, f32[4096]{0:T(1024)S(1)}, u32[]{:S(2)}) copy-start(f32[4096]{0:T(1024)S(1)} %convert_element_type.123) | copy-start | bytes 49156
  65.3 12.5 %copy-start.51 = (bf16[16,256]{1,0:T(8,128)(2,1)S(1)}, bf16[16,256]{1,0:T(8,128)(2,1)}, u32[]{:S(2)}) copy-start(bf16[16,256]{1,0:T(8,128)(2,1)} %param.38) | copy-start | bytes 24580
  90.2 20.1 %copy-start.50 = (s32[512,2]{0,1:T(2,128)S(1)}, s32[512,2]{0,1:T(2,128)}, u32[]{:S(2)}) copy-start(s32[512,2]{0,1:T(2,128)} %param.25) | copy-start | bytes 12292
  110.4 81.7 %copy-start.53 = (s32[512]{0:T(512)S(1)}, s32[512]{0:T(512)}, u32[]{:S(2)}) copy-start(s32[512]{0:T(512)} %param.26) | copy-start | bytes 6148
  110.4 83.0 %copy-start.23 = (f32[4,512,2,4]{1,0,3,2:T(4,128)S(1)}, f32[4,512,2,4]{1,0,3,2:T(4,128)}, u32[]{:S(2)}) copy-start(f32[4,512,2,4]{1,0,3,2:T(4,128)} %get-tuple-element.128) | copy-start | bytes 196612
  110.4 83.1 %copy-start.32 = (f32[4,16]{1,0:T(4,128)S(1)}, f32[4,16]{1,0:T(4,128)}, u32[]{:S(2)}) copy-start(f32[4,16]{1,0:T(4,128)} %copy-done.31) | copy-start | bytes 772
  110.4 83.1 %copy-start.34 = (f32[4,16]{1,0:T(4,128)S(1)}, f32[4,16]{1,0:T(4,128)}, u32[]{:S(2)}) copy-start(f32[4,16]{1,0:T(4,128)} %copy-done.33) | copy-start | bytes 772
  110.4 84.3 %copy-start.55 = (bf16[2,128]{1,0:T(2,128)(2,1)S(1)}, bf16[2,128]{1,0:T(2,128)(2,1)}, u32[]{:S(2)}) copy-start(bf16[2,128]{1,0:T(2,128)(2,1)} %param.41) | copy-start | bytes 1540
  110.5 84.3 %copy-start.29 = (bf16[2,256,128]{2,1,0:T(8,128)(2,1)S(1)}, bf16[2,256,128]{2,1,0:T(8,128)(2,1)}, u32[]{:S(2)}) copy-start(bf16[2,256,128]{2,1,0:T(8,128)(2,1)} %param.39) | copy-start | bytes 393220
  123.4 74.8 %copy-start.16 = (bf16[512,2,256]{0,2,1:T(8,128)(2,1)}, bf16[512,2,256]{0,2,1:T(8,128)(2,1)S(1)}, u32[]{:S(2)}) copy-start(bf16[512,2,256]{0,2,1:T(8,128)(2,1)S(1)} %copy.140) | copy-start | bytes 1572868
  198.6 27.2 %copy-start.19 = (f32[512,32]{0,1:T(8,128)S(1)}, f32[512,32]{0,1:T(8,128)}, u32[]{:S(2)}) copy-start(f32[512,32]{0,1:T(8,128)} %get-tuple-element.135) | copy-start | bytes 196612
  224.5 69.6 %copy-start.25 = (f32[512,2,4]{0,2,1:T(4,128)}, f32[512,2,4]{0,2,1:T(4,128)S(1)}, u32[]{:S(2)}) copy-start(f32[512,2,4]{0,2,1:T(4,128)S(1)} %fusion.62) | copy-start | bytes 49156
  290.6 15.0 %copy-start.7 = (bf16[16,256,256]{2,1,0:T(8,128)(2,1)S(1)}, bf16[16,256,256]{2,1,0:T(8,128)(2,1)}, u32[]{:S(2)}) copy-start(bf16[16,256,256]{2,1,0:T(8,128)(2,1)} %param.31) | copy-start | bytes 6291460
  292.5 13.1 %copy-start.22 = (bf16[512,2,16]{0,2,1:T(8,128)(2,1)}, bf16[512,2,16]{0,2,1:T(8,128)(2,1)S(1)}, u32[]{:S(2)}) copy-start(bf16[512,2,16]{0,2,1:T(8,128)(2,1)S(1)} %fusion.73) | copy-start | bytes 98308
  295.2 10.4 %copy-start.6 = (f32[512,2,256]{2,0,1:T(8,128)}, f32[512,2,256]{2,0,1:T(8,128)S(1)}, u32[]{:S(2)}) copy-start(f32[512,2,256]{2,0,1:T(8,128)S(1)} %fusion.31) | copy-start | bytes 3145732
  305.6 6.6 copy-start.2
  305.6 10.5 %slice-start = ((s8[8388608]{0:T(1024)(128)(4,1)}), s8[4194304]{0:T(1024)(128)(4,1)S(1)}, s32[]{:S(2)}) async-start(s8[8388608]{0:T(1024)(128)(4,1)} %bitcast.199), calls=%async_computation.2 | async-start | bytes 8388608
  305.6 15.1 %slice-start.2 = ((s8[8388608]{0:T(1024)(128)(4,1)}), s8[4194304]{0:T(1024)(128)(4,1)S(1)}, s32[]{:S(2)}) async-start(s8[8388608]{0:T(1024)(128)(4,1)} %bitcast.202), calls=%async_computation.4 | async-start | bytes 8388608
  312.2 8.5 %slice-start.3 = ((s8[8388608]{0:T(1024)(128)(4,1)}), s8[4194304]{0:T(1024)(128)(4,1)S(1)}, s32[]{:S(2)}) async-start(s8[8388608]{0:T(1024)(128)(4,1)} %bitcast.202), calls=%async_computation.5 | async-start | bytes 8388608
  326.2 9.0 %copy-start.37 = (f32[4096]{0:T(1024)S(1)}, f32[4096]{0:T(1024)}, u32[]{:S(2)}) copy-start(f32[4096]{0:T(1024)} %copy-done.36) | copy-start | bytes 49156
  335.2 12.3 %copy-start.8 = (bf16[512,256]{1,0:T(8,128)(2,1)S(1)}, bf16[512,256]{1,0:T(8,128)(2,1)}, u32[]{:S(2)}) copy-start(bf16[512,256]{1,0:T(8,128)(2,1)} %param.24) | copy-start | bytes 786436
  350.9 31.1 %copy-start.21 = (f32[512,2,4]{0,2,1:T(4,128)S(1)}, f32[512,2,4]{0,2,1:T(4,128)}, u32[]{:S(2)}) copy-start(f32[512,2,4]{0,2,1:T(4,128)} %copy-done.20) | copy-start | bytes 49156
  350.9 372.4 %all-reduce.13.cloned.1.call-start = ((), (), s32[]{:S(2)}) async-start(), calls=%async_computation | async-start | bytes 300032 | tf_op jit(solution)/shard_map/psum | solution.py:207
  381.3 19.0 %copy-start.35 = (bf16[256,32]{0,1:T(8,128)(2,1)S(1)}, bf16[256,32]{0,1:T(8,128)(2,1)}, u32[]{:S(2)}) copy-start(bf16[256,32]{0,1:T(8,128)(2,1)} %param.27) | copy-start | bytes 49156
  382.7 17.9 %copy-start.44 = (bf16[256,8]{0,1:T(8,128)(2,1)S(1)}, bf16[256,8]{0,1:T(8,128)(2,1)}, u32[]{:S(2)}) copy-start(bf16[256,8]{0,1:T(8,128)(2,1)} %param.28) | copy-start | bytes 12292
  723.3 8.9 %copy-start.49 = (f32[16,256]{1,0:T(8,128)S(1)}, f32[16,256]{1,0:T(8,128)}, u32[]{:S(2)}) copy-start(f32[16,256]{1,0:T(8,128)} %get-tuple-element.158) | copy-start | bytes 49156
  723.3 9.5 %copy-start.42 = (f32[256,32]{0,1:T(8,128)S(1)}, f32[256,32]{0,1:T(8,128)}, u32[]{:S(2)}) copy-start(f32[256,32]{0,1:T(8,128)} %get-tuple-element.159) | copy-start | bytes 98308
  723.3 10.1 %copy-start.52 = (f32[256,8]{0,1:T(8,128)S(1)}, f32[256,8]{0,1:T(8,128)}, u32[]{:S(2)}) copy-start(f32[256,8]{0,1:T(8,128)} %get-tuple-element.160) | copy-start | bytes 24580
  723.3 10.7 %copy-start.13 = (f32[256,4096]{1,0:T(8,128)S(1)}, f32[256,4096]{1,0:T(8,128)}, u32[]{:S(2)}) copy-start(f32[256,4096]{1,0:T(8,128)} %get-tuple-element.161) | copy-start | bytes 12582916
  727.5 8.6 %copy-start.48 = (f32[4096]{0:T(1024)S(1)}, f32[4096]{0:T(1024)}, u32[]{:S(2)}) copy-start(f32[4096]{0:T(1024)} %get-tuple-element.162) | copy-start | bytes 49156
  727.5 9.2 %copy-start.12 = (f32[16,256,256]{2,1,0:T(8,128)S(1)}, f32[16,256,256]{2,1,0:T(8,128)}, u32[]{:S(2)}) copy-start(f32[16,256,256]{2,1,0:T(8,128)} %get-tuple-element.163) | copy-start | bytes 12582916
  734.0 6.0 copy-start.57
  734.1 6.5 copy-start.56
  734.1 7.1 copy-start.58
  (17 other events, 44.7 us)
Sparse Core Ops, SparseCore 0:
  351.0 217.5 all-reduce.14
  577.9 145.3 all-reduce.12
where the time goes:
time: 755 us; the launch traced here: 749 us
  waiting for transfers between devices  316 us (42%)
  matrix products  151 us (20%)
  local copies, waits for them, and re-layouts  125 us (17%)
  other arithmetic  72.9 us (10%)
  blocking collectives  68.7 us (9%)
  between operations  15.1 us (2%)
    psum x2, waiting for transfers between devices, on_device(): lax.psum((grad_codes_one, grad_mixing_one, grad_inner_one, grad_inner_bia...  316 us
    psum x1, blocking collectives, on_device(): positives = lax.psum(jnp.sum(labels_f, axis=0), 'batch')  68.7 us
    unnamed x143, local copies, waits for them, and re-layouts  37.6 us
    reduce_sum x2, other arithmetic, experts_backward(): grad_inner_bias = jnp.sum(grad_pre.astype(jnp.float32), axis=0)  27.2 us
    reshape x2, local copies, waits for them, and re-layouts, experts_backward(): grad_hidden = jnp.einsum('ned,ejd->nej', grad_out, outer, preferred_eleme...  26.5 us
    dot_general x1, matrix products, on_device(): jnp.einsum('nted,ntd->nte', out_two, grad_y_two, precision=highest)  21.5 us
    dot_general x2, matrix products, experts_forward(): jnp.dot(inputs, inner, preferred_element_type=jnp.float32)  21.1 us
    reshape x1, local copies, waits for them, and re-layouts, on_device(): out_flat.reshape(local_rows, num_tasks, out_flat.shape[1], model_width)  20.1 us
  transfers between devices with their start and end apart: 2, of which 2 were waited for; matrix products, arithmetic and copies ran while one was open for 7% of the time, Pallas kernels for 0%

commit v1 on v0

v1 whole, which is shorter than its diff:
```python
import functools

import jax
import jax.numpy as jnp
from jax import lax
from jax.experimental import pallas as pl
from jax.experimental.pallas import tpu as pltpu
from jax.sharding import PartitionSpec as P

EXPERTS = 16
SEL = 4
BITS = 4
TASKS = 2
WIDTH = 256
HID = 256
TOWER = 128
PAIR = 2
STEPS = EXPERTS // PAIR
F32 = jnp.float32
BF16 = jnp.bfloat16
ROOT = 0.7978845608028654
CUBE = 0.044715
BYTES = 56 * 1024 * 1024


def nn(a, b):
    return lax.dot_general(a, b, (((1,), (0,)), ((), ())), preferred_element_type=F32)


def nt(a, b):
    return lax.dot_general(a, b, (((1,), (1,)), ((), ())), preferred_element_type=F32)


def tn(a, b):
    return lax.dot_general(a, b, (((0,), (0,)), ((), ())), preferred_element_type=F32)


def pieces(x):
    hi = x.astype(BF16)
    rest = x - hi.astype(F32)
    mid = rest.astype(BF16)
    return hi, mid, (rest - mid.astype(F32)).astype(BF16)


def gelu_both(x):
    square = x * x
    slope = square * (ROOT * CUBE) + ROOT
    s = 0.5 + 0.5 * jnp.tanh(x * slope)
    value = x * s
    return value, s + value * (1.0 - s) * (slope * 6.0 - 4.0 * ROOT)


def soft_parts(mix):
    top = jnp.maximum(jnp.maximum(mix[0], mix[1]), jnp.maximum(mix[2], mix[3]))
    raised = [jnp.exp(m - top) for m in mix]
    total = raised[0] + raised[1] + raised[2] + raised[3]
    return [r / total for r in raised]


def bit_factors(code):
    rows = code[0].shape[1]
    expert = lax.broadcasted_iota(jnp.int32, (EXPERTS, rows), 0)
    found = []
    for i in range(SEL):
        per_bit = []
        for b in range(BITS):
            k = jnp.clip(code[i * BITS + b], -5.0, 5.0)
            s = -0.002 * (k * k * k) + 0.15 * k + 0.5
            on = (expert >> b) & 1 == 1
            per_bit.append(jnp.where(on, s, 1.0 - s))
        found.append(per_bit)
    return found


def gate_of(code, mix):
    w = soft_parts(mix)
    total = None
    for i, f in enumerate(bit_factors(code)):
        r = w[i] * ((f[0] * f[1]) * (f[2] * f[3]))
        total = r if total is None else total + r
    return total


def gate_back(code, mix, grad):
    rows = grad.shape[1]
    expert = lax.broadcasted_iota(jnp.int32, (EXPERTS, rows), 0)
    w = soft_parts(mix)
    grad_w, grad_code = [], []
    for i, f in enumerate(bit_factors(code)):
        low, high = f[0] * f[1], f[2] * f[3]
        grad_w.append(jnp.sum(grad * (low * high), axis=0, keepdims=True))
        up = grad * w[i]
        others = (f[1] * high, f[0] * high, low * f[3], low * f[2])
        for b in range(BITS):
            on = (expert >> b) & 1 == 1
            term = up * others[b]
            ds = jnp.sum(jnp.where(on, term, -term), axis=0, keepdims=True)
            c = code[i * BITS + b]
            k = jnp.clip(c, -5.0, 5.0)
            inside = jnp.where(jnp.abs(c) <= 5.0, 0.15 - 0.006 * (k * k), 0.0)
            grad_code.append(ds * inside)
    mean = w[0] * grad_w[0] + w[1] * grad_w[1] + w[2] * grad_w[2] + w[3] * grad_w[3]
    return grad_code, [w[i] * (grad_w[i] - mean) for i in range(SEL)]


def task_rows(logits, mixes, task, lanes):
    code = [logits[task * 16 + k : task * 16 + k + 1, lanes] for k in range(16)]
    mix = [mixes[task * 4 + k : task * 4 + k + 1, lanes] for k in range(4)]
    return code, mix


def task_lanes(task, rows, shared):
    return slice(0, rows) if shared else slice(task * rows, (task + 1) * rows)


def forward_kernel(
    shared,
    rows,
    u_ref,
    codes_ref,
    mixing_ref,
    inner_ref,
    bias_ref,
    outer_ref,
    outer_bias_ref,
    hid_ref,
    slope_ref,
    out_ref,
    next_ref,
    gate_ref,
    code_ref,
    mix_ref,
    *rest,
):
    step = pl.program_id(0)
    if shared:
        turned_ref, acc_ref = rest
    else:
        (acc_ref,) = rest
        turned_ref = u_ref

    @pl.when(step == 0)
    def _():
        if shared:
            turned_ref[...] = u_ref[...].astype(F32).T.astype(BF16)
        u = turned_ref[...]
        code_ref[...] = tn(codes_ref[...], u)
        mix_ref[...] = tn(mixing_ref[...], u)
        outer_bias = outer_bias_ref[...]
        for t in range(TASKS):
            lanes = task_lanes(t, rows, shared)
            code, mix = task_rows(code_ref, mix_ref, t, lanes)
            gate = gate_of(code, mix)
            gate_ref[:, t * rows : (t + 1) * rows] = gate
            hi, mid, low = pieces(gate)
            acc_ref[:, t * rows : (t + 1) * rows] = (
                tn(outer_bias, hi) + tn(outer_bias, mid) + tn(outer_bias, low)
            )

    u = turned_ref[...]
    bias = bias_ref[0].astype(F32).T
    for p in range(PAIR):
        e = step * PAIR + p
        pre = tn(inner_ref[:, p * HID : (p + 1) * HID], u) + bias[:, p : p + 1]
        hid, slope = gelu_both(pre)
        hid = hid.astype(BF16)
        hid_ref[p] = hid
        slope_ref[p] = slope.astype(BF16)
        out = tn(outer_ref[p], hid)
        out_ref[p] = out.astype(BF16)
        gate = gate_ref[pl.ds(e, 1), :]
        if shared:
            acc_ref[:, :rows] += gate[:, :rows] * out
            acc_ref[:, rows:] += gate[:, rows:] * out
        else:
            acc_ref[...] += gate * out

    @pl.when(step == STEPS - 1)
    def _():
        next_ref[...] = acc_ref[...].astype(BF16)


def whole(shape):
    return pl.BlockSpec(shape, lambda *_: (0,) * len(shape))


def forward(shared, u, codes, mixing, inner, inner_bias, outer, outer_bias):
    rows = u.shape[0] if shared else u.shape[1] // TASKS
    lanes = rows if shared else rows * TASKS
    state = jax.ShapeDtypeStruct((EXPERTS, HID, lanes), BF16)
    state_spec = pl.BlockSpec((PAIR, HID, lanes), lambda i: (i, 0, 0))
    out_shape = [
        state,
        state,
        state,
        jax.ShapeDtypeStruct((WIDTH, TASKS * rows), BF16),
        jax.ShapeDtypeStruct((EXPERTS, TASKS * rows), F32),
        jax.ShapeDtypeStruct((32, lanes), F32),
        jax.ShapeDtypeStruct((8, lanes), F32),
    ]
    out_specs = [state_spec] * 3 + [whole(s.shape) for s in out_shape[3:]]
    if shared:
        out_shape.append(jax.ShapeDtypeStruct((WIDTH, rows), BF16))
        out_specs.append(whole((WIDTH, rows)))
    return pl.pallas_call(
        functools.partial(forward_kernel, shared, rows),
        grid=(STEPS,),
        in_specs=[
            whole(u.shape),
            whole(codes.shape),
            whole(mixing.shape),
            pl.BlockSpec((WIDTH, PAIR * HID), lambda i: (0, i)),
            pl.BlockSpec((1, PAIR, HID), lambda i: (i, 0, 0)),
            pl.BlockSpec((PAIR, HID, WIDTH), lambda i: (i, 0, 0)),
            whole(outer_bias.shape),
        ],
        out_specs=out_specs,
        out_shape=out_shape,
        scratch_shapes=[pltpu.VMEM((WIDTH, TASKS * rows), F32)],
        compiler_params=pltpu.CompilerParams(
            dimension_semantics=("arbitrary",), vmem_limit_bytes=BYTES
        ),
        name="forward_one" if shared else "forward_two",
    )(u, codes, mixing, inner, inner_bias.reshape(STEPS, PAIR, HID), outer, outer_bias)


def tower(
    rows,
    v_ref,
    labels_ref,
    counts_ref,
    lengths_ref,
    base_ref,
    inner_ref,
    bias_ref,
    outer_ref,
    outer_bias_ref,
    predictions_ref,
    small_ref,
    grad_inner_ref,
    dy_ref,
):
    sessions = lengths_ref.shape[1]
    lens = jnp.broadcast_to(lengths_ref[...], (8, sessions)).astype(F32).astype(BF16)
    before = lax.broadcasted_iota(jnp.int32, (sessions, sessions), 0)
    after = lax.broadcasted_iota(jnp.int32, (sessions, sessions), 1)
    upto = jnp.where(before <= after, 1.0, 0.0).astype(BF16)
    ends = nn(lens, upto)[0:1, :]
    starts = ends - lens[0:1, :].astype(F32)
    ids = (lax.broadcasted_iota(jnp.int32, (rows, sessions), 0) + base_ref[0]).astype(F32)
    inside = jnp.where((ids >= starts) & (ids < ends), 1.0, 0.0).astype(BF16)
    row_length = nt(lens, inside)[0:1, :]
    all_rows = float(rows * counts_ref.shape[0])
    weight = (all_rows / sessions) / row_length
    positives = jnp.sum(counts_ref[...], axis=0, keepdims=True)
    bias = bias_ref[...].astype(F32).T
    columns = outer_ref[...].astype(F32).T
    small_ref[...] = jnp.zeros_like(small_ref)
    for t in range(TASKS):
        lanes = slice(t * rows, (t + 1) * rows)
        v = v_ref[:, lanes]
        pre = tn(inner_ref[t], v) + bias[:, t : t + 1]
        hid, slope = gelu_both(pre)
        hid = hid.astype(BF16)
        column = columns[:, t : t + 1]
        logit = jnp.sum(hid.astype(F32) * column, axis=0, keepdims=True)
        logit = logit + outer_bias_ref[0:1, t : t + 1].astype(F32)
        y = labels_ref[t : t + 1, :].astype(F32)
        count = positives[:, t : t + 1]
        ratio = (all_rows - count) / count
        chance = jax.nn.sigmoid(logit)
        predictions_ref[t : t + 1, :] = chance
        grad = weight * (-ratio * y * jax.nn.sigmoid(-logit) + (1.0 - y) * chance)
        grad = grad.astype(BF16)
        back = (grad.astype(F32) * column * slope).astype(BF16)
        picked = lax.broadcasted_iota(jnp.int32, (16, rows), 0)
        stack = jnp.where(picked == 0, grad.astype(F32), jnp.where(picked == 1, 1.0, 0.0))
        stack = stack.astype(BF16)
        by_hid = nt(stack, hid)
        by_back = nt(stack, back)
        small_ref[t : t + 1, :TOWER] = by_hid[0:1]
        small_ref[2 + t : 3 + t, :TOWER] = by_back[1:2]
        total = jnp.sum(grad.astype(F32), axis=1, keepdims=True)
        small_ref[4 + t : 5 + t, :TOWER] = jnp.broadcast_to(total, (1, TOWER))
        grad_inner_ref[t] = nt(v, back)
        dy_ref[:, lanes] = nn(inner_ref[t], back)


def backward_kernel(shared, rows, *refs):
    (u_ref, codes_ref, mixing_ref, inner_ref, outer_ref, outer_bias_ref) = refs[:6]
    (hid_ref, slope_ref, out_ref, gate_ref, code_ref, mix_ref) = refs[6:12]
    refs = refs[12:]
    if shared:
        dy_ref, refs = refs[0], refs[1:]
    else:
        tower_in, refs = refs[:9], refs[9:]
    grad_inner_ref, grad_outer_ref, grad_bias_ref, grad_rest_ref, back_ref = refs[:5]
    refs = refs[5:]
    if not shared:
        tower_out, refs = refs[:3], refs[3:]
        dy_ref, refs = refs[0], refs[1:]
    aug_ref, dgate_ref, acc_ref, dcode_ref, dmix_ref = refs
    step = pl.program_id(0)
    lanes = rows if shared else rows * TASKS

    @pl.when(step == 0)
    def _():
        if not shared:
            tower(rows, *tower_in, *tower_out, dy_ref)
        aug_ref[:WIDTH, :] = u_ref[...]
        first = lax.broadcasted_iota(jnp.int32, (16, lanes), 0) == 0
        aug_ref[WIDTH:, :] = jnp.where(first, 1.0, 0.0).astype(BF16)
        acc_ref[...] = jnp.zeros_like(acc_ref)

    pre_pair = []
    for p in range(PAIR):
        e = step * PAIR + p
        gate = gate_ref[pl.ds(e, 1), :]
        out = out_ref[p].astype(F32)
        if shared:
            one, two = dy_ref[:, :rows], dy_ref[:, rows:]
            dout = (gate[:, :rows] * one + gate[:, rows:] * two).astype(BF16)
            dgate_ref[pl.ds(e, 1), :rows] = jnp.sum(out * one, axis=0, keepdims=True)
            dgate_ref[pl.ds(e, 1), rows:] = jnp.sum(out * two, axis=0, keepdims=True)
        else:
            dy = dy_ref[...]
            dout = (gate * dy).astype(BF16)
            dgate_ref[pl.ds(e, 1), :] = jnp.sum(out * dy, axis=0, keepdims=True)
        dpre = (nn(outer_ref[p], dout) * slope_ref[p].astype(F32)).astype(BF16)
        grad_outer_ref[p] = nt(hid_ref[p], dout)
        grad = nt(aug_ref[...], dpre)
        grad_inner_ref[:, p * HID : (p + 1) * HID] = grad[:WIDTH]
        grad_bias_ref[0, p : p + 1, :] = grad[WIDTH : WIDTH + 1]
        pre_pair.append(dpre)
    acc_ref[...] += nn(inner_ref[...], jnp.concatenate(pre_pair, axis=0))

    @pl.when(step == STEPS - 1)
    def _():
        dcode_ref[...] = jnp.zeros_like(dcode_ref)
        dmix_ref[...] = jnp.zeros_like(dmix_ref)
        outer_bias = outer_bias_ref[...]
        for t in range(TASKS):
            span = slice(t * rows, (t + 1) * rows)
            here = task_lanes(t, rows, shared)
            hi, mid, low = pieces(dy_ref[:, span])
            upto = nn(outer_bias, hi) + nn(outer_bias, mid) + nn(outer_bias, low)
            code, mix = task_rows(code_ref, mix_ref, t, here)
            grad_code, grad_mix = gate_back(code, mix, dgate_ref[:, span] + upto)
            for k in range(16):
                dcode_ref[t * 16 + k : t * 16 + k + 1, here] = grad_code[k]
            for k in range(4):
                dmix_ref[t * 4 + k : t * 4 + k + 1, here] = grad_mix[k]
        dcode = dcode_ref[...].astype(BF16)
        dmix = dmix_ref[...].astype(BF16)
        u = u_ref[...]
        grad_rest_ref[:32, :] = nt(dcode, u)
        grad_rest_ref[32:40, :] = nt(dmix, u)
        g_hi, g_mid, _ = pieces(gate_ref[...])
        y_hi, y_mid, _ = pieces(dy_ref[...])
        grad_rest_ref[40:56, :] = nt(g_hi, y_hi) + nt(g_hi, y_mid) + nt(g_mid, y_hi)
        du = acc_ref[...] + nn(codes_ref[...], dcode) + nn(mixing_ref[...], dmix)
        back_ref[...] = du.T if shared else du


def backward(shared, u, codes, mixing, inner, outer, outer_bias, state, extra):
    rows = u.shape[1] if shared else u.shape[1] // TASKS
    lanes = u.shape[1]
    state_spec = pl.BlockSpec((PAIR, HID, lanes), lambda i: (i, 0, 0))
    in_arrays = [u, codes, mixing, inner, outer, outer_bias, *state, *extra]
    in_specs = [
        whole(u.shape),
        whole(codes.shape),
        whole(mixing.shape),
        pl.BlockSpec((WIDTH, PAIR * HID), lambda i: (0, i)),
        pl.BlockSpec((PAIR, HID, WIDTH), lambda i: (i, 0, 0)),
        whole(outer_bias.shape),
        state_spec,
        state_spec,
        state_spec,
    ]
    in_specs += [whole(a.shape) for a in in_arrays[9:]]
    if not shared:
        in_specs[16] = pl.BlockSpec(memory_space=pltpu.SMEM)
    back_shape = (rows, WIDTH) if shared else (WIDTH, lanes)
    out_shape = [
        jax.ShapeDtypeStruct((WIDTH, EXPERTS * HID), F32),
        jax.ShapeDtypeStruct((EXPERTS, HID, WIDTH), F32),
        jax.ShapeDtypeStruct((STEPS, PAIR, HID), F32),
        jax.ShapeDtypeStruct((56, WIDTH), F32),
        jax.ShapeDtypeStruct(back_shape, F32),
    ]
    out_specs = [
        pl.BlockSpec((WIDTH, PAIR * HID), lambda i: (0, i)),
        pl.BlockSpec((PAIR, HID, WIDTH), lambda i: (i, 0, 0)),
        pl.BlockSpec((1, PAIR, HID), lambda i: (i, 0, 0)),
        whole((56, WIDTH)),
        whole(back_shape),
    ]
    scratch = []
    if not shared:
        more = [
            jax.ShapeDtypeStruct((TASKS, rows), F32),
            jax.ShapeDtypeStruct((8, TOWER), F32),
            jax.ShapeDtypeStruct((TASKS, WIDTH, TOWER), F32),
        ]
        out_shape += more
        out_specs += [whole(s.shape) for s in more]
        scratch.append(pltpu.VMEM((WIDTH, lanes), F32))
    scratch += [
        pltpu.VMEM((WIDTH + 16, lanes), BF16),
        pltpu.VMEM((EXPERTS, TASKS * rows), F32),
        pltpu.VMEM((WIDTH, lanes), F32),
        pltpu.VMEM((32, lanes), F32),
        pltpu.VMEM((8, lanes), F32),
    ]
    return pl.pallas_call(
        functools.partial(backward_kernel, shared, rows),
        grid=(STEPS,),
        in_specs=in_specs,
        out_specs=out_specs,
        out_shape=out_shape,
        scratch_shapes=scratch,
        compiler_params=pltpu.CompilerParams(
            dimension_semantics=("arbitrary",), vmem_limit_bytes=BYTES
        ),
        name="backward_one" if shared else "backward_two",
    )(*in_arrays)


def local_part(
    tokens,
    labels,
    lengths,
    counts,
    base,
    codes_one,
    mixing_one,
    inner_one,
    inner_bias_one,
    outer_one,
    outer_bias_one,
    codes_two,
    mixing_two,
    inner_two,
    inner_bias_two,
    outer_two,
    outer_bias_two,
    tower_inner,
    tower_inner_bias,
    tower_outer,
    tower_outer_bias,
):
    one = forward(
        True, tokens, codes_one, mixing_one, inner_one, inner_bias_one, outer_one, outer_bias_one
    )
    hid_one, slope_one, out_one, u_two, gate_one, code_one, mix_one, u_one = one
    two = forward(
        False, u_two, codes_two, mixing_two, inner_two, inner_bias_two, outer_two, outer_bias_two
    )
    hid_two, slope_two, out_two, v_two, gate_two, code_two, mix_two = two
    extra = (
        v_two,
        labels.T,
        counts(two),
        lengths.reshape(1, -1),
        base,
        tower_inner,
        tower_inner_bias,
        tower_outer,
        tower_outer_bias.reshape(1, TASKS),
    )
    back_two = backward(
        False,
        u_two,
        codes_two,
        mixing_two,
        inner_two,
        outer_two,
        outer_bias_two,
        (hid_two, slope_two, out_two, gate_two, code_two, mix_two),
        extra,
    )
    back_one = backward(
        True,
        u_one,
        codes_one,
        mixing_one,
        inner_one,
        outer_one,
        outer_bias_one,
        (hid_one, slope_one, out_one, gate_one, code_one, mix_one),
        (back_two[4],),
    )
    return back_one, back_two


def on_device(tokens, labels, lengths, *params):
    local_rows = tokens.shape[0]
    devices = lax.axis_size("batch")
    count = jnp.sum(labels.astype(F32), axis=0)
    sent = jnp.broadcast_to(jnp.pad(count, (0, 126))[None, :], (devices, 128))
    counts = lax.all_to_all(sent, "batch", 0, 0, tiled=True)
    base = (lax.axis_index("batch") * local_rows).astype(jnp.int32).reshape(1)
    back_one, back_two = local_part(
        tokens, labels, lengths, lambda _: counts, base, *params
    )
    inner_one, outer_one, bias_one, rest_one, grad_tokens = back_one
    inner_two, outer_two, bias_two, rest_two, _, predictions, small, tower_inner = back_two
    pack = jnp.concatenate(
        [
            rest_one,
            bias_one.reshape(16, 256),
            rest_two,
            bias_two.reshape(16, 256),
            jnp.pad(small, ((0, 0), (0, 128))),
        ],
        axis=0,
    )
    inner_one, outer_one, inner_two, outer_two, tower_inner, pack = lax.psum(
        (inner_one, outer_one, inner_two, outer_two, tower_inner, pack), "batch"
    )
    return (
        predictions.T,
        grad_tokens,
        pack[0:32].T,
        pack[32:40].T,
        inner_one,
        pack[56:72].reshape(-1),
        outer_one,
        pack[40:56],
        pack[72:104].T,
        pack[104:112].T,
        inner_two,
        pack[128:144].reshape(-1),
        outer_two,
        pack[112:128],
        tower_inner,
        pack[146:148, :128],
        pack[144:146, :128],
        pack[148:150, 0],
    )


def solution(mesh):
    rows, copied = P("batch", None), P()
    return jax.shard_map(
        on_device,
        mesh=mesh,
        in_specs=(rows, rows) + (copied,) * 17,
        out_specs=(rows, rows) + (copied,) * 16,
        check_vma=False,
    )
```

time: 755 us -> 359 us (0.48)
  matrix products: 151 us -> 0 us
  waiting for transfers between devices: 316 us -> 224 us
  local copies, waits for them, and re-layouts: 125 us -> 34.8 us
  Pallas kernels: 0 us -> 72.4 us
  other arithmetic: 72.9 us -> 0.81 us
  blocking collectives: 68.7 us -> 0 us
  starting transfers between devices: 0.25 us -> 11.5 us
    dot_general x33 -> x0, matrix products: 150 us -> none  [the longest x1 21.5 us: on_device(): jnp.einsum('nted,ntd->nte', out_two, grad_y_two, precision=highest)]
    psum x2 -> x1, waiting for transfers between devices: 316 us -> 224 us  [on_device(): lax.psum((inner_one, outer_one, inner_two, outer_two, tower_inner, pack),...]
    pallas_call x0 -> x4, Pallas kernels: none -> 72.4 us  [the longest x2 38.5 us: backward(): pl.pallas_call(functools.partial(backward_kernel, shared, rows), grid=(ST...]
    psum x1 -> x0, blocking collectives: 68.7 us -> none  [on_device(): positives = lax.psum(jnp.sum(labels_f, axis=0), 'batch')]
    reshape x10 -> x4, local copies, waits for them, and re-layouts: 69.3 us -> 3.37 us  [the longest x2 2.62 us: forward(): inner_bias.reshape(STEPS, PAIR, HID)]
    reduce_sum x15 -> x1, other arithmetic: 39.9 us -> 0.81 us  [on_device(): count = jnp.sum(labels.astype(F32), axis=0)]
    unnamed x143 -> x33, local copies, waits for them, and re-layouts: 37.6 us -> 24 us
    unnamed x3 -> x0, other arithmetic: 12.2 us -> none
  transfers between devices with their start and end apart: 2 -> 2, of which waited for: 2 -> 1; matrix products, arithmetic and copies ran while one was open for 7% -> 2% of each run, Pallas kernels for 0% -> 10%
where the time goes in v1:
time: 359 us; the launch traced here: 357 us
  waiting for transfers between devices  224 us (62%)
  Pallas kernels  72.4 us (20%)
  local copies, waits for them, and re-layouts  34.8 us (10%)
  between operations  14.2 us (4%)
  starting transfers between devices  11.5 us (3%)
    psum x1, waiting for transfers between devices, on_device(): lax.psum((inner_one, outer_one, inner_two, outer_two, tower_inner, pack),...  224 us
    pallas_call x2, Pallas kernels, backward(): pl.pallas_call(functools.partial(backward_kernel, shared, rows), grid=(ST...  38.5 us
    pallas_call x2, Pallas kernels, forward(): pl.pallas_call(functools.partial(forward_kernel, shared, rows), grid=(STE...  34 us
    unnamed x33, local copies, waits for them, and re-layouts  24 us
    all_to_all x1, starting transfers between devices, on_device(): counts = lax.all_to_all(sent, 'batch', 0, 0, tiled=True)  11.5 us
  transfers between devices with their start and end apart: 2, of which 1 were waited for; matrix products, arithmetic and copies ran while one was open for 2% of the time, Pallas kernels for 10%

profile of v1, /device:TPU:1, one launch (start us, length us, event | category | flops | bytes accessed | tf_op | source)
XLA Modules:
  0.0 357.5 jit_solution(18101856235431554072)
XLA Ops:
  7.2 0.8 convert_reduce_fusion
  8.0 0.7 broadcast_in_dim.2
  8.7 11.5 %all-to-all-start = ((f32[128,1,128]{2,1,0:T(1,128)}), f32[128,1,128]{2,1,0:T(1,128)S(1)}, u32[]{:S(2)}, u32[]{:S(2)}) async-start(f32[128,1,128]{2,1,0:T(1,128)} %broadcast_in_dim.2), calls=%async_computation | async-start | bytes 131072 | tf_op jit(solution)/shard_map/all_to_all | solution.py:502
  20.2 0.0 all-reduce.5.cloned.1.call-start
  20.2 1.3 reshape.69.bias_ref
  21.5 1.3 reshape.70.bias_ref
  22.8 1.4 copy.53.codes_ref.refs_1_
  24.3 1.4 copy.54.mixing_ref.refs_2_
  25.7 1.4 copy.57.codes_ref.refs_1_
  27.1 1.4 copy.58.mixing_ref.refs_2_
  28.5 14.6 %forward_one.1 = (bf16[16,256,512]{2,1,0:T(8,128)(2,1)}, bf16[16,256,512]{2,1,0:T(8,128)(2,1)}, bf16[16,256,512]{2,1,0:T(8,128)(2,1)}, bf16[256,1024]{1,0:T(8,12...) custom-call(bf16[512,256]{1,0:T(8,128)(2,1)} %u_ref.1, ...), custom_call_target="tpu_custom_call" | custom-call | tf_op jit(solution)/shard_map/forward_one/pallas_call | solution.py:205
  43.2 19.4 %forward_two.1 = (bf16[16,256,1024]{2,1,0:T(8,128)(2,1)}, bf16[16,256,1024]{2,1,0:T(8,128)(2,1)}, bf16[16,256,1024]{2,1,0:T(8,128)(2,1)}, bf16[256,1024]{1,0:T(8...) custom-call(bf16[256,1024]{1,0:T(8,128)(2,1)} %get-tuple-element.46.u_ref.refs_0_, ...), custom_call_target="tpu_custom_call" | custom-call | tf_op jit(solution)/shard_map/forward_two/pallas_call | solution.py:205
  62.6 0.0 all-to-all-done
  62.6 0.0 copy-start.4
  62.6 0.6 copy-done.4
  63.2 22.3 %backward_two.1 = (f32[256,4096]{1,0:T(8,128)}, f32[16,256,256]{2,1,0:T(8,128)}, f32[8,2,256]{2,1,0:T(2,128)}, f32[56,256]{1,0:T(8,128)}, f32[256,1024]{1,0:T(8,...) custom-call(bf16[256,1024]{1,0:T(8,128)(2,1)} %get-tuple-element.46.u_ref.refs_0_, ...), custom_call_target="tpu_custom_call" | custom-call | tf_op jit(solution)/shard_map/backward_two/pallas_call | solution.py:416
  85.5 0.0 copy-start.7
  85.5 0.0 copy-start.6
  85.5 0.0 copy-start.8
  85.5 16.2 %backward_one.1 = (f32[256,4096]{1,0:T(8,128)}, f32[16,256,256]{2,1,0:T(8,128)}, f32[8,2,256]{2,1,0:T(2,128)}, f32[56,256]{1,0:T(8,128)}, f32[512,256]{1,0:T(8,128)}) custom-call(bf16[256,512]{1,0:T(8,128)(2,1)} %get-tuple-element.55.refs_0_, bf16[256,32]{1,0:T(8,128)(2,1)} %copy.53.codes_ref.refs_1_, bf16[256,8]{1,0:T(8,128)(2,1)} %copy.54.mixing_ref.refs_2_, ...), custom_call_target="tpu_custom_call" | custom-call | tf_op jit(solution)/shard_map/backward_one/pallas_call | solution.py:416
  101.7 0.7 reshape.74
  102.4 0.0 copy-done.7
  102.4 0.8 constant_dynamic-update-slice_fusion.4
  103.3 0.0 copy-done.6
  103.3 0.0 copy-done.8
  103.3 0.0 copy-start.3
  103.3 0.7 copy-done.3
  104.0 0.0 all-reduce.5.cloned.1.call-update
  104.0 223.7 %all-reduce.5.cloned.1.call-done = (f32[152,256]{1,0:T(8,128)}, f32[256,4096]{1,0:T(8,128)}, f32[16,256,256]{2,1,0:T(8,128)}, f32[256,4096]{1,0:T(8,128)}, f32[1...) async-done(((f32[152,256]{1,0:T(8,128)}, f32[256,4096]{1,0:T(8,128)}, f32[16,256,256]{2,1,0:T(8,128)}, f32[256,4096]{1,0:T(8,128)}, f32[16,256,256]{2,1,0:T(8,128)}, ...) | async-done | bytes 17195024 | tf_op jit(solution)/shard_map/psum | solution.py:519
  327.7 1.3 slice_reduce_fusion
  329.0 1.3 fusion
  330.4 1.3 slice_bitcast_fusion.4
  331.7 1.4 fusion.1
  333.1 1.4 slice_bitcast_fusion
  334.5 0.6 copy.62
  335.1 0.6 copy.61
  335.7 0.0 copy-start.2
  335.7 4.8 %copy.73 = f32[256,4096]{1,0:T(8,128)} copy(f32[256,4096]{1,0:T(8,128)} %get-tuple-element.94) | data formatting | bytes 8388608
  340.5 0.0 copy-done.2
  340.5 0.0 copy-start.1
  340.5 2.1 copy.74
  342.6 1.6 copy-done.1
  344.2 0.0 copy-start
  344.2 2.1 copy.75
  346.3 1.6 copy-done
  347.9 2.0 copy.76
  349.9 0.0 copy-done.5
  349.9 0.7 copy.77
  (7 shorter events, 0.0 us)
Async XLA Ops:
  8.7 53.9 %all-to-all-start = ((f32[128,1,128]{2,1,0:T(1,128)}), f32[128,1,128]{2,1,0:T(1,128)S(1)}, u32[]{:S(2)}, u32[]{:S(2)}) async-start(f32[128,1,128]{2,1,0:T(1,128)} %broadcast_in_dim.2), calls=%async_computation | async-start | bytes 131072 | tf_op jit(solution)/shard_map/all_to_all | solution.py:502
  20.2 307.6 %all-reduce.5.cloned.1.call-start = ((), (), s32[]{:S(2)}) async-start(), calls=%async_computation.1 | async-start | bytes 34390016 | tf_op jit(solution)/shard_map/psum | solution.py:519
  62.6 0.6 copy-start.4
  85.5 16.9 %copy-start.7 = (f32[8,2,256]{2,1,0:T(2,128)S(1)}, f32[8,2,256]{2,1,0:T(2,128)}, u32[]{:S(2)}) copy-start(f32[8,2,256]{2,1,0:T(2,128)} %get-tuple-element.67) | copy-start | bytes 49156
  85.5 17.8 %copy-start.6 = (f32[56,256]{1,0:T(8,128)S(1)}, f32[56,256]{1,0:T(8,128)}, u32[]{:S(2)}) copy-start(f32[56,256]{1,0:T(8,128)} %get-tuple-element.66) | copy-start | bytes 172036
  85.5 17.8 %copy-start.8 = (f32[8,128]{1,0:T(8,128)S(1)}, f32[8,128]{1,0:T(8,128)}, u32[]{:S(2)}) copy-start(f32[8,128]{1,0:T(8,128)} %get-tuple-element.68) | copy-start | bytes 12292
  103.3 0.7 copy-start.3
  335.7 4.8 %copy-start.2 = (f32[16,256,256]{2,1,0:T(8,128)S(1)}, f32[16,256,256]{2,1,0:T(8,128)}, u32[]{:S(2)}) copy-start(f32[16,256,256]{2,1,0:T(8,128)} %get-tuple-element.96) | copy-start | bytes 12582916
  340.5 3.7 %copy-start.1 = (f32[256,4096]{1,0:T(8,128)S(1)}, f32[256,4096]{1,0:T(8,128)}, u32[]{:S(2)}) copy-start(f32[256,4096]{1,0:T(8,128)} %get-tuple-element.100) | copy-start | bytes 12582916
  344.2 3.7 %copy-start = (f32[16,256,256]{2,1,0:T(8,128)S(1)}, f32[16,256,256]{2,1,0:T(8,128)}, u32[]{:S(2)}) copy-start(f32[16,256,256]{2,1,0:T(8,128)} %get-tuple-element.102) | copy-start | bytes 12582916
  347.9 2.0 copy-start.5
Sparse Core Ops, SparseCore 0:
  104.1 223.5 all-reduce.4

commit v2 on v1

v2 whole, which is shorter than its diff:
```python
import functools

import jax
import jax.numpy as jnp
from jax import lax
from jax.experimental import pallas as pl
from jax.experimental.pallas import tpu as pltpu
from jax.sharding import Mesh, PartitionSpec as P

EXPERTS = 16
SEL = 4
BITS = 4
TASKS = 2
WIDTH = 256
HID = 256
TOWER = 128
PAIR = 2
STEPS = EXPERTS // PAIR
HALF = STEPS // 2
GROUP = 4
WAVES = EXPERTS // GROUP
SLAB = 1024
SMALL = 1024
HALF_ROWS = 8 * SLAB
ONE = (48, 48, 40)
TWO = (40, 40, 48)
CHUNK = 88
AXES = ((0, 4, 2), (4, 2, 0), (2, 0, 4))
F32 = jnp.float32
BF16 = jnp.bfloat16
ROOT = 0.7978845608028654
CUBE = 0.044715
BYTES = 61 * 1024 * 1024


def nn(a, b):
    return lax.dot_general(a, b, (((1,), (0,)), ((), ())), preferred_element_type=F32)


def nt(a, b):
    return lax.dot_general(a, b, (((1,), (1,)), ((), ())), preferred_element_type=F32)


def tn(a, b):
    return lax.dot_general(a, b, (((0,), (0,)), ((), ())), preferred_element_type=F32)


def pieces(x):
    hi = x.astype(BF16)
    rest = x - hi.astype(F32)
    mid = rest.astype(BF16)
    return hi, mid, (rest - mid.astype(F32)).astype(BF16)


def gelu_both(x):
    square = x * x
    slope = square * (ROOT * CUBE) + ROOT
    s = 0.5 + 0.5 * jnp.tanh(x * slope)
    value = x * s
    return value, s + value * (1.0 - s) * (slope * 6.0 - 4.0 * ROOT)


def soft_parts(mix):
    top = jnp.maximum(jnp.maximum(mix[0], mix[1]), jnp.maximum(mix[2], mix[3]))
    raised = [jnp.exp(m - top) for m in mix]
    total = raised[0] + raised[1] + raised[2] + raised[3]
    return [r / total for r in raised]


def bit_factors(code):
    rows = code[0].shape[1]
    expert = lax.broadcasted_iota(jnp.int32, (EXPERTS, rows), 0)
    found = []
    for i in range(SEL):
        per_bit = []
        for b in range(BITS):
            k = jnp.clip(code[i * BITS + b], -5.0, 5.0)
            s = -0.002 * (k * k * k) + 0.15 * k + 0.5
            on = (expert >> b) & 1 == 1
            per_bit.append(jnp.where(on, s, 1.0 - s))
        found.append(per_bit)
    return found


def gate_of(code, mix):
    w = soft_parts(mix)
    total = None
    for i, f in enumerate(bit_factors(code)):
        r = w[i] * ((f[0] * f[1]) * (f[2] * f[3]))
        total = r if total is None else total + r
    return total


def gate_back(code, mix, grad):
    rows = grad.shape[1]
    expert = lax.broadcasted_iota(jnp.int32, (EXPERTS, rows), 0)
    w = soft_parts(mix)
    grad_w, grad_code = [], []
    for i, f in enumerate(bit_factors(code)):
        low, high = f[0] * f[1], f[2] * f[3]
        grad_w.append(jnp.sum(grad * (low * high), axis=0, keepdims=True))
        up = grad * w[i]
        others = (f[1] * high, f[0] * high, low * f[3], low * f[2])
        for b in range(BITS):
            on = (expert >> b) & 1 == 1
            term = up * others[b]
            ds = jnp.sum(jnp.where(on, term, -term), axis=0, keepdims=True)
            c = code[i * BITS + b]
            k = jnp.clip(c, -5.0, 5.0)
            inside = jnp.where(jnp.abs(c) <= 5.0, 0.15 - 0.006 * (k * k), 0.0)
            grad_code.append(ds * inside)
    mean = w[0] * grad_w[0] + w[1] * grad_w[1] + w[2] * grad_w[2] + w[3] * grad_w[3]
    return grad_code, [w[i] * (grad_w[i] - mean) for i in range(SEL)]


def task_rows(logits, mixes, task, lanes):
    code = [logits[task * 16 + k : task * 16 + k + 1, lanes] for k in range(16)]
    mix = [mixes[task * 4 + k : task * 4 + k + 1, lanes] for k in range(4)]
    return code, mix


def task_lanes(task, rows, shared):
    return slice(0, rows) if shared else slice(task * rows, (task + 1) * rows)


def whole(shape):
    return pl.BlockSpec(shape, lambda *_: (0,) * len(shape))


def tower(
    rows,
    v_ref,
    labels_ref,
    counts_ref,
    lengths_ref,
    base_ref,
    inner_ref,
    bias_ref,
    outer_ref,
    outer_bias_ref,
    predictions_ref,
    small_ref,
    grad_inner_ref,
    dy_ref,
):
    sessions = lengths_ref.shape[1]
    lens = jnp.broadcast_to(lengths_ref[...], (8, sessions)).astype(F32).astype(BF16)
    before = lax.broadcasted_iota(jnp.int32, (sessions, sessions), 0)
    after = lax.broadcasted_iota(jnp.int32, (sessions, sessions), 1)
    upto = jnp.where(before <= after, 1.0, 0.0).astype(BF16)
    ends = nn(lens, upto)[0:1, :]
    starts = ends - lens[0:1, :].astype(F32)
    ids = (lax.broadcasted_iota(jnp.int32, (rows, sessions), 0) + base_ref[0]).astype(F32)
    inside = jnp.where((ids >= starts) & (ids < ends), 1.0, 0.0).astype(BF16)
    row_length = nt(lens, inside)[0:1, :]
    all_rows = float(rows * counts_ref.shape[0])
    weight = (all_rows / sessions) / row_length
    positives = jnp.sum(counts_ref[...], axis=0, keepdims=True)
    bias = bias_ref[...].astype(F32).T
    columns = outer_ref[...].astype(F32).T
    small_ref[...] = jnp.zeros_like(small_ref)
    for t in range(TASKS):
        lanes = slice(t * rows, (t + 1) * rows)
        v = v_ref[:, lanes]
        pre = tn(inner_ref[t], v) + bias[:, t : t + 1]
        hid, slope = gelu_both(pre)
        hid = hid.astype(BF16)
        column = columns[:, t : t + 1]
        logit = jnp.sum(hid.astype(F32) * column, axis=0, keepdims=True)
        logit = logit + outer_bias_ref[0:1, t : t + 1].astype(F32)
        y = labels_ref[t : t + 1, :].astype(F32)
        count = positives[:, t : t + 1]
        ratio = (all_rows - count) / count
        chance = jax.nn.sigmoid(logit)
        predictions_ref[t : t + 1, :] = chance
        grad = weight * (-ratio * y * jax.nn.sigmoid(-logit) + (1.0 - y) * chance)
        grad = grad.astype(BF16)
        back = (grad.astype(F32) * column * slope).astype(BF16)
        picked = lax.broadcasted_iota(jnp.int32, (16, rows), 0)
        stack = jnp.where(picked == 0, grad.astype(F32), jnp.where(picked == 1, 1.0, 0.0))
        stack = stack.astype(BF16)
        by_hid = nt(stack, hid)
        by_back = nt(stack, back)
        small_ref[t : t + 1, :TOWER] = by_hid[0:1]
        small_ref[2 + t : 3 + t, :TOWER] = by_back[1:2]
        total = jnp.sum(grad.astype(F32), axis=1, keepdims=True)
        small_ref[4 + t : 5 + t, :TOWER] = jnp.broadcast_to(total, (1, TOWER))
        grad_inner_ref[t] = nt(v, back)
        dy_ref[:, lanes] = nn(inner_ref[t], back)


def pipeline(count, tiles, stages):
    for slot in range(count + len(stages) - 1):
        for q in range(tiles):
            for late, stage in enumerate(stages):
                if 0 <= slot - late < count:
                    stage(slot - late, q)


def prepare(shared, rows, u, codes_ref, mixing_ref, outer_bias_ref, code_ref, mix_ref, gate_ref, acc_ref):
    code_ref[...] = nn(codes_ref[...], u)
    mix_ref[...] = nn(mixing_ref[...], u)
    outer_bias = outer_bias_ref[...]
    for t in range(TASKS):
        code, mix = task_rows(code_ref, mix_ref, t, task_lanes(t, rows, shared))
        gate = gate_of(code, mix)
        span = slice(t * rows, (t + 1) * rows)
        gate_ref[:, span] = gate
        hi, mid, low = pieces(gate)
        acc_ref[:, span] = tn(outer_bias, hi) + tn(outer_bias, mid) + tn(outer_bias, low)


def forward_wave(shared, rows, wave, u_ref, inner_ref, bias_ref, outer_ref, state, gate_ref, acc_ref, work):
    bias = bias_ref[0].astype(F32).T
    lanes = rows if shared else rows * TASKS
    tiles = lanes // 256
    part = WIDTH // tiles
    tall = 16 * 1024 // lanes
    pre_refs, mid_refs = work[:2], work[2:]
    kept = {}

    def start_pre(p, q):
        if q == 0:
            kept["inner", p] = inner_ref[:, p * HID : (p + 1) * HID].T
        span = slice(q * 256, (q + 1) * 256)
        pre_refs[p % 2][:, span] = nn(kept["inner", p], u_ref[:WIDTH, span])

    def bend(p, q):
        hid_ref, slope_ref, _ = state(p)
        for at in range(q * part, (q + 1) * part, tall):
            here = slice(at, at + tall)
            hid, slope = gelu_both(pre_refs[p % 2][here, :lanes] + bias[here, p : p + 1])
            hid_ref[here, :] = hid.astype(BF16)
            slope_ref[here, :] = slope.astype(BF16)

    def start_out(p, q):
        if q == 0:
            kept["outer", p] = outer_ref[p].T
        span = slice(q * 256, (q + 1) * 256)
        mid_refs[p % 2][:, span] = nn(kept["outer", p], state(p)[0][:, span])

    def combine(p, q):
        if q == 0:
            kept["gate", p] = gate_ref[pl.ds(wave * GROUP + p, 1), :]
        gate = kept["gate", p]
        for at in range(q * part, (q + 1) * part, tall):
            here = slice(at, at + tall)
            out = mid_refs[p % 2][here, :lanes]
            state(p)[2][here, :] = out.astype(BF16)
            for t in range(TASKS if shared else 1):
                span = slice(t * rows, (t + 1) * rows) if shared else slice(0, lanes)
                acc_ref[here, span] += gate[:, span] * out

    pipeline(GROUP, tiles, (start_pre, bend, start_out, combine))


def backward_wave(shared, rows, wave, aug_ref, inner_ref, outer_ref, state, gate_ref, dy_ref, acc_ref, dgate_ref, slab_ref, bias_ref, dout_ref, dpre_ref, work):
    lanes = rows if shared else rows * TASKS
    tiles = lanes // 256
    part = WIDTH // tiles
    tall = 16 * 1024 // lanes
    tasks = TASKS if shared else 1
    spans = [slice(t * rows, (t + 1) * rows) if shared else slice(0, lanes) for t in range(tasks)]
    kept = {}

    def share(p, q):
        e = pl.ds(wave * GROUP + p, 1)
        if q == 0:
            kept["gate", p] = gate_ref[e, :]
            kept["sum", p] = [None] * tasks
        gate, sums = kept["gate", p], kept["sum", p]
        for at in range(q * part, (q + 1) * part, tall):
            here = slice(at, at + tall)
            dys = [dy_ref[here, s] for s in spans]
            dout = gate[:, spans[0]] * dys[0]
            if shared:
                dout = dout + gate[:, spans[1]] * dys[1]
            dout_ref[p, here, :] = dout.astype(BF16)
            out = state(p)[2][here, :].astype(F32)
            for t in range(tasks):
                term = jnp.sum((out * dys[t]).reshape(tall // 8, 8, -1), axis=0)
                sums[t] = term if at == 0 else sums[t] + term
        if q == tiles - 1:
            for t in range(tasks):
                dgate_ref[e, spans[t]] = jnp.sum(sums[t], axis=0, keepdims=True)

    def back_out(p, q):
        span = slice(q * 256, (q + 1) * 256)
        work[p % 2][:, span] = nn(outer_ref[p], dout_ref[p, :, span])

    def unbend(p, q):
        slope_ref = state(p)[1]
        for at in range(q * part, (q + 1) * part, tall):
            here = slice(at, at + tall)
            dpre = work[p % 2][here, :lanes] * slope_ref[here, :].astype(F32)
            dpre_ref[p * HID + at : p * HID + at + tall, :] = dpre.astype(BF16)

    def grads(p, q):
        if q == 0:
            grad = nt(state(p)[0][...], dout_ref[p])
            slab_ref[p, :HID] = grad[:, :128]
            slab_ref[p, 512 : 512 + HID] = grad[:, 128:]
        if q == tiles // 2:
            grad = nt(aug_ref[...], dpre_ref[p * HID : (p + 1) * HID, :])
            slab_ref[p, HID:512] = grad[:WIDTH, :128]
            slab_ref[p, 512 + HID :] = grad[:WIDTH, 128:]
            bias_ref[0, p : p + 1, :] = grad[WIDTH : WIDTH + 1]

    pipeline(GROUP, tiles, (share, back_out, unbend, grads))
    acc_ref[...] += nn(inner_ref[...], dpre_ref[...])


def finish(shared, rows, u, codes_ref, mixing_ref, outer_bias_ref, code_ref, mix_ref, gate_ref, dy_ref, dgate_ref, acc_ref, dcode_ref, dmix_ref, rest_ref):
    dcode_ref[...] = jnp.zeros_like(dcode_ref)
    dmix_ref[...] = jnp.zeros_like(dmix_ref)
    outer_bias = outer_bias_ref[...]
    for t in range(TASKS):
        span = slice(t * rows, (t + 1) * rows)
        here = task_lanes(t, rows, shared)
        hi, mid, low = pieces(dy_ref[:, span])
        upto = nn(outer_bias, hi) + nn(outer_bias, mid) + nn(outer_bias, low)
        code, mix = task_rows(code_ref, mix_ref, t, here)
        grad_code, grad_mix = gate_back(code, mix, dgate_ref[:, span] + upto)
        for k in range(16):
            dcode_ref[t * 16 + k : t * 16 + k + 1, here] = grad_code[k]
        for k in range(4):
            dmix_ref[t * 4 + k : t * 4 + k + 1, here] = grad_mix[k]
    dcode = dcode_ref[...].astype(BF16)
    dmix = dmix_ref[...].astype(BF16)
    rest_ref[:32, :] = nt(dcode, u)
    rest_ref[32:40, :] = nt(dmix, u)
    g_hi, g_mid, _ = pieces(gate_ref[...])
    y_hi, y_mid, _ = pieces(dy_ref[...])
    rest_ref[40:56, :] = nt(g_hi, y_hi) + nt(g_hi, y_mid) + nt(g_mid, y_hi)
    return acc_ref[...] + tn(codes_ref[...], dcode) + tn(mixing_ref[...], dmix)


def extend(aug_ref, u):
    aug_ref[:WIDTH, :] = u
    one = lax.broadcasted_iota(jnp.int32, (16, u.shape[1]), 0) == 0
    aug_ref[WIDTH:, :] = jnp.where(one, 1.0, 0.0).astype(BF16)


def first_kernel(rows, tokens_ref, codes_ref, mixing_ref, inner_ref, bias_ref, outer_ref, outer_bias_ref, *refs):
    (hid_ref, slope_ref, out_ref, gate_ref, code_ref, mix_ref, turned, next_ref, acc_ref), work = refs[:9], refs[9:]
    step = pl.program_id(0)

    @pl.when(step == 0)
    def _():
        turned[...] = tokens_ref[...].astype(F32).T.astype(BF16)
        prepare(True, rows, turned[...], codes_ref, mixing_ref, outer_bias_ref, code_ref, mix_ref, gate_ref, acc_ref)

    def state(p):
        return hid_ref.at[p], slope_ref.at[p], out_ref.at[p]

    forward_wave(True, rows, step, turned, inner_ref, bias_ref, outer_ref, state, gate_ref, acc_ref, work)

    @pl.when(step == WAVES - 1)
    def _():
        next_ref[...] = acc_ref[...].astype(BF16)


def first_part(tokens, codes, mixing, inner, inner_bias, outer, outer_bias):
    rows = tokens.shape[0]
    wide = rows * TASKS
    state = jax.ShapeDtypeStruct((EXPERTS, HID, rows), BF16)
    plain = [
        jax.ShapeDtypeStruct((EXPERTS, wide), F32),
        jax.ShapeDtypeStruct((32, rows), F32),
        jax.ShapeDtypeStruct((8, rows), F32),
        jax.ShapeDtypeStruct((WIDTH, rows), BF16),
        jax.ShapeDtypeStruct((WIDTH, wide), BF16),
    ]
    state_spec = pl.BlockSpec((GROUP, HID, rows), lambda i: (i, 0, 0))
    return pl.pallas_call(
        functools.partial(first_kernel, rows),
        grid=(WAVES,),
        in_specs=[
            whole(tokens.shape),
            whole(codes.shape),
            whole(mixing.shape),
            pl.BlockSpec((WIDTH, GROUP * HID), lambda i: (0, i)),
            pl.BlockSpec((1, GROUP, HID), lambda i: (i, 0, 0)),
            pl.BlockSpec((GROUP, HID, WIDTH), lambda i: (i, 0, 0)),
            whole(outer_bias.shape),
        ],
        out_specs=[state_spec] * 3 + [whole(s.shape) for s in plain],
        out_shape=[state] * 3 + plain,
        scratch_shapes=[pltpu.VMEM((WIDTH, wide), F32)] + [pltpu.VMEM((HID, rows), F32)] * 4,
        cost_estimate=pl.CostEstimate(flops=8_000_000_000, bytes_accessed=20_000_000, transcendentals=0),
        compiler_params=pltpu.CompilerParams(
            dimension_semantics=("arbitrary",), vmem_limit_bytes=BYTES
        ),
        name="first_part",
    )(tokens, codes, mixing, inner, inner_bias.reshape(WAVES, GROUP, HID), outer, outer_bias)


def main_kernel(rows, core_ref, *refs):
    (u_ref, codes_two, mixing_two, inner_two, bias_two, outer_two, outer_bias_two), refs = refs[:7], refs[7:]
    tower_in, refs = refs[:8], refs[8:]
    (send_ref, keep_ref, grad_bias, rest_ref, dy_one), refs = refs[:5], refs[5:]
    tower_out, refs = refs[:3], refs[3:]
    (hid_two, slope_two, out_two, gate_two, code_two, mix_two, aug, v_ref), refs = refs[:8], refs[8:]
    (acc_ref, dy_two, dgate_ref, dcode_ref, dmix_ref, dout_ref, dpre_ref), work = refs[:7], refs[7:]
    step = pl.program_id(0)

    def state_two(wave):
        return lambda p: tuple(r.at[wave * GROUP + p] for r in (hid_two, slope_two, out_two))

    @pl.when(step == 0)
    def _():
        extend(aug, u_ref[...])
        prepare(False, rows, u_ref[...], codes_two, mixing_two, outer_bias_two, code_two, mix_two, gate_two, acc_ref)

    @pl.when(step < WAVES)
    def _():
        forward_wave(False, rows, step, aug, inner_two, bias_two, outer_two, state_two(step), gate_two, acc_ref, work)

    @pl.when(step == WAVES)
    def _():
        v_ref[...] = acc_ref[...].astype(BF16)
        tower(rows, v_ref, *tower_in, *tower_out, dy_two)
        acc_ref[...] = jnp.zeros_like(acc_ref)

    def back(slab_ref):
        wave = (step + 2 * (1 - core_ref[0])) % WAVES
        backward_wave(False, rows, wave, aug, inner_two, outer_two, state_two(wave), gate_two, dy_two, acc_ref, dgate_ref, slab_ref, grad_bias, dout_ref, dpre_ref, work)

    @pl.when((step >= WAVES) & (step < WAVES + 2))
    def _():
        back(send_ref)

    @pl.when(step >= WAVES + 2)
    def _():
        back(keep_ref)

    @pl.when(step == 2 * WAVES - 1)
    def _():
        dy_one[...] = finish(False, rows, u_ref[...], codes_two, mixing_two, outer_bias_two, code_two, mix_two, gate_two, dy_two, dgate_ref, acc_ref, dcode_ref, dmix_ref, rest_ref)


def fixed(shape):
    return pl.BlockSpec(shape, lambda i, core: (0,) * len(shape))


def main_part(core, u, codes, mixing, inner, inner_bias, outer, outer_bias, tower_in):
    wide = u.shape[1]
    rows = wide // TASKS

    def order(i, core):
        return jnp.where(i < WAVES, i, (i + 2 * (1 - core[0])) % WAVES)

    def back(i, core):
        return (jnp.maximum(i, WAVES) + 2 * (1 - core[0])) % WAVES

    slab = jax.ShapeDtypeStruct((EXPERTS // 2, SLAB, 128), F32)

    def slab_spec(begin):
        return pl.BlockSpec((GROUP, SLAB, 128), lambda i, core: (jnp.clip(i - begin, 0, 1), 0, 0))

    rest = [
        jax.ShapeDtypeStruct((56, WIDTH), F32),
        jax.ShapeDtypeStruct((WIDTH, wide), F32),
        jax.ShapeDtypeStruct((TASKS, rows), F32),
        jax.ShapeDtypeStruct((8, TOWER), F32),
        jax.ShapeDtypeStruct((TASKS, WIDTH, TOWER), F32),
    ]
    tower_specs = [fixed(a.shape) for a in tower_in]
    tower_specs[3] = pl.BlockSpec(memory_space=pltpu.SMEM)
    return pl.pallas_call(
        functools.partial(main_kernel, rows),
        grid_spec=pltpu.PrefetchScalarGridSpec(
            num_scalar_prefetch=1,
            grid=(2 * WAVES,),
            in_specs=[
                fixed(u.shape),
                fixed(codes.shape),
                fixed(mixing.shape),
                pl.BlockSpec((WIDTH, GROUP * HID), lambda i, core: (0, order(i, core))),
                pl.BlockSpec((1, GROUP, HID), lambda i, core: (order(i, core), 0, 0)),
                pl.BlockSpec((GROUP, HID, WIDTH), lambda i, core: (order(i, core), 0, 0)),
                fixed(outer_bias.shape),
            ]
            + tower_specs,
            out_specs=[slab_spec(WAVES), slab_spec(WAVES + 2)]
            + [pl.BlockSpec((1, GROUP, HID), lambda i, core: (back(i, core), 0, 0))]
            + [fixed(s.shape) for s in rest],
            scratch_shapes=[
                *[pltpu.VMEM((EXPERTS, HID, wide), BF16)] * 3,
                pltpu.VMEM((EXPERTS, wide), F32),
                pltpu.VMEM((32, wide), F32),
                pltpu.VMEM((8, wide), F32),
                pltpu.VMEM((WIDTH + 16, wide), BF16),
                pltpu.VMEM((WIDTH, wide), BF16),
                pltpu.VMEM((WIDTH, wide), F32),
                pltpu.VMEM((WIDTH, wide), F32),
                pltpu.VMEM((EXPERTS, wide), F32),
                pltpu.VMEM((32, wide), F32),
                pltpu.VMEM((8, wide), F32),
                pltpu.VMEM((GROUP, WIDTH, wide), BF16),
                pltpu.VMEM((GROUP * HID, wide), BF16),
                *[pltpu.VMEM((HID, wide), F32)] * 4,
            ],
        ),
        out_shape=[slab, slab, jax.ShapeDtypeStruct((WAVES, GROUP, HID), F32)] + rest,
        cost_estimate=pl.CostEstimate(flops=14_000_000_000, bytes_accessed=40_000_000, transcendentals=0),
        compiler_params=pltpu.CompilerParams(
            dimension_semantics=("arbitrary",), vmem_limit_bytes=BYTES
        ),
        name="main_part",
    )(
        core,
        u,
        codes,
        mixing,
        inner,
        inner_bias.reshape(WAVES, GROUP, HID),
        outer,
        outer_bias,
        *tower_in,
    )


def last_kernel(sending, rows, core_ref, *refs):
    (u_ref, inner_ref, outer_ref, hid_ref, slope_ref, out_ref, gate_ref, dy_ref), refs = refs[:8], refs[8:]
    step = pl.program_id(0)
    if sending:
        (slab_ref, bias_ref, acc_ref, dgate_ref), refs = refs[:4], refs[4:]
        aug, dout_ref, dpre_ref, *work = refs
        wave = step + 2 * (1 - core_ref[0])
        bias_at = bias_ref
    else:
        (acc_in, dgate_in, codes_ref, mixing_ref, outer_bias_ref, code_ref, mix_ref), refs = refs[:7], refs[7:]
        (other_bias, bias_two, rest_two, little, tower_inner), refs = refs[:5], refs[5:]
        (slab_ref, back_ref, small_send, small_keep), refs = refs[:4], refs[4:]
        aug, dout_ref, dpre_ref, acc_ref, dgate_ref, dcode_ref, dmix_ref, bias_ref, rest_ref, small_ref, *work = refs
        wave = step + 2 * core_ref[0]
        bias_at = bias_ref.at[pl.ds(step, 1)]

    @pl.when(step == 0)
    def _():
        extend(aug, u_ref[...])
        if sending:
            acc_ref[...] = jnp.zeros_like(acc_ref)
            dgate_ref[...] = jnp.zeros_like(dgate_ref)
        else:
            acc_ref[...] = acc_in[...]
            dgate_ref[...] = dgate_in[...]

    def state(p):
        return hid_ref.at[p], slope_ref.at[p], out_ref.at[p]

    backward_wave(True, rows, wave, aug, inner_ref, outer_ref, state, gate_ref, dy_ref, acc_ref, dgate_ref, slab_ref, bias_at, dout_ref, dpre_ref, work)
    if sending:
        return

    @pl.when(step == 1)
    def _():
        du = finish(True, rows, u_ref[...], codes_ref, mixing_ref, outer_bias_ref, code_ref, mix_ref, gate_ref, dy_ref, dgate_ref, acc_ref, dcode_ref, dmix_ref, rest_ref)
        back_ref[...] = du.T
        core = core_ref[0]
        small_ref[0:256, :] = tower_inner[0]
        small_ref[256:512, :] = tower_inner[1]
        small_ref[808:, :] = jnp.zeros((SMALL - 808, 128), F32)
        for at, ref in ((512, rest_ref), (624, rest_two)):
            small_ref[at : at + 56, :] = ref[:, :128]
            small_ref[at + 56 : at + 112, :] = ref[:, 128:]
        for w in range(WAVES):
            mine, j = core == w // 2, w % 2
            rows_one = jnp.where(mine, bias_ref[j], other_bias[w])
            for at, found in ((736, rows_one), (768, bias_two[w])):
                at += GROUP * w
                small_ref[at : at + GROUP, :] = found[:, :128]
                small_ref[at + 16 : at + 16 + GROUP, :] = found[:, 128:]
        small_ref[800:808, :] = little[...]
        small_send[...] = small_ref[pl.ds((1 - core) * 512, 512), :]
        small_keep[...] = small_ref[pl.ds(core * 512, 512), :]


def last_part(sending, core, u, inner, outer, state, gate, dy, more):
    rows = u.shape[1]

    def wave(i, core):
        return i + 2 * (1 - core[0] if sending else core[0])

    state_spec = pl.BlockSpec((GROUP, HID, rows), lambda i, core: (wave(i, core), 0, 0))
    arrays = [u, inner, outer, *state, gate, dy, *more]
    in_specs = [
        fixed(u.shape),
        pl.BlockSpec((WIDTH, GROUP * HID), lambda i, core: (0, wave(i, core))),
        pl.BlockSpec((GROUP, HID, WIDTH), lambda i, core: (wave(i, core), 0, 0)),
        state_spec,
        state_spec,
        state_spec,
    ]
    in_specs += [fixed(a.shape) for a in arrays[6:]]
    out_shape = [jax.ShapeDtypeStruct((EXPERTS // 2, SLAB, 128), F32)]
    out_specs = [pl.BlockSpec((GROUP, SLAB, 128), lambda i, core: (i, 0, 0))]
    scratch = [
        pltpu.VMEM((WIDTH + 16, rows), BF16),
        pltpu.VMEM((GROUP, WIDTH, rows), BF16),
        pltpu.VMEM((GROUP * HID, rows), BF16),
    ]
    if sending:
        out_shape.append(jax.ShapeDtypeStruct((WAVES, GROUP, HID), F32))
        out_specs.append(pl.BlockSpec((1, GROUP, HID), lambda i, core: (wave(i, core), 0, 0)))
        added = [
            jax.ShapeDtypeStruct((WIDTH, rows), F32),
            jax.ShapeDtypeStruct((EXPERTS, TASKS * rows), F32),
        ]
    else:
        added = [
            jax.ShapeDtypeStruct((rows, WIDTH), F32),
            jax.ShapeDtypeStruct((SMALL // 2, 128), F32),
            jax.ShapeDtypeStruct((SMALL // 2, 128), F32),
        ]
        scratch += [
            pltpu.VMEM((WIDTH, rows), F32),
            pltpu.VMEM((EXPERTS, TASKS * rows), F32),
            pltpu.VMEM((32, rows), F32),
            pltpu.VMEM((8, rows), F32),
            pltpu.VMEM((2, GROUP, HID), F32),
            pltpu.VMEM((56, WIDTH), F32),
            pltpu.VMEM((SMALL, 128), F32),
        ]
    scratch += [pltpu.VMEM((HID, rows), F32)] * 2
    out_shape += added
    out_specs += [fixed(s.shape) for s in added]
    return pl.pallas_call(
        functools.partial(last_kernel, sending, rows),
        grid_spec=pltpu.PrefetchScalarGridSpec(
            num_scalar_prefetch=1,
            grid=(2,),
            in_specs=in_specs,
            out_specs=out_specs,
            scratch_shapes=scratch,
        ),
        out_shape=out_shape,
        cost_estimate=pl.CostEstimate(flops=8_000_000_000, bytes_accessed=20_000_000, transcendentals=0),
        compiler_params=pltpu.CompilerParams(
            dimension_semantics=("arbitrary",), vmem_limit_bytes=40 * 1024 * 1024
        ),
        name="last_send" if sending else "last_keep",
    )(core, *arrays)


def place(chip, core):
    found = []
    for axes in AXES:
        halves = []
        for shift in axes:
            low, high = (chip >> shift) & 1, (chip >> (shift + 1)) & 1
            halves += [jnp.where(core == 0, low ^ high, high), jnp.where(core == 0, high, low)]
        found.append(halves)
    return found


def swaps(shift, step):
    pairs = []
    for chip in range(64):
        c = (chip >> shift) & 3
        for core in range(2):
            n = c ^ 1 if (core + step) % 2 == 0 else 3 - c
            pairs.append((chip * 2 + core, (chip + ((n - c) << shift)) * 2 + core))
    return pairs


def swap(step, sent):
    return [
        lax.ppermute(s, ("chip", "core"), swaps(axes[step // 2], step))
        for s, axes in zip(sent, AXES)
    ]


def plain_call(kernel, sizes, name, chip, core, *arrays, scratch=()):
    smem = pl.BlockSpec(memory_space=pltpu.SMEM)
    vmem = pl.BlockSpec(memory_space=pltpu.VMEM)
    return pl.pallas_call(
        kernel,
        in_specs=[smem, smem] + [vmem] * len(arrays),
        out_specs=[vmem] * len(sizes),
        out_shape=[jax.ShapeDtypeStruct((n, 128), F32) for n in sizes],
        scratch_shapes=scratch,
        cost_estimate=pl.CostEstimate(flops=0, bytes_accessed=2_000_000, transcendentals=0),
        compiler_params=pltpu.CompilerParams(vmem_limit_bytes=28 * 1024 * 1024),
        name=name,
    )(chip, core, *arrays)


def span(at, h, size):
    return pl.ds(pl.multiple_of(at + h * size, 8), size)


def open_kernel(counts, with_small, chip_ref, core_ref, keep_ref, got_ref, *refs):
    if with_small:
        (small_keep, small_got), refs = refs[:2], refs[2:]
        tail_ref = refs[-1]
        tail_ref[:2048, :] = keep_ref[6144:, :] + got_ref[6144:, :]
        tail_ref[2048:, :] = small_keep[...] + small_got[...]
    places = place(chip_ref[0], core_ref[0])
    at = kept = 0
    for i, m in enumerate(counts):
        size, h = 32 * m, places[i][0]

        def read(h):
            if with_small and i == 2:
                return tail_ref[span(0, h, size), :]
            return keep_ref[span(at, h, size), :] + got_ref[span(at, h, size), :]

        refs[i][...] = read(1 - h)
        refs[3][kept : kept + size, :] = read(h)
        at, kept = at + 2 * size, kept + size


def open_rows(counts, chip, core, keep, got, *small):
    sizes = [32 * m for m in counts]
    return plain_call(
        functools.partial(open_kernel, counts, bool(small)),
        sizes + [sum(sizes)],
        "open_one" if small else "open_two",
        chip,
        core,
        keep.reshape(HALF_ROWS, 128),
        got.reshape(HALF_ROWS, 128),
        *small,
        scratch=[pltpu.VMEM((2560, 128), F32)] if small else [],
    )


def halve_kernel(step, sizes, chip_ref, core_ref, keep_ref, *refs):
    got, sent, kept_ref = refs[:3], refs[3:6], refs[6]
    places = place(chip_ref[0], core_ref[0])
    at = kept = 0
    for i, size in enumerate(sizes):
        half, h = size // 2, places[i][step]
        sent[i][...] = keep_ref[span(at, 1 - h, half), :] + got[i][span(0, 1 - h, half), :]
        kept_ref[kept : kept + half, :] = keep_ref[span(at, h, half), :] + got[i][span(0, h, half), :]
        at, kept = at + size, kept + half


def halve(step, sizes, chip, core, keep, got):
    halves = [s // 2 for s in sizes]
    return plain_call(
        functools.partial(halve_kernel, step, sizes),
        halves + [sum(halves)],
        "halve_%d" % step,
        chip,
        core,
        keep,
        *got,
    )


def blend_kernel(chip_ref, core_ref, one_ref, two_ref, *refs):
    got_one, got_two, sent, kept_ref = refs[:3], refs[3:6], refs[6:9], refs[9]
    places = place(chip_ref[0], core_ref[0])
    at_one = at_two = 0
    for i in range(3):
        h = places[i][2]
        for ref, got, at, m, begin in (
            (one_ref, got_one[i], at_one, ONE[i], 0),
            (two_ref, got_two[i], at_two, TWO[i], ONE[i]),
        ):
            for k in range(8):
                for side, out, base in ((1 - h, sent[i], 0), (h, kept_ref, 704 * i)):
                    start = pl.multiple_of(side * (8 * m) + m * k, 8)
                    value = ref[pl.ds(at + start, m), :] + got[pl.ds(start, m), :]
                    out[base + CHUNK * k + begin : base + CHUNK * k + begin + m, :] = value
        at_one, at_two = at_one + 16 * ONE[i], at_two + 16 * TWO[i]


def blend(chip, core, one, two, got_one, got_two):
    return plain_call(
        blend_kernel, [704] * 3 + [2112], "blend", chip, core, one, two, *got_one, *got_two
    )


def close_kernel(chip_ref, core_ref, keep_ref, *refs):
    for i in range(3):
        refs[3 + i][...] = keep_ref[CHUNK * i : CHUNK * (i + 1), :] + refs[i][...]


def double_kernel(step, chip_ref, core_ref, *refs):
    places = place(chip_ref[0], core_ref[0])
    for i in range(3):
        own, got, out = refs[i], refs[3 + i], refs[6 + i]
        n, h = own.shape[0], places[i][step]
        out[span(0, h, n), :] = own[...]
        out[span(0, 1 - h, n), :] = got[...]


def double(step, chip, core, own, got):
    return plain_call(
        functools.partial(double_kernel, step),
        [2 * own[0].shape[0]] * 3,
        "double_%d" % step,
        chip,
        core,
        *own,
        *got,
    )


def layer_rows(layer):
    counts, begin = (ONE, (0, 0, 0)) if layer == 0 else (TWO, ONE)
    return [(i, counts[i], begin[i]) for i in range(3)]


def lay_kernel(mine, chip_ref, core_ref, *refs):
    own, got, refs = refs[:3], refs[3:6], refs[6:]
    if not mine:
        small_in, refs = refs[0], refs[5:]
    outs, refs = refs[:4], refs[4:]
    core = core_ref[0] if mine else 1 - core_ref[0]
    first = [p[0] for p in place(chip_ref[0], core)]
    step = pl.program_id(0)

    def rows_of(i, chunk, begin, count):
        lower = chunk < 32
        at = (chunk % 32) * CHUNK + begin
        a, b = own[i][at : at + count, :], got[i][at : at + count, :]
        return jnp.where((first[i] == 0) == lower, a, b)

    def put(layer, row, value):
        e, part, at = row // SLAB % PAIR, row // 256 % 4, row % 256
        count = value.shape[0]
        lanes = slice(128 * (part // 2), 128 * (part // 2 + 1))
        if part % 2 == 0:
            outs[2 * layer + 1][e, at : at + count, lanes] = value
        else:
            lanes = slice(e * HID + lanes.start, e * HID + lanes.stop)
            outs[2 * layer][at : at + count, lanes] = value

    for s in range(4):

        @pl.when(step == s)
        def _():
            for layer in range(2):
                base = 0
                for i, m, begin in layer_rows(layer):
                    for chunk in range(64):
                        row = base + chunk * m
                        low, high = max(row, s * 2 * SLAB), min(row + m, (s + 1) * 2 * SLAB)
                        while low < high:
                            stop = min(high, (low // 256 + 1) * 256)
                            put(layer, low, rows_of(i, chunk, begin + low - row, stop - low))
                            low = stop
                    base += 64 * m

    def small_rows():
        found = []
        m = ONE[2]
        for chunk in range(64):
            row = 6144 + chunk * m
            low = max(row, HALF_ROWS)
            if low < row + m:
                found.append((low - HALF_ROWS, rows_of(2, chunk, low - row, row + m - low)))
        return found

    if mine:
        (small_out,) = refs

        @pl.when(step == 0)
        def _():
            for at, value in small_rows():
                small_out[at : at + value.shape[0], :] = value

        return

    codes_one, mix_one, back_one, bias_one = refs[:4]
    codes_two, mix_two, back_two, bias_two = refs[4:8]
    tower_inner, tower_bias, tower_outer, tower_last, acc_ref = refs[8:]

    @pl.when(step == 0)
    def _():
        half = 512 * core
        acc_ref[pl.ds(pl.multiple_of(512 - half, 8), 512), :] = small_in[...]
        for at, value in small_rows():
            acc_ref[pl.ds(pl.multiple_of(half + at, 8), value.shape[0]), :] = value
        tower_inner[0] = acc_ref[0:256, :]
        tower_inner[1] = acc_ref[256:512, :]
        for s in range(2):
            lanes = slice(s * 128, (s + 1) * 128)
            for at, codes, mix, back in (
                (512, codes_one, mix_one, back_one),
                (624, codes_two, mix_two, back_two),
            ):
                at += 56 * s
                codes[:, lanes] = acc_ref[at : at + 32, :]
                mix[:, lanes] = acc_ref[at + 32 : at + 40, :]
                back[:, lanes] = acc_ref[at + 40 : at + 56, :]
            bias_one[:, lanes] = acc_ref[736 + 16 * s : 752 + 16 * s, :]
            bias_two[:, lanes] = acc_ref[768 + 16 * s : 784 + 16 * s, :]
        tower_outer[...] = acc_ref[800:802, :]
        tower_bias[...] = acc_ref[802:804, :]
        lane = lax.broadcasted_iota(jnp.int32, (1, 128), 1)
        tower_last[...] = jnp.where(lane == 0, acc_ref[804:805, :], acc_ref[805:806, :])


def lay(mine, chip, core, own, got, more):
    def at(core):
        return core[0] if mine else 1 - core[0]

    shapes = [(WIDTH, EXPERTS * HID), (EXPERTS, HID, WIDTH)] * 2
    out_specs = [
        pl.BlockSpec((WIDTH, PAIR * HID), lambda i, chip, core: (0, 4 * at(core) + i)),
        pl.BlockSpec((PAIR, HID, WIDTH), lambda i, chip, core: (4 * at(core) + i, 0, 0)),
    ] * 2

    def still(shape):
        return pl.BlockSpec(shape, lambda i, chip, core: (0,) * len(shape))

    in_specs = [still(a.shape) for a in (*own, *got)]
    if mine:
        little = [(SMALL // 2, 128)]
        scratch, aliases = [], {}
    else:
        in_specs += [still(more[0].shape)] + [pl.BlockSpec(memory_space=pl.ANY)] * 4
        aliases = {9: 0, 10: 1, 11: 2, 12: 3}
        little = [(32, WIDTH), (8, WIDTH), (EXPERTS, WIDTH), (EXPERTS, HID)] * 2
        little += [(TASKS, WIDTH, TOWER), (TASKS, TOWER), (TASKS, TOWER), (1, 128)]
        scratch = [pltpu.VMEM((SMALL, 128), F32)]
    shapes += little
    out_specs += [still(s) for s in little]
    return pl.pallas_call(
        functools.partial(lay_kernel, mine),
        grid_spec=pltpu.PrefetchScalarGridSpec(
            num_scalar_prefetch=2,
            grid=(4,),
            in_specs=in_specs,
            out_specs=out_specs,
            scratch_shapes=scratch,
        ),
        out_shape=[jax.ShapeDtypeStruct(s, F32) for s in shapes],
        input_output_aliases=aliases,
        cost_estimate=pl.CostEstimate(flops=0, bytes_accessed=16_000_000, transcendentals=0),
        compiler_params=pltpu.CompilerParams(
            dimension_semantics=("arbitrary",), vmem_limit_bytes=32 * 1024 * 1024
        ),
        name="lay_own" if mine else "lay_other",
    )(chip, core, *own, *got, *more)


def on_device(
    tokens,
    labels,
    lengths,
    codes_one,
    mixing_one,
    inner_one,
    inner_bias_one,
    outer_one,
    outer_bias_one,
    codes_two,
    mixing_two,
    inner_two,
    inner_bias_two,
    outer_two,
    outer_bias_two,
    tower_inner,
    tower_inner_bias,
    tower_outer,
    tower_outer_bias,
):
    rows = tokens.shape[0]
    core = lax.axis_index("core").astype(jnp.int32).reshape(1)
    chip = lax.axis_index("chip").astype(jnp.int32).reshape(1)
    base = (lax.axis_index(("chip", "core")) * rows).astype(jnp.int32).reshape(1)

    def cross(a):
        return lax.ppermute(a, "core", [(0, 1), (1, 0)])

    codes_one, mixing_one, codes_two, mixing_two = (
        codes_one.T,
        mixing_one.T,
        codes_two.T,
        mixing_two.T,
    )
    count = jnp.sum(labels.astype(F32), axis=0)
    sent = jnp.broadcast_to(jnp.pad(count, (0, 126))[None, :], (128, 128))
    counts = lax.all_to_all(sent, ("chip", "core"), 0, 0, tiled=True)
    *state, gate, code, mix, u, u_two = first_part(
        tokens, codes_one, mixing_one, inner_one, inner_bias_one, outer_one, outer_bias_one
    )
    towers = (tower_inner, tower_inner_bias, tower_outer, tower_outer_bias.reshape(1, TASKS))
    towers = (labels.T, counts, lengths.reshape(1, -1), base, *towers)
    send, keep_two, bias_two, rest_two, dy, predictions, little, grad_tower_inner = main_part(
        core, u_two, codes_two, mixing_two, inner_two, inner_bias_two, outer_two, outer_bias_two, towers
    )
    got_two = cross(send)
    send, bias_one, acc, dgate = last_part(
        True, core, u, inner_one, outer_one, state, gate, dy, ()
    )
    got_one = cross(send)
    *sent, kept_two = open_rows(TWO, chip, core, keep_two, got_two)
    got_two = swap(0, sent)
    more = (acc, dgate, codes_one, mixing_one, outer_bias_one, code, mix)
    more += (bias_one, bias_two, rest_two, little, grad_tower_inner)
    keep_one, grad_tokens, small_send, small_keep = last_part(
        False, core, u, inner_one, outer_one, state, gate, dy, more
    )
    small_got = cross(small_send)
    *got_two, keep_one = lax.optimization_barrier((*got_two, keep_one))
    *sent, kept_two = halve(1, [32 * m for m in TWO], chip, core, kept_two, got_two)
    got_two = swap(1, sent)
    *sent, kept_one = open_rows(ONE, chip, core, keep_one, got_one, small_keep, small_got)
    got_one = swap(0, sent)
    *sent, kept_one = halve(1, [32 * m for m in ONE], chip, core, kept_one, got_one)
    got_one = swap(1, sent)
    *sent, kept = blend(chip, core, kept_one, kept_two, got_one, got_two)
    for step in (3, 4, 5):
        got = swap(step - 1, sent)
        *sent, kept = halve(step, [CHUNK * 64 >> step] * 3, chip, core, kept, got)
    got = swap(5, sent)
    own = plain_call(close_kernel, [CHUNK] * 3, "close", chip, core, kept, *got)
    for step in (5, 4, 3, 2, 1):
        own = double(step, chip, core, own, swap(step, own))
    got = swap(0, own)
    own_other = [cross(a) for a in own]
    got_other = [cross(a) for a in got]
    *found, small = lay(True, chip, core, own, got, ())
    found = lay(False, chip, core, own_other, got_other, (small, *found))
    inner_one, outer_one, inner_two, outer_two = found[:4]
    codes_one, mix_one, back_one, bias_one, codes_two, mix_two, back_two, bias_two = found[4:12]
    tower_inner, tower_bias, tower_outer, tower_last = found[12:]
    return (
        predictions.T,
        grad_tokens,
        codes_one.T,
        mix_one.T,
        inner_one,
        bias_one.reshape(-1),
        outer_one,
        back_one,
        codes_two.T,
        mix_two.T,
        inner_two,
        bias_two.reshape(-1),
        outer_two,
        back_two,
        tower_inner,
        tower_bias,
        tower_outer,
        tower_last[0, :2],
    )


def solution(mesh):
    chips = Mesh(mesh.devices.reshape(-1, 2), ("chip", "core"))
    rows, copied = P(("chip", "core"), None), P()
    return jax.shard_map(
        on_device,
        mesh=chips,
        in_specs=(rows, rows) + (copied,) * 17,
        out_specs=(rows, rows) + (copied,) * 16,
        check_vma=False,
    )
```

time: 359 us -> 254 us (0.71)
  waiting for transfers between devices: 224 us -> 70.3 us
  starting transfers between devices: 11.5 us -> 94.2 us
  local copies, waits for them, and re-layouts: 34.8 us -> 11.4 us
  between operations: 14.2 us -> 1.24 us
    psum x1 -> x0, waiting for transfers between devices: 224 us -> none  [on_device(): lax.psum((inner_one, outer_one, inner_two, outer_two, tower_inner, pack),...]
    ppermute x0 -> x51, starting transfers between devices: none -> 82.7 us  [the longest x42 45.6 us: swap(): lax.ppermute(s, ('chip', 'core'), swaps(axes[step // 2], step))]
    ppermute x0 -> x51, waiting for transfers between devices: none -> 70.3 us  [the longest x42 67.9 us: swap(): lax.ppermute(s, ('chip', 'core'), swaps(axes[step // 2], step))]
    unnamed x33 -> x46, local copies, waits for them, and re-layouts: 24 us -> 8.25 us
    slice x3 -> x0, local copies, waits for them, and re-layouts: 4.02 us -> none  [the longest x1 1.38 us: on_device(): pack[112:128]]
    pallas_call x4 -> x20, Pallas kernels: 72.4 us -> 71.7 us  [the longest x1 35 us: main_part(): pl.pallas_call(functools.partial(main_kernel, rows), grid_spec=pltpu.Pref...]
  transfers between devices with their start and end apart: 2 -> 52, of which waited for: 1 -> 34; matrix products, arithmetic and copies ran while one was open for 2% -> 1% of each run, Pallas kernels for 10% -> 12%
where the time goes in v2:
time: 254 us; the launch traced here: 250 us
  starting transfers between devices  94.2 us (37%)
  Pallas kernels  71.7 us (28%)
  waiting for transfers between devices  70.3 us (28%)
  local copies, waits for them, and re-layouts  11.4 us (4%)
    ppermute x42, waiting for transfers between devices, swap(): lax.ppermute(s, ('chip', 'core'), swaps(axes[step // 2], step))  67.9 us
    ppermute x42, starting transfers between devices, swap(): lax.ppermute(s, ('chip', 'core'), swaps(axes[step // 2], step))  45.6 us
    ppermute x9, starting transfers between devices, cross(): return lax.ppermute(a, 'core', [(0, 1), (1, 0)])  37.1 us
    pallas_call x1, Pallas kernels, main_part(): pl.pallas_call(functools.partial(main_kernel, rows), grid_spec=pltpu.Pref...  35 us
    pallas_call x2, Pallas kernels, last_part(): pl.pallas_call(functools.partial(last_kernel, sending, rows), grid_spec=p...  14 us
    pallas_call x1, Pallas kernels, first_part(): pl.pallas_call(functools.partial(first_kernel, rows), grid=(WAVES,), in_s...  12.3 us
    all_to_all x1, starting transfers between devices, on_device(): counts = lax.all_to_all(sent, ('chip', 'core'), 0, 0, tiled=True)  11.5 us
    unnamed x46, local copies, waits for them, and re-layouts  8.25 us
  transfers between devices with their start and end apart: 52, of which 34 were waited for; matrix products, arithmetic and copies ran while one was open for 1% of the time, Pallas kernels for 12%

profile of v2, /device:TPU:1, one launch (start us, length us, event | category | flops | bytes accessed | tf_op | source)
XLA Modules:
  0.0 249.6 jit_solution(1803027411643564800)
XLA Ops:
  2.1 11.5 %all-to-all-start = ((f32[128,1,128]{2,1,0:T(1,128)}), f32[128,1,128]{2,1,0:T(1,128)S(1)}, u32[]{:S(2)}, u32[]{:S(2)}) async-start(f32[128,1,128]{2,1,0:T(1,128)} %broadcast_in_dim.2), calls=%async_computation | async-start | bytes 131072 | tf_op jit(solution)/shard_map/all_to_all | solution.py:981
  13.6 1.3 reshape.82.bias_ref
  15.0 12.3 %first_part.1 = (bf16[16,256,512]{2,1,0:T(8,128)(2,1)}, bf16[16,256,512]{2,1,0:T(8,128)(2,1)}, bf16[16,256,512]{2,1,0:T(8,128)(2,1)}, f32[16,1024]{1,0:T(8,128)}...) custom-call(bf16[512,256]{1,0:T(8,128)(2,1)} %tokens_ref.1, ...), custom_call_target="tpu_custom_call" | custom-call | flops 8000000000 | bytes 20000000 | tf_op jit(solution)/shard_map/first_part/pallas_call | solution.py:375
  28.5 35.0 %main_part.1 = (f32[8,1024,128]{2,1,0:T(8,128)}, f32[8,1024,128]{2,1,0:T(8,128)}, f32[4,4,256]{2,1,0:T(4,128)}, f32[56,256]{1,0:T(8,128)}, f32[256,1024]{1,0:T(8...) custom-call(s32[1]{0:T(128)} %bitcast.core_ref, bf16[256,1024]{1,0:T(8,128)(2,1)} %get-tuple-element.117.refs_0_, ...), custom_call_target="tpu_custom_call" | custom-call | flops 14000000000 | bytes 40000000 | tf_op jit(solution)/shard_map/main_part/pallas_call | solution.py:470
  64.7 1.6 copy-done.4
  66.3 2.2 copy-done.9
  69.7 6.2 %last_send.1 = (f32[8,1024,128]{2,1,0:T(8,128)}, f32[4,4,256]{2,1,0:T(4,128)S(1)}, f32[256,512]{1,0:T(8,128)S(1)}, f32[16,1024]{1,0:T(8,128)S(1)}) custom-call(s32[1]{0:T(128)} %bitcast.core_ref, bf16[256,512]{1,0:T(8,128)(2,1)S(1)} %copy-done.12, bf16[256,4096]{1,0:T(8,128)(2,1)S(1)} %copy-done.3, bf16[16,256,256]{2,1,0:T(8,128)(2,1)S(1)} %copy-done.4, ...), custom_call_target="tpu_custom_call" | custom-call | flops 8000000000 | bytes 20000000 | tf_op jit(solution)/shard_map/last_send/pallas_call | solution.py:629
  77.9 2.0 collective-permute-start.1
  79.9 2.5 %collective-permute-start.2 = (f32[1280,128]{1,0:T(8,128)S(1)}, f32[1280,128]{1,0:T(8,128)S(1)}, u32[]{:S(2)}, u32[]{:S(2)}) collective-permute-start(f32[1280,128]{1,0:T(8,128)S(1)} %get-tuple-element.138), channel_id=1, source_target_pairs={{0,32},{1,97},{2,34},{3,99},{4,36},{5,101},{6,38},{7,103},{8,40},{... | collective-permute-start | bytes 1966088 | tf_op jit(solution)/shard_map/ppermute | solution.py:670
  82.4 3.2 %collective-permute-start.3 = (f32[1536,128]{1,0:T(8,128)S(1)}, f32[1536,128]{1,0:T(8,128)S(1)}, u32[]{:S(2)}, u32[]{:S(2)}) collective-permute-start(f32[1536,128]{1,0:T(8,128)S(1)} %get-tuple-element.139), channel_id=1, source_target_pairs={{0,8},{1,25},{2,10},{3,27},{4,12},{5,29},{6,14},{7,31},{8,0},{9,17... | collective-permute-start | bytes 2359304 | tf_op jit(solution)/shard_map/ppermute | solution.py:670
  85.7 7.7 %last_keep.1 = (f32[8,1024,128]{2,1,0:T(8,128)S(1)}, f32[512,256]{1,0:T(8,128)}, f32[512,128]{1,0:T(8,128)S(1)}, f32[512,128]{1,0:T(8,128)S(1)}) custom-call(s32[1]{0:T(128)} %bitcast.core_ref, bf16[256,512]{1,0:T(8,128)(2,1)S(1)} %copy-done.12, bf16[256,4096]{1,0:T(8,128)(2,1)S(1)} %copy-done.3, bf16[16,256,256]{2,1,0:T(8,128)(2,1)S(1)} %copy-done.5, ...), custom_call_target="tpu_custom_call" | custom-call | flops 8000000000 | bytes 20000000 | tf_op jit(solution)/shard_map/last_keep/pallas_call | solution.py:629
  93.4 1.5 collective-permute-done.3.refs_2_
  96.0 2.7 %collective-permute-start.8 = (f32[1280,128]{1,0:T(8,128)S(1)}, f32[1280,128]{1,0:T(8,128)S(1)}, u32[]{:S(2)}, u32[]{:S(2)}) collective-permute-start(f32[1280,128]{1,0:T(8,128)S(1)} %get-tuple-element.148), channel_id=1, source_target_pairs={{0,8},{1,25},{2,10},{3,27},{4,12},{5,29},{6,14},{7,31},{8,0},{9,17... | collective-permute-start | bytes 1966088 | tf_op jit(solution)/shard_map/ppermute | solution.py:670
  99.1 11.1 %collective-permute-done.8.refs_2_ = f32[1280,128]{1,0:T(8,128)S(1)} collective-permute-done((f32[1280,128]{1,0:T(8,128)S(1)}, f32[1280,128]{1,0:T(8,128)S(1)}, u32[]{:S(2)}, u32[]{:S(2)}) %collective-permute-start.8) | collective-permute-done | bytes 655392 | tf_op jit(solution)/shard_map/ppermute | solution.py:670
  111.7 1.4 collective-permute-start.13
  113.1 9.0 %collective-permute-done.13.refs_4_ = f32[640,128]{1,0:T(8,128)S(1)} collective-permute-done((f32[640,128]{1,0:T(8,128)S(1)}, f32[640,128]{1,0:T(8,128)S(1)}, u32[]{:S(2)}, u32[]{:S(2)}) %collective-permute-start.13) | collective-permute-done | bytes 327712 | tf_op jit(solution)/shard_map/ppermute | solution.py:670
  122.4 1.7 collective-permute-start.15
  124.0 3.3 %collective-permute-start.16 = (f32[704,128]{1,0:T(8,128)S(1)}, f32[704,128]{1,0:T(8,128)S(1)}, u32[]{:S(2)}, u32[]{:S(2)}) collective-permute-start(f32[704,128]{1,0:T(8,128)S(1)} %get-tuple-element.163), channel_id=1, source_target_pairs={{0,8},{1,25},{2,10},{3,27},{4,12},{5,29},{6,14},{7,31},{8,0},{9,17... | collective-permute-start | bytes 1081352 | tf_op jit(solution)/shard_map/ppermute | solution.py:670
  127.3 2.5 collective-permute-start.17
  129.9 2.2 collective-permute-done.16.refs_1_
  132.1 2.7 %collective-permute-done.17.refs_2_ = f32[704,128]{1,0:T(8,128)S(1)} collective-permute-done((f32[704,128]{1,0:T(8,128)S(1)}, f32[704,128]{1,0:T(8,128)S(1)}, u32[]{:S(2)}, u32[]{:S(2)}) %collective-permute-start.17) | collective-permute-done | bytes 360480 | tf_op jit(solution)/shard_map/ppermute | solution.py:670
  135.9 3.6 %collective-permute-done.18.refs_0_ = f32[352,128]{1,0:T(8,128)S(1)} collective-permute-done((f32[352,128]{1,0:T(8,128)S(1)}, f32[352,128]{1,0:T(8,128)S(1)}, u32[]{:S(2)}, u32[]{:S(2)}) %collective-permute-start.18) | collective-permute-done | bytes 180256 | tf_op jit(solution)/shard_map/ppermute | solution.py:670
  139.8 2.8 %collective-permute-start.22 = (f32[176,128]{1,0:T(8,128)S(1)}, f32[176,128]{1,0:T(8,128)S(1)}, u32[]{:S(2)}, u32[]{:S(2)}) collective-permute-start(f32[176,128]{1,0:T(8,128)S(1)} %get-tuple-element.171), channel_id=1, source_target_pairs={{0,2},{1,7},{2,0},{3,5},{4,6},{5,3},{6,4},{7,1},{8,10},{9,15},{10,... | collective-permute-start | bytes 270344 | tf_op jit(solution)/shard_map/ppermute | solution.py:670
  142.8 2.0 collective-permute-done.21.refs_0_
  144.9 2.4 collective-permute-done.23.refs_2_
  147.3 1.7 collective-permute-start.24
  149.1 1.4 collective-permute-done.24.refs_0_
  150.5 1.5 collective-permute-done.25.refs_1_
  152.6 1.4 collective-permute-start.28
  155.4 1.4 collective-permute-done.29.refs_5_
  156.9 2.1 collective-permute-start.30
  159.5 2.0 collective-permute-done.30.refs_3_
  161.5 2.0 collective-permute-done.31.refs_4_
  164.7 3.7 %collective-permute-done.33.refs_3_ = f32[352,128]{1,0:T(8,128)S(1)} collective-permute-done((f32[352,128]{1,0:T(8,128)S(1)}, f32[352,128]{1,0:T(8,128)S(1)}, u32[]{:S(2)}, u32[]{:S(2)}) %collective-permute-start.33) | collective-permute-done | bytes 180256 | tf_op jit(solution)/shard_map/ppermute | solution.py:670
  169.6 1.4 collective-permute-start.37
  170.9 1.5 collective-permute-start.38
  172.5 4.2 %collective-permute-done.36.refs_3_ = f32[704,128]{1,0:T(8,128)S(1)} collective-permute-done((f32[704,128]{1,0:T(8,128)S(1)}, f32[704,128]{1,0:T(8,128)S(1)}, u32[]{:S(2)}, u32[]{:S(2)}) %collective-permute-start.36) | collective-permute-done | bytes 360480 | tf_op jit(solution)/shard_map/ppermute | solution.py:670
  177.1 1.4 collective-permute-done.38.refs_5_
  180.3 8.5 %collective-permute-done.39.refs_3_ = f32[1408,128]{1,0:T(8,128)S(1)} collective-permute-done((f32[1408,128]{1,0:T(8,128)S(1)}, f32[1408,128]{1,0:T(8,128)S(1)}, u32[]{:S(2)}, u32[]{:S(2)}) %collective-permute-start.39) | collective-permute-done | bytes 720928 | tf_op jit(solution)/shard_map/ppermute | solution.py:670
  189.9 4.3 %collective-permute-start.45 = (f32[2816,128]{1,0:T(8,128)S(1)}, f32[2816,128]{1,0:T(8,128)S(1)}, u32[]{:S(2)}, u32[]{:S(2)}) collective-permute-start(f32[2816,128]{1,0:T(8,128)S(1)} %get-tuple-element.192.refs_0_), channel_id=1, source_target_pairs={{0,2},{1,7},{2,0},{3,5},{4,6},{5,3},{6,4},{7,1},{8,10},{9,15},{10,... | collective-permute-start | bytes 4325384 | tf_op jit(solution)/shard_map/ppermute | solution.py:670
  194.2 21.5 %collective-permute-start.42 = (f32[2816,128]{1,0:T(8,128)S(1)}, f32[2816,128]{1,0:T(8,128)S(1)}, u32[]{:S(2)}, u32[]{:S(2)}) collective-permute-start(f32[2816,128]{1,0:T(8,128)S(1)} %get-tuple-element.192.refs_0_), channel_id=1, source_target_pairs={{0,1},{1,0},{2,3},{3,2},{4,5},{5,4},{6,7},{7,6},{8,9},{9,8},{10,11... | collective-permute-start | bytes 4325384 | tf_op jit(solution)/shard_map/ppermute | solution.py:971
  215.7 2.7 %collective-permute-start.47 = (f32[2816,128]{1,0:T(8,128)S(1)}, f32[2816,128]{1,0:T(8,128)S(1)}, u32[]{:S(2)}, u32[]{:S(2)}) collective-permute-start(f32[2816,128]{1,0:T(8,128)S(1)} %get-tuple-element.193.refs_1_), channel_id=1, source_target_pairs={{0,32},{1,97},{2,34},{3,99},{4,36},{5,101},{6,38},{7,103},{8,40},{... | collective-permute-start | bytes 4325384 | tf_op jit(solution)/shard_map/ppermute | solution.py:670
  218.4 2.2 collective-permute-start.49
  220.6 14.0 %collective-permute-start.44 = (f32[2816,128]{1,0:T(8,128)S(1)}, f32[2816,128]{1,0:T(8,128)S(1)}, u32[]{:S(2)}, u32[]{:S(2)}) collective-permute-start(f32[2816,128]{1,0:T(8,128)S(1)} %get-tuple-element.194.refs_2_), channel_id=1, source_target_pairs={{0,1},{1,0},{2,3},{3,2},{4,5},{5,4},{6,7},{7,6},{8,9},{9,8},{10,11... | collective-permute-start | bytes 4325384 | tf_op jit(solution)/shard_map/ppermute | solution.py:971
  235.1 2.3 collective-permute-done.49.refs_5_
  237.4 3.9 %lay_own.1 = (f32[256,4096]{1,0:T(8,128)}, f32[16,256,256]{2,1,0:T(8,128)}, f32[256,4096]{1,0:T(8,128)}, f32[16,256,256]{2,1,0:T(8,128)}, f32[512,128]{1,0:T(8,128)S(1)}) custom-call(s32[1]{0:T(128)} %bitcast.11.chip_ref, s32[1]{0:T(128)} %bitcast.core_ref, f32[2816,128]{1,0:T(8,128)S(1)} %get-tuple-element.192.refs_0_, ...), custom_call_target="tpu_custom_call" | custom-call | bytes 16000000 | tf_op jit(solution)/shard_map/lay_own/pallas_call | solution.py:925
  241.6 2.1 collective-permute-done.50.refs_5_
  243.7 4.0 %lay_other.1 = (f32[256,4096]{1,0:T(8,128)}, f32[16,256,256]{2,1,0:T(8,128)}, f32[256,4096]{1,0:T(8,128)}, f32[16,256,256]{2,1,0:T(8,128)}, f32[32,256]{1,0:T(8,...) custom-call(s32[1]{0:T(128)} %bitcast.11.chip_ref, ...), custom_call_target="tpu_custom_call", output_to_operand_aliasing={{0}: (9, {}), {1}: (10, {}), {2}: (11, {}), {3}: (12, {})} | custom-call | bytes 16000000 | tf_op jit(solution)/shard_map/lay_other/pallas_call | solution.py:925
  (128 shorter events, 22.9 us)
Async XLA Ops:
  2.1 25.8 %all-to-all-start = ((f32[128,1,128]{2,1,0:T(1,128)}), f32[128,1,128]{2,1,0:T(1,128)S(1)}, u32[]{:S(2)}, u32[]{:S(2)}) async-start(f32[128,1,128]{2,1,0:T(1,128)} %broadcast_in_dim.2), calls=%async_computation | async-start | bytes 131072 | tf_op jit(solution)/shard_map/all_to_all | solution.py:981
  63.6 12.4 %collective-permute-start = (f32[8,1024,128]{2,1,0:T(8,128)}, f32[8,1024,128]{2,1,0:T(8,128)S(1)}, u32[]{:S(2)}, u32[]{:S(2)}) collective-permute-start(f32[8,1024,128]{2,1,0:T(8,128)} %get-tuple-element.136), channel_id=1, source_target_pairs={{0,1},{1,0},{2,3},{3,2},{4,5},{5,4},{6,7},{7,6},{8,9},{9,8},{10,11... | collective-permute-start | bytes 12582920 | tf_op jit(solution)/shard_map/ppermute | solution.py:971
  76.0 19.0 %collective-permute-start.4 = (f32[8,1024,128]{2,1,0:T(8,128)}, f32[8,1024,128]{2,1,0:T(8,128)S(1)}, u32[]{:S(2)}, u32[]{:S(2)}) collective-permute-start(f32[8,1024,128]{2,1,0:T(8,128)} %get-tuple-element.142), channel_id=1, source_target_pairs={{0,1},{1,0},{2,3},{3,2},{4,5},{5,4},{6,7},{7,6},{8,9},{9,8},{10,11... | collective-permute-start | bytes 12582920 | tf_op jit(solution)/shard_map/ppermute | solution.py:971
  77.9 15.5 %collective-permute-start.1 = (f32[1280,128]{1,0:T(8,128)S(1)}, f32[1280,128]{1,0:T(8,128)S(1)}, u32[]{:S(2)}, u32[]{:S(2)}) collective-permute-start(f32[1280,128]{1,0:T(8,128)S(1)} %get-tuple-element.137), channel_id=1, source_target_pairs={{0,2},{1,7},{2,0},{3,5},{4,6},{5,3},{6,4},{7,1},{8,10},{9,15},{10,... | collective-permute-start | bytes 1966088 | tf_op jit(solution)/shard_map/ppermute | solution.py:670
  79.9 13.5 %collective-permute-start.2 = (f32[1280,128]{1,0:T(8,128)S(1)}, f32[1280,128]{1,0:T(8,128)S(1)}, u32[]{:S(2)}, u32[]{:S(2)}) collective-permute-start(f32[1280,128]{1,0:T(8,128)S(1)} %get-tuple-element.138), channel_id=1, source_target_pairs={{0,32},{1,97},{2,34},{3,99},{4,36},{5,101},{6,38},{7,103},{8,40},{... | collective-permute-start | bytes 1966088 | tf_op jit(solution)/shard_map/ppermute | solution.py:670
  82.4 12.6 %collective-permute-start.3 = (f32[1536,128]{1,0:T(8,128)S(1)}, f32[1536,128]{1,0:T(8,128)S(1)}, u32[]{:S(2)}, u32[]{:S(2)}) collective-permute-start(f32[1536,128]{1,0:T(8,128)S(1)} %get-tuple-element.139), channel_id=1, source_target_pairs={{0,8},{1,25},{2,10},{3,27},{4,12},{5,29},{6,14},{7,31},{8,0},{9,17... | collective-permute-start | bytes 2359304 | tf_op jit(solution)/shard_map/ppermute | solution.py:670
  95.6 15.6 %collective-permute-start.6 = (f32[1536,128]{1,0:T(8,128)S(1)}, f32[1536,128]{1,0:T(8,128)S(1)}, u32[]{:S(2)}, u32[]{:S(2)}) collective-permute-start(f32[1536,128]{1,0:T(8,128)S(1)} %get-tuple-element.146), channel_id=1, source_target_pairs={{0,2},{1,7},{2,0},{3,5},{4,6},{5,3},{6,4},{7,1},{8,10},{9,15},{10,... | collective-permute-start | bytes 2359304 | tf_op jit(solution)/shard_map/ppermute | solution.py:670
  95.9 15.3 %collective-permute-start.7 = (f32[1536,128]{1,0:T(8,128)S(1)}, f32[1536,128]{1,0:T(8,128)S(1)}, u32[]{:S(2)}, u32[]{:S(2)}) collective-permute-start(f32[1536,128]{1,0:T(8,128)S(1)} %get-tuple-element.147), channel_id=1, source_target_pairs={{0,32},{1,97},{2,34},{3,99},{4,36},{5,101},{6,38},{7,103},{8,40},{... | collective-permute-start | bytes 2359304 | tf_op jit(solution)/shard_map/ppermute | solution.py:670
  96.0 14.2 %collective-permute-start.8 = (f32[1280,128]{1,0:T(8,128)S(1)}, f32[1280,128]{1,0:T(8,128)S(1)}, u32[]{:S(2)}, u32[]{:S(2)}) collective-permute-start(f32[1280,128]{1,0:T(8,128)S(1)} %get-tuple-element.148), channel_id=1, source_target_pairs={{0,8},{1,25},{2,10},{3,27},{4,12},{5,29},{6,14},{7,31},{8,0},{9,17... | collective-permute-start | bytes 1966088 | tf_op jit(solution)/shard_map/ppermute | solution.py:670
  98.9 14.2 %collective-permute-start.12 = (f32[640,128]{1,0:T(8,128)S(1)}, f32[640,128]{1,0:T(8,128)S(1)}, u32[]{:S(2)}, u32[]{:S(2)}) collective-permute-start(f32[640,128]{1,0:T(8,128)S(1)} %get-tuple-element.158), channel_id=1, source_target_pairs={{0,6},{1,3},{2,4},{3,1},{4,2},{5,7},{6,0},{7,5},{8,14},{9,11},{10,... | collective-permute-start | bytes 983048 | tf_op jit(solution)/shard_map/ppermute | solution.py:670
  99.0 23.1 %collective-permute-start.14 = (f32[768,128]{1,0:T(8,128)S(1)}, f32[768,128]{1,0:T(8,128)S(1)}, u32[]{:S(2)}, u32[]{:S(2)}) collective-permute-start(f32[768,128]{1,0:T(8,128)S(1)} %get-tuple-element.160), channel_id=1, source_target_pairs={{0,24},{1,9},{2,26},{3,11},{4,28},{5,13},{6,30},{7,15},{8,16},{9,1... | collective-permute-start | bytes 1179656 | tf_op jit(solution)/shard_map/ppermute | solution.py:670
  111.5 10.6 %collective-permute-start.9 = (f32[768,128]{1,0:T(8,128)S(1)}, f32[768,128]{1,0:T(8,128)S(1)}, u32[]{:S(2)}, u32[]{:S(2)}) collective-permute-start(f32[768,128]{1,0:T(8,128)S(1)} %get-tuple-element.155), channel_id=1, source_target_pairs={{0,6},{1,3},{2,4},{3,1},{4,2},{5,7},{6,0},{7,5},{8,14},{9,11},{10,... | collective-permute-start | bytes 1179656 | tf_op jit(solution)/shard_map/ppermute | solution.py:670
  111.6 10.5 %collective-permute-start.10 = (f32[768,128]{1,0:T(8,128)S(1)}, f32[768,128]{1,0:T(8,128)S(1)}, u32[]{:S(2)}, u32[]{:S(2)}) collective-permute-start(f32[768,128]{1,0:T(8,128)S(1)} %get-tuple-element.156), channel_id=1, source_target_pairs={{0,96},{1,33},{2,98},{3,35},{4,100},{5,37},{6,102},{7,39},{8,104},... | collective-permute-start | bytes 1179656 | tf_op jit(solution)/shard_map/ppermute | solution.py:670
  111.7 10.4 %collective-permute-start.13 = (f32[640,128]{1,0:T(8,128)S(1)}, f32[640,128]{1,0:T(8,128)S(1)}, u32[]{:S(2)}, u32[]{:S(2)}) collective-permute-start(f32[640,128]{1,0:T(8,128)S(1)} %get-tuple-element.159), channel_id=1, source_target_pairs={{0,96},{1,33},{2,98},{3,35},{4,100},{5,37},{6,102},{7,39},{8,104},... | collective-permute-start | bytes 983048 | tf_op jit(solution)/shard_map/ppermute | solution.py:670
  113.1 9.0 %collective-permute-start.11 = (f32[640,128]{1,0:T(8,128)S(1)}, f32[640,128]{1,0:T(8,128)S(1)}, u32[]{:S(2)}, u32[]{:S(2)}) collective-permute-start(f32[640,128]{1,0:T(8,128)S(1)} %get-tuple-element.157), channel_id=1, source_target_pairs={{0,24},{1,9},{2,26},{3,11},{4,28},{5,13},{6,30},{7,15},{8,16},{9,1... | collective-permute-start | bytes 983048 | tf_op jit(solution)/shard_map/ppermute | solution.py:670
  122.4 7.6 %collective-permute-start.15 = (f32[704,128]{1,0:T(8,128)S(1)}, f32[704,128]{1,0:T(8,128)S(1)}, u32[]{:S(2)}, u32[]{:S(2)}) collective-permute-start(f32[704,128]{1,0:T(8,128)S(1)} %get-tuple-element.162), channel_id=1, source_target_pairs={{0,32},{1,97},{2,34},{3,99},{4,36},{5,101},{6,38},{7,103},{8,40},{... | collective-permute-start | bytes 1081352 | tf_op jit(solution)/shard_map/ppermute | solution.py:670
  124.0 8.1 %collective-permute-start.16 = (f32[704,128]{1,0:T(8,128)S(1)}, f32[704,128]{1,0:T(8,128)S(1)}, u32[]{:S(2)}, u32[]{:S(2)}) collective-permute-start(f32[704,128]{1,0:T(8,128)S(1)} %get-tuple-element.163), channel_id=1, source_target_pairs={{0,8},{1,25},{2,10},{3,27},{4,12},{5,29},{6,14},{7,31},{8,0},{9,17... | collective-permute-start | bytes 1081352 | tf_op jit(solution)/shard_map/ppermute | solution.py:670
  127.3 7.5 %collective-permute-start.17 = (f32[704,128]{1,0:T(8,128)S(1)}, f32[704,128]{1,0:T(8,128)S(1)}, u32[]{:S(2)}, u32[]{:S(2)}) collective-permute-start(f32[704,128]{1,0:T(8,128)S(1)} %get-tuple-element.164), channel_id=1, source_target_pairs={{0,2},{1,7},{2,0},{3,5},{4,6},{5,3},{6,4},{7,1},{8,10},{9,15},{10,... | collective-permute-start | bytes 1081352 | tf_op jit(solution)/shard_map/ppermute | solution.py:670
  134.9 4.6 %collective-permute-start.18 = (f32[352,128]{1,0:T(8,128)S(1)}, f32[352,128]{1,0:T(8,128)S(1)}, u32[]{:S(2)}, u32[]{:S(2)}) collective-permute-start(f32[352,128]{1,0:T(8,128)S(1)} %get-tuple-element.166), channel_id=1, source_target_pairs={{0,96},{1,33},{2,98},{3,35},{4,100},{5,37},{6,102},{7,39},{8,104},... | collective-permute-start | bytes 540680 | tf_op jit(solution)/shard_map/ppermute | solution.py:670
  135.2 4.4 %collective-permute-start.19 = (f32[352,128]{1,0:T(8,128)S(1)}, f32[352,128]{1,0:T(8,128)S(1)}, u32[]{:S(2)}, u32[]{:S(2)}) collective-permute-start(f32[352,128]{1,0:T(8,128)S(1)} %get-tuple-element.167), channel_id=1, source_target_pairs={{0,24},{1,9},{2,26},{3,11},{4,28},{5,13},{6,30},{7,15},{8,16},{9,1... | collective-permute-start | bytes 540680 | tf_op jit(solution)/shard_map/ppermute | solution.py:670
  135.3 4.4 %collective-permute-start.20 = (f32[352,128]{1,0:T(8,128)S(1)}, f32[352,128]{1,0:T(8,128)S(1)}, u32[]{:S(2)}, u32[]{:S(2)}) collective-permute-start(f32[352,128]{1,0:T(8,128)S(1)} %get-tuple-element.168), channel_id=1, source_target_pairs={{0,6},{1,3},{2,4},{3,1},{4,2},{5,7},{6,0},{7,5},{8,14},{9,11},{10,... | collective-permute-start | bytes 540680 | tf_op jit(solution)/shard_map/ppermute | solution.py:670
  139.8 5.0 %collective-permute-start.21 = (f32[176,128]{1,0:T(8,128)S(1)}, f32[176,128]{1,0:T(8,128)S(1)}, u32[]{:S(2)}, u32[]{:S(2)}) collective-permute-start(f32[176,128]{1,0:T(8,128)S(1)} %get-tuple-element.170), channel_id=1, source_target_pairs={{0,8},{1,25},{2,10},{3,27},{4,12},{5,29},{6,14},{7,31},{8,0},{9,17... | collective-permute-start | bytes 270344 | tf_op jit(solution)/shard_map/ppermute | solution.py:670
  139.8 5.1 %collective-permute-start.22 = (f32[176,128]{1,0:T(8,128)S(1)}, f32[176,128]{1,0:T(8,128)S(1)}, u32[]{:S(2)}, u32[]{:S(2)}) collective-permute-start(f32[176,128]{1,0:T(8,128)S(1)} %get-tuple-element.171), channel_id=1, source_target_pairs={{0,2},{1,7},{2,0},{3,5},{4,6},{5,3},{6,4},{7,1},{8,10},{9,15},{10,... | collective-permute-start | bytes 270344 | tf_op jit(solution)/shard_map/ppermute | solution.py:670
  142.7 4.6 %collective-permute-start.23 = (f32[176,128]{1,0:T(8,128)S(1)}, f32[176,128]{1,0:T(8,128)S(1)}, u32[]{:S(2)}, u32[]{:S(2)}) collective-permute-start(f32[176,128]{1,0:T(8,128)S(1)} %get-tuple-element.172), channel_id=1, source_target_pairs={{0,32},{1,97},{2,34},{3,99},{4,36},{5,101},{6,38},{7,103},{8,40},{... | collective-permute-start | bytes 270344 | tf_op jit(solution)/shard_map/ppermute | solution.py:670
  147.3 3.2 %collective-permute-start.24 = (f32[88,128]{1,0:T(8,128)S(1)}, f32[88,128]{1,0:T(8,128)S(1)}, u32[]{:S(2)}, u32[]{:S(2)}) collective-permute-start(f32[88,128]{1,0:T(8,128)S(1)} %get-tuple-element.174), channel_id=1, source_target_pairs={{0,24},{1,9},{2,26},{3,11},{4,28},{5,13},{6,30},{7,15},{8,16},{9,1... | collective-permute-start | bytes 135176 | tf_op jit(solution)/shard_map/ppermute | solution.py:670
  149.1 2.9 %collective-permute-start.25 = (f32[88,128]{1,0:T(8,128)S(1)}, f32[88,128]{1,0:T(8,128)S(1)}, u32[]{:S(2)}, u32[]{:S(2)}) collective-permute-start(f32[88,128]{1,0:T(8,128)S(1)} %get-tuple-element.175), channel_id=1, source_target_pairs={{0,6},{1,3},{2,4},{3,1},{4,2},{5,7},{6,0},{7,5},{8,14},{9,11},{10,... | collective-permute-start | bytes 135176 | tf_op jit(solution)/shard_map/ppermute | solution.py:670
  152.0 3.0 %collective-permute-start.27 = (f32[88,128]{1,0:T(8,128)S(1)}, f32[88,128]{1,0:T(8,128)S(1)}, u32[]{:S(2)}, u32[]{:S(2)}) collective-permute-start(f32[88,128]{1,0:T(8,128)S(1)} %get-tuple-element.177.refs_0_), channel_id=1, source_target_pairs={{0,24},{1,9},{2,26},{3,11},{4,28},{5,13},{6,30},{7,15},{8,16},{9,1... | collective-permute-start | bytes 135176 | tf_op jit(solution)/shard_map/ppermute | solution.py:670
  156.9 4.7 %collective-permute-start.30 = (f32[176,128]{1,0:T(8,128)S(1)}, f32[176,128]{1,0:T(8,128)S(1)}, u32[]{:S(2)}, u32[]{:S(2)}) collective-permute-start(f32[176,128]{1,0:T(8,128)S(1)} %get-tuple-element.180.refs_0_), channel_id=1, source_target_pairs={{0,8},{1,25},{2,10},{3,27},{4,12},{5,29},{6,14},{7,31},{8,0},{9,17... | collective-permute-start | bytes 270344 | tf_op jit(solution)/shard_map/ppermute | solution.py:670
  158.9 4.6 %collective-permute-start.31 = (f32[176,128]{1,0:T(8,128)S(1)}, f32[176,128]{1,0:T(8,128)S(1)}, u32[]{:S(2)}, u32[]{:S(2)}) collective-permute-start(f32[176,128]{1,0:T(8,128)S(1)} %get-tuple-element.181.refs_1_), channel_id=1, source_target_pairs={{0,2},{1,7},{2,0},{3,5},{4,6},{5,3},{6,4},{7,1},{8,10},{9,15},{10,... | collective-permute-start | bytes 270344 | tf_op jit(solution)/shard_map/ppermute | solution.py:670
  159.0 4.6 %collective-permute-start.32 = (f32[176,128]{1,0:T(8,128)S(1)}, f32[176,128]{1,0:T(8,128)S(1)}, u32[]{:S(2)}, u32[]{:S(2)}) collective-permute-start(f32[176,128]{1,0:T(8,128)S(1)} %get-tuple-element.182.refs_2_), channel_id=1, source_target_pairs={{0,32},{1,97},{2,34},{3,99},{4,36},{5,101},{6,38},{7,103},{8,40},{... | collective-permute-start | bytes 270344 | tf_op jit(solution)/shard_map/ppermute | solution.py:670
  163.7 4.7 %collective-permute-start.33 = (f32[352,128]{1,0:T(8,128)S(1)}, f32[352,128]{1,0:T(8,128)S(1)}, u32[]{:S(2)}, u32[]{:S(2)}) collective-permute-start(f32[352,128]{1,0:T(8,128)S(1)} %get-tuple-element.183.refs_0_), channel_id=1, source_target_pairs={{0,96},{1,33},{2,98},{3,35},{4,100},{5,37},{6,102},{7,39},{8,104},... | collective-permute-start | bytes 540680 | tf_op jit(solution)/shard_map/ppermute | solution.py:670
  164.3 4.4 %collective-permute-start.34 = (f32[352,128]{1,0:T(8,128)S(1)}, f32[352,128]{1,0:T(8,128)S(1)}, u32[]{:S(2)}, u32[]{:S(2)}) collective-permute-start(f32[352,128]{1,0:T(8,128)S(1)} %get-tuple-element.184.refs_1_), channel_id=1, source_target_pairs={{0,24},{1,9},{2,26},{3,11},{4,28},{5,13},{6,30},{7,15},{8,16},{9,1... | collective-permute-start | bytes 540680 | tf_op jit(solution)/shard_map/ppermute | solution.py:670
  164.7 4.3 %collective-permute-start.35 = (f32[352,128]{1,0:T(8,128)S(1)}, f32[352,128]{1,0:T(8,128)S(1)}, u32[]{:S(2)}, u32[]{:S(2)}) collective-permute-start(f32[352,128]{1,0:T(8,128)S(1)} %get-tuple-element.185.refs_2_), channel_id=1, source_target_pairs={{0,6},{1,3},{2,4},{3,1},{4,2},{5,7},{6,0},{7,5},{8,14},{9,11},{10,... | collective-permute-start | bytes 540680 | tf_op jit(solution)/shard_map/ppermute | solution.py:670
  169.1 7.6 %collective-permute-start.36 = (f32[704,128]{1,0:T(8,128)S(1)}, f32[704,128]{1,0:T(8,128)S(1)}, u32[]{:S(2)}, u32[]{:S(2)}) collective-permute-start(f32[704,128]{1,0:T(8,128)S(1)} %get-tuple-element.186.refs_0_), channel_id=1, source_target_pairs={{0,32},{1,97},{2,34},{3,99},{4,36},{5,101},{6,38},{7,103},{8,40},{... | collective-permute-start | bytes 1081352 | tf_op jit(solution)/shard_map/ppermute | solution.py:670
  169.6 7.5 %collective-permute-start.37 = (f32[704,128]{1,0:T(8,128)S(1)}, f32[704,128]{1,0:T(8,128)S(1)}, u32[]{:S(2)}, u32[]{:S(2)}) collective-permute-start(f32[704,128]{1,0:T(8,128)S(1)} %get-tuple-element.187.refs_1_), channel_id=1, source_target_pairs={{0,8},{1,25},{2,10},{3,27},{4,12},{5,29},{6,14},{7,31},{8,0},{9,17... | collective-permute-start | bytes 1081352 | tf_op jit(solution)/shard_map/ppermute | solution.py:670
  170.9 7.5 %collective-permute-start.38 = (f32[704,128]{1,0:T(8,128)S(1)}, f32[704,128]{1,0:T(8,128)S(1)}, u32[]{:S(2)}, u32[]{:S(2)}) collective-permute-start(f32[704,128]{1,0:T(8,128)S(1)} %get-tuple-element.188.refs_2_), channel_id=1, source_target_pairs={{0,2},{1,7},{2,0},{3,5},{4,6},{5,3},{6,4},{7,1},{8,10},{9,15},{10,... | collective-permute-start | bytes 1081352 | tf_op jit(solution)/shard_map/ppermute | solution.py:670
  178.6 10.2 %collective-permute-start.39 = (f32[1408,128]{1,0:T(8,128)S(1)}, f32[1408,128]{1,0:T(8,128)S(1)}, u32[]{:S(2)}, u32[]{:S(2)}) collective-permute-start(f32[1408,128]{1,0:T(8,128)S(1)} %get-tuple-element.189.refs_0_), channel_id=1, source_target_pairs={{0,6},{1,3},{2,4},{3,1},{4,2},{5,7},{6,0},{7,5},{8,14},{9,11},{10,... | collective-permute-start | bytes 2162696 | tf_op jit(solution)/shard_map/ppermute | solution.py:670
  178.7 10.2 %collective-permute-start.40 = (f32[1408,128]{1,0:T(8,128)S(1)}, f32[1408,128]{1,0:T(8,128)S(1)}, u32[]{:S(2)}, u32[]{:S(2)}) collective-permute-start(f32[1408,128]{1,0:T(8,128)S(1)} %get-tuple-element.190.refs_1_), channel_id=1, source_target_pairs={{0,96},{1,33},{2,98},{3,35},{4,100},{5,37},{6,102},{7,39},{8,104},... | collective-permute-start | bytes 2162696 | tf_op jit(solution)/shard_map/ppermute | solution.py:670
  179.4 10.1 %collective-permute-start.41 = (f32[1408,128]{1,0:T(8,128)S(1)}, f32[1408,128]{1,0:T(8,128)S(1)}, u32[]{:S(2)}, u32[]{:S(2)}) collective-permute-start(f32[1408,128]{1,0:T(8,128)S(1)} %get-tuple-element.191.refs_2_), channel_id=1, source_target_pairs={{0,24},{1,9},{2,26},{3,11},{4,28},{5,13},{6,30},{7,15},{8,16},{9,1... | collective-permute-start | bytes 2162696 | tf_op jit(solution)/shard_map/ppermute | solution.py:670
  189.9 30.7 %collective-permute-start.45 = (f32[2816,128]{1,0:T(8,128)S(1)}, f32[2816,128]{1,0:T(8,128)S(1)}, u32[]{:S(2)}, u32[]{:S(2)}) collective-permute-start(f32[2816,128]{1,0:T(8,128)S(1)} %get-tuple-element.192.refs_0_), channel_id=1, source_target_pairs={{0,2},{1,7},{2,0},{3,5},{4,6},{5,3},{6,4},{7,1},{8,10},{9,15},{10,... | collective-permute-start | bytes 4325384 | tf_op jit(solution)/shard_map/ppermute | solution.py:670
  194.2 40.5 %collective-permute-start.42 = (f32[2816,128]{1,0:T(8,128)S(1)}, f32[2816,128]{1,0:T(8,128)S(1)}, u32[]{:S(2)}, u32[]{:S(2)}) collective-permute-start(f32[2816,128]{1,0:T(8,128)S(1)} %get-tuple-element.192.refs_0_), channel_id=1, source_target_pairs={{0,1},{1,0},{2,3},{3,2},{4,5},{5,4},{6,7},{7,6},{8,9},{9,8},{10,11... | collective-permute-start | bytes 4325384 | tf_op jit(solution)/shard_map/ppermute | solution.py:971
  215.7 19.1 %collective-permute-start.47 = (f32[2816,128]{1,0:T(8,128)S(1)}, f32[2816,128]{1,0:T(8,128)S(1)}, u32[]{:S(2)}, u32[]{:S(2)}) collective-permute-start(f32[2816,128]{1,0:T(8,128)S(1)} %get-tuple-element.193.refs_1_), channel_id=1, source_target_pairs={{0,32},{1,97},{2,34},{3,99},{4,36},{5,101},{6,38},{7,103},{8,40},{... | collective-permute-start | bytes 4325384 | tf_op jit(solution)/shard_map/ppermute | solution.py:670
  218.4 19.1 %collective-permute-start.49 = (f32[2816,128]{1,0:T(8,128)S(1)}, f32[2816,128]{1,0:T(8,128)S(1)}, u32[]{:S(2)}, u32[]{:S(2)}) collective-permute-start(f32[2816,128]{1,0:T(8,128)S(1)} %get-tuple-element.194.refs_2_), channel_id=1, source_target_pairs={{0,8},{1,25},{2,10},{3,27},{4,12},{5,29},{6,14},{7,31},{8,0},{9,17... | collective-permute-start | bytes 4325384 | tf_op jit(solution)/shard_map/ppermute | solution.py:670
  220.6 20.7 %collective-permute-start.43 = (f32[2816,128]{1,0:T(8,128)S(1)}, f32[2816,128]{1,0:T(8,128)S(1)}, u32[]{:S(2)}, u32[]{:S(2)}) collective-permute-start(f32[2816,128]{1,0:T(8,128)S(1)} %get-tuple-element.193.refs_1_), channel_id=1, source_target_pairs={{0,1},{1,0},{2,3},{3,2},{4,5},{5,4},{6,7},{7,6},{8,9},{9,8},{10,11... | collective-permute-start | bytes 4325384 | tf_op jit(solution)/shard_map/ppermute | solution.py:971
  220.6 20.7 %collective-permute-start.44 = (f32[2816,128]{1,0:T(8,128)S(1)}, f32[2816,128]{1,0:T(8,128)S(1)}, u32[]{:S(2)}, u32[]{:S(2)}) collective-permute-start(f32[2816,128]{1,0:T(8,128)S(1)} %get-tuple-element.194.refs_2_), channel_id=1, source_target_pairs={{0,1},{1,0},{2,3},{3,2},{4,5},{5,4},{6,7},{7,6},{8,9},{9,8},{10,11... | collective-permute-start | bytes 4325384 | tf_op jit(solution)/shard_map/ppermute | solution.py:971
  234.6 6.7 %collective-permute-start.46 = (f32[2816,128]{1,0:T(8,128)S(1)}, f32[2816,128]{1,0:T(8,128)S(1)}, u32[]{:S(2)}, u32[]{:S(2)}) collective-permute-start(f32[2816,128]{1,0:T(8,128)S(1)} %collective-permute-done.45.refs_3_), channel_id=1, source_target_pairs={{0,1},{1,0},{2,3},{3,2},{4,5},{5,4},{6,7},{7,6},{8,9},{9,8},{10,11... | collective-permute-start | bytes 4325384 | tf_op jit(solution)/shard_map/ppermute | solution.py:971
  234.8 6.8 %collective-permute-start.48 = (f32[2816,128]{1,0:T(8,128)S(1)}, f32[2816,128]{1,0:T(8,128)S(1)}, u32[]{:S(2)}, u32[]{:S(2)}) collective-permute-start(f32[2816,128]{1,0:T(8,128)S(1)} %collective-permute-done.47.refs_4_), channel_id=1, source_target_pairs={{0,1},{1,0},{2,3},{3,2},{4,5},{5,4},{6,7},{7,6},{8,9},{9,8},{10,11... | collective-permute-start | bytes 4325384 | tf_op jit(solution)/shard_map/ppermute | solution.py:971
  237.4 6.2 %collective-permute-start.50 = (f32[2816,128]{1,0:T(8,128)S(1)}, f32[2816,128]{1,0:T(8,128)S(1)}, u32[]{:S(2)}, u32[]{:S(2)}) collective-permute-start(f32[2816,128]{1,0:T(8,128)S(1)} %collective-permute-done.49.refs_5_), channel_id=1, source_target_pairs={{0,1},{1,0},{2,3},{3,2},{4,5},{5,4},{6,7},{7,6},{8,9},{9,8},{10,11... | collective-permute-start | bytes 4325384 | tf_op jit(solution)/shard_map/ppermute | solution.py:971
  (26 other events, 253.3 us)

commit v3 on v2

--- a/solution.py
+++ b/solution.py
@@ -20,7 +20,9 @@
 GROUP = 4
 WAVES = EXPERTS // GROUP
 SLAB = 1024
-SMALL = 1024
+SMALL = 672
+SHARE = SMALL // 2
+OWN = 144
 HALF_ROWS = 8 * SLAB
 ONE = (48, 48, 40)
 TWO = (40, 40, 48)
@@ -30,7 +32,7 @@
 BF16 = jnp.bfloat16
 ROOT = 0.7978845608028654
 CUBE = 0.044715
-BYTES = 61 * 1024 * 1024
+MIB = 1024 * 1024
 
 
 def nn(a, b):
@@ -211,7 +213,7 @@
 
 
 def forward_wave(shared, rows, wave, u_ref, inner_ref, bias_ref, outer_ref, state, gate_ref, acc_ref, work):
-    bias = bias_ref[0].astype(F32).T
+    bias = bias_ref[...].astype(F32).T
     lanes = rows if shared else rows * TASKS
     tiles = lanes // 256
     part = WIDTH // tiles
@@ -229,7 +231,9 @@
         hid_ref, slope_ref, _ = state(p)
         for at in range(q * part, (q + 1) * part, tall):
             here = slice(at, at + tall)
-            hid, slope = gelu_both(pre_refs[p % 2][here, :lanes] + bias[here, p : p + 1])
+            half, top = at // 128, at % 128
+            column = bias[top : top + tall, 2 * p + half : 2 * p + half + 1]
+            hid, slope = gelu_both(pre_refs[p % 2][here, :lanes] + column)
             hid_ref[here, :] = hid.astype(BF16)
             slope_ref[here, :] = slope.astype(BF16)
 
@@ -380,7 +384,7 @@
             whole(codes.shape),
             whole(mixing.shape),
             pl.BlockSpec((WIDTH, GROUP * HID), lambda i: (0, i)),
-            pl.BlockSpec((1, GROUP, HID), lambda i: (i, 0, 0)),
+            pl.BlockSpec((2 * GROUP, 128), lambda i: (i, 0)),
             pl.BlockSpec((GROUP, HID, WIDTH), lambda i: (i, 0, 0)),
             whole(outer_bias.shape),
         ],
@@ -389,17 +393,18 @@
         scratch_shapes=[pltpu.VMEM((WIDTH, wide), F32)] + [pltpu.VMEM((HID, rows), F32)] * 4,
         cost_estimate=pl.CostEstimate(flops=8_000_000_000, bytes_accessed=20_000_000, transcendentals=0),
         compiler_params=pltpu.CompilerParams(
-            dimension_semantics=("arbitrary",), vmem_limit_bytes=BYTES
+            dimension_semantics=("arbitrary",), vmem_limit_bytes=61 * MIB
         ),
         name="first_part",
-    )(tokens, codes, mixing, inner, inner_bias.reshape(WAVES, GROUP, HID), outer, outer_bias)
+    )(tokens, codes, mixing, inner, inner_bias.reshape(2 * EXPERTS, 128), outer, outer_bias)
 
 
 def main_kernel(rows, core_ref, *refs):
     (u_ref, codes_two, mixing_two, inner_two, bias_two, outer_two, outer_bias_two), refs = refs[:7], refs[7:]
     tower_in, refs = refs[:8], refs[8:]
-    (send_ref, keep_ref, grad_bias, rest_ref, dy_one), refs = refs[:5], refs[5:]
-    tower_out, refs = refs[:3], refs[3:]
+    (send_ref, keep_ref, dy_one, predictions, small_send, small_keep), refs = refs[:6], refs[6:]
+    (grad_bias, rest_ref, little, tower_inner, small_ref), refs = refs[:5], refs[5:]
+    tower_out = (predictions, little, tower_inner)
     (hid_two, slope_two, out_two, gate_two, code_two, mix_two, aug, v_ref), refs = refs[:8], refs[8:]
     (acc_ref, dy_two, dgate_ref, dcode_ref, dmix_ref, dout_ref, dpre_ref), work = refs[:7], refs[7:]
     step = pl.program_id(0)
@@ -424,7 +429,7 @@
 
     def back(slab_ref):
         wave = (step + 2 * (1 - core_ref[0])) % WAVES
-        backward_wave(False, rows, wave, aug, inner_two, outer_two, state_two(wave), gate_two, dy_two, acc_ref, dgate_ref, slab_ref, grad_bias, dout_ref, dpre_ref, work)
+        backward_wave(False, rows, wave, aug, inner_two, outer_two, state_two(wave), gate_two, dy_two, acc_ref, dgate_ref, slab_ref, grad_bias.at[pl.ds(wave, 1)], dout_ref, dpre_ref, work)
 
     @pl.when((step >= WAVES) & (step < WAVES + 2))
     def _():
@@ -437,6 +442,18 @@
     @pl.when(step == 2 * WAVES - 1)
     def _():
         dy_one[...] = finish(False, rows, u_ref[...], codes_two, mixing_two, outer_bias_two, code_two, mix_two, gate_two, dy_two, dgate_ref, acc_ref, dcode_ref, dmix_ref, rest_ref)
+        small_ref[0:256, :] = tower_inner[0]
+        small_ref[256:512, :] = tower_inner[1]
+        small_ref[512:568, :] = rest_ref[:, :128]
+        small_ref[568:624, :] = rest_ref[:, 128:]
+        for w in range(WAVES):
+            small_ref[624 + GROUP * w : 624 + GROUP * (w + 1), :] = grad_bias[w, :, :128]
+            small_ref[640 + GROUP * w : 640 + GROUP * (w + 1), :] = grad_bias[w, :, 128:]
+        small_ref[656:664, :] = little[...]
+        small_ref[664:, :] = jnp.zeros((8, 128), F32)
+        core = core_ref[0]
+        small_send[...] = small_ref[pl.ds(pl.multiple_of((1 - core) * SHARE, 8), SHARE), :]
+        small_keep[...] = small_ref[pl.ds(pl.multiple_of(core * SHARE, 8), SHARE), :]
 
 
 def fixed(shape):
@@ -450,20 +467,16 @@
     def order(i, core):
         return jnp.where(i < WAVES, i, (i + 2 * (1 - core[0])) % WAVES)
 
-    def back(i, core):
-        return (jnp.maximum(i, WAVES) + 2 * (1 - core[0])) % WAVES
-
     slab = jax.ShapeDtypeStruct((EXPERTS // 2, SLAB, 128), F32)
 
     def slab_spec(begin):
         return pl.BlockSpec((GROUP, SLAB, 128), lambda i, core: (jnp.clip(i - begin, 0, 1), 0, 0))
 
     rest = [
-        jax.ShapeDtypeStruct((56, WIDTH), F32),
         jax.ShapeDtypeStruct((WIDTH, wide), F32),
         jax.ShapeDtypeStruct((TASKS, rows), F32),
-        jax.ShapeDtypeStruct((8, TOWER), F32),
-        jax.ShapeDtypeStruct((TASKS, WIDTH, TOWER), F32),
+        jax.ShapeDtypeStruct((SHARE, 128), F32),
+        jax.ShapeDtypeStruct((SHARE, 128), F32),
     ]
     tower_specs = [fixed(a.shape) for a in tower_in]
     tower_specs[3] = pl.BlockSpec(memory_space=pltpu.SMEM)
@@ -477,15 +490,19 @@
                 fixed(codes.shape),
                 fixed(mixing.shape),
                 pl.BlockSpec((WIDTH, GROUP * HID), lambda i, core: (0, order(i, core))),
-                pl.BlockSpec((1, GROUP, HID), lambda i, core: (order(i, core), 0, 0)),
+                pl.BlockSpec((2 * GROUP, 128), lambda i, core: (order(i, core), 0)),
                 pl.BlockSpec((GROUP, HID, WIDTH), lambda i, core: (order(i, core), 0, 0)),
                 fixed(outer_bias.shape),
             ]
             + tower_specs,
             out_specs=[slab_spec(WAVES), slab_spec(WAVES + 2)]
-            + [pl.BlockSpec((1, GROUP, HID), lambda i, core: (back(i, core), 0, 0))]
             + [fixed(s.shape) for s in rest],
             scratch_shapes=[
+                pltpu.VMEM((WAVES, GROUP, HID), F32),
+                pltpu.VMEM((56, WIDTH), F32),
+                pltpu.VMEM((8, TOWER), F32),
+                pltpu.VMEM((TASKS, WIDTH, TOWER), F32),
+                pltpu.VMEM((SMALL, 128), F32),
                 *[pltpu.VMEM((EXPERTS, HID, wide), BF16)] * 3,
                 pltpu.VMEM((EXPERTS, wide), F32),
                 pltpu.VMEM((32, wide), F32),
@@ -502,10 +519,10 @@
                 *[pltpu.VMEM((HID, wide), F32)] * 4,
             ],
         ),
-        out_shape=[slab, slab, jax.ShapeDtypeStruct((WAVES, GROUP, HID), F32)] + rest,
+        out_shape=[slab, slab] + rest,
         cost_estimate=pl.CostEstimate(flops=14_000_000_000, bytes_accessed=40_000_000, transcendentals=0),
         compiler_params=pltpu.CompilerParams(
-            dimension_semantics=("arbitrary",), vmem_limit_bytes=BYTES
+            dimension_semantics=("arbitrary",), vmem_limit_bytes=61 * MIB
         ),
         name="main_part",
     )(
@@ -514,7 +531,7 @@
         codes,
         mixing,
         inner,
-        inner_bias.reshape(WAVES, GROUP, HID),
+        inner_bias.reshape(2 * EXPERTS, 128),
         outer,
         outer_bias,
         *tower_in,
@@ -531,9 +548,8 @@
         bias_at = bias_ref
     else:
         (acc_in, dgate_in, codes_ref, mixing_ref, outer_bias_ref, code_ref, mix_ref), refs = refs[:7], refs[7:]
-        (other_bias, bias_two, rest_two, little, tower_inner), refs = refs[:5], refs[5:]
-        (slab_ref, back_ref, small_send, small_keep), refs = refs[:4], refs[4:]
-        aug, dout_ref, dpre_ref, acc_ref, dgate_ref, dcode_ref, dmix_ref, bias_ref, rest_ref, small_ref, *work = refs
+        (other_bias, slab_ref, back_ref, small_ref), refs = refs[:4], refs[4:]
+        aug, dout_ref, dpre_ref, acc_ref, dgate_ref, dcode_ref, dmix_ref, bias_ref, rest_ref, *work = refs
         wave = step + 2 * core_ref[0]
         bias_at = bias_ref.at[pl.ds(step, 1)]
 
@@ -559,22 +575,12 @@
         du = finish(True, rows, u_ref[...], codes_ref, mixing_ref, outer_bias_ref, code_ref, mix_ref, gate_ref, dy_ref, dgate_ref, acc_ref, dcode_ref, dmix_ref, rest_ref)
         back_ref[...] = du.T
         core = core_ref[0]
-        small_ref[0:256, :] = tower_inner[0]
-        small_ref[256:512, :] = tower_inner[1]
-        small_ref[808:, :] = jnp.zeros((SMALL - 808, 128), F32)
-        for at, ref in ((512, rest_ref), (624, rest_two)):
-            small_ref[at : at + 56, :] = ref[:, :128]
-            small_ref[at + 56 : at + 112, :] = ref[:, 128:]
+        small_ref[0:56, :] = rest_ref[:, :128]
+        small_ref[56:112, :] = rest_ref[:, 128:]
         for w in range(WAVES):
-            mine, j = core == w // 2, w % 2
-            rows_one = jnp.where(mine, bias_ref[j], other_bias[w])
-            for at, found in ((736, rows_one), (768, bias_two[w])):
-                at += GROUP * w
-                small_ref[at : at + GROUP, :] = found[:, :128]
-                small_ref[at + 16 : at + 16 + GROUP, :] = found[:, 128:]
-        small_ref[800:808, :] = little[...]
-        small_send[...] = small_ref[pl.ds((1 - core) * 512, 512), :]
-        small_keep[...] = small_ref[pl.ds(core * 512, 512), :]
+            found = jnp.where(core == w // 2, bias_ref[w % 2], other_bias[w])
+            small_ref[112 + GROUP * w : 112 + GROUP * (w + 1), :] = found[:, :128]
+            small_ref[128 + GROUP * w : 128 + GROUP * (w + 1), :] = found[:, 128:]
 
 
 def last_part(sending, core, u, inner, outer, state, gate, dy, more):
@@ -611,8 +617,7 @@
     else:
         added = [
             jax.ShapeDtypeStruct((rows, WIDTH), F32),
-            jax.ShapeDtypeStruct((SMALL // 2, 128), F32),
-            jax.ShapeDtypeStruct((SMALL // 2, 128), F32),
+            jax.ShapeDtypeStruct((OWN, 128), F32),
         ]
         scratch += [
             pltpu.VMEM((WIDTH, rows), F32),
@@ -621,7 +626,6 @@
             pltpu.VMEM((8, rows), F32),
             pltpu.VMEM((2, GROUP, HID), F32),
             pltpu.VMEM((56, WIDTH), F32),
-            pltpu.VMEM((SMALL, 128), F32),
         ]
     scratch += [pltpu.VMEM((HID, rows), F32)] * 2
     out_shape += added
@@ -638,7 +642,7 @@
         out_shape=out_shape,
         cost_estimate=pl.CostEstimate(flops=8_000_000_000, bytes_accessed=20_000_000, transcendentals=0),
         compiler_params=pltpu.CompilerParams(
-            dimension_semantics=("arbitrary",), vmem_limit_bytes=40 * 1024 * 1024
+            dimension_semantics=("arbitrary",), vmem_limit_bytes=40 * MIB
         ),
         name="last_send" if sending else "last_keep",
     )(core, *arrays)
@@ -647,11 +651,12 @@
 def place(chip, core):
     found = []
     for axes in AXES:
-        halves = []
+        early, late = [], []
         for shift in axes:
             low, high = (chip >> shift) & 1, (chip >> (shift + 1)) & 1
-            halves += [jnp.where(core == 0, low ^ high, high), jnp.where(core == 0, high, low)]
-        found.append(halves)
+            early.append(jnp.where(core == 0, low ^ high, high))
+            late.append(jnp.where(core == 0, high, low))
+        found.append(early + late)
     return found
 
 
@@ -660,14 +665,14 @@
     for chip in range(64):
         c = (chip >> shift) & 3
         for core in range(2):
-            n = c ^ 1 if (core + step) % 2 == 0 else 3 - c
+            n = c ^ 1 if (core + step // 3) % 2 == 0 else 3 - c
             pairs.append((chip * 2 + core, (chip + ((n - c) << shift)) * 2 + core))
     return pairs
 
 
 def swap(step, sent):
     return [
-        lax.ppermute(s, ("chip", "core"), swaps(axes[step // 2], step))
+        lax.ppermute(s, ("chip", "core"), swaps(axes[step % 3], step))
         for s, axes in zip(sent, AXES)
     ]
 
@@ -682,7 +687,7 @@
         out_shape=[jax.ShapeDtypeStruct((n, 128), F32) for n in sizes],
         scratch_shapes=scratch,
         cost_estimate=pl.CostEstimate(flops=0, bytes_accessed=2_000_000, transcendentals=0),
-        compiler_params=pltpu.CompilerParams(vmem_limit_bytes=28 * 1024 * 1024),
+        compiler_params=pltpu.CompilerParams(vmem_limit_bytes=28 * MIB),
         name=name,
     )(chip, core, *arrays)
 
@@ -693,12 +698,14 @@
 
 def open_kernel(counts, with_small, chip_ref, core_ref, keep_ref, got_ref, *refs):
     if with_small:
-        (small_keep, small_got), refs = refs[:2], refs[2:]
+        (small_keep, small_got, small_own), refs = refs[:3], refs[3:]
         tail_ref = refs[-1]
         tail_ref[:2048, :] = keep_ref[6144:, :] + got_ref[6144:, :]
-        tail_ref[2048:, :] = small_keep[...] + small_got[...]
+        tail_ref[2048 : 2048 + SHARE, :] = small_keep[...] + small_got[...]
+        tail_ref[2048 + SHARE : 2048 + SHARE + OWN, :] = small_own[...]
+        tail_ref[2048 + SHARE + OWN :, :] = jnp.zeros((512 - SHARE - OWN, 128), F32)
     places = place(chip_ref[0], core_ref[0])
-    at = kept = 0
+    at = 0
     for i, m in enumerate(counts):
         size, h = 32 * m, places[i][0]
 
@@ -708,15 +715,15 @@
             return keep_ref[span(at, h, size), :] + got_ref[span(at, h, size), :]
 
         refs[i][...] = read(1 - h)
-        refs[3][kept : kept + size, :] = read(h)
-        at, kept = at + 2 * size, kept + size
+        refs[3 + i][...] = read(h)
+        at += 2 * size
 
 
 def open_rows(counts, chip, core, keep, got, *small):
     sizes = [32 * m for m in counts]
     return plain_call(
         functools.partial(open_kernel, counts, bool(small)),
-        sizes + [sum(sizes)],
+        sizes * 2,
         "open_one" if small else "open_two",
         chip,
         core,
@@ -727,78 +734,68 @@
     )
 
 
-def halve_kernel(step, sizes, chip_ref, core_ref, keep_ref, *refs):
-    got, sent, kept_ref = refs[:3], refs[3:6], refs[6]
-    places = place(chip_ref[0], core_ref[0])
-    at = kept = 0
-    for i, size in enumerate(sizes):
-        half, h = size // 2, places[i][step]
-        sent[i][...] = keep_ref[span(at, 1 - h, half), :] + got[i][span(0, 1 - h, half), :]
-        kept_ref[kept : kept + half, :] = keep_ref[span(at, h, half), :] + got[i][span(0, h, half), :]
-        at, kept = at + size, kept + half
-
-
-def halve(step, sizes, chip, core, keep, got):
-    halves = [s // 2 for s in sizes]
-    return plain_call(
-        functools.partial(halve_kernel, step, sizes),
-        halves + [sum(halves)],
-        "halve_%d" % step,
-        chip,
-        core,
-        keep,
-        *got,
+def blend_kernel(i, chip_ref, core_ref, one_ref, two_ref, got_one, got_two, sent, kept):
+    h = place(chip_ref[0], core_ref[0])[i][1]
+    for ref, got, m, begin in ((one_ref, got_one, ONE[i], 0), (two_ref, got_two, TWO[i], ONE[i])):
+        for k in range(16):
+            to = slice(CHUNK * k + begin, CHUNK * k + begin + m)
+            for side, out in ((1 - h, sent), (h, kept)):
+                at = pl.ds(pl.multiple_of(side * (16 * m) + m * k, 8), m)
+                out[to, :] = ref[at, :] + got[at, :]
+
+
+def halve_kernel(i, step, chip_ref, core_ref, keep_ref, got_ref, sent, kept):
+    n, h = sent.shape[0], place(chip_ref[0], core_ref[0])[i][step]
+    sent[...] = keep_ref[span(0, 1 - h, n), :] + got_ref[span(0, 1 - h, n), :]
+    kept[...] = keep_ref[span(0, h, n), :] + got_ref[span(0, h, n), :]
+
+
+def add_kernel(chip_ref, core_ref, own_ref, got_ref, out_ref):
+    out_ref[...] = own_ref[...] + got_ref[...]
+
+
+def double_kernel(i, step, chip_ref, core_ref, own_ref, got_ref, out_ref):
+    n, h = own_ref.shape[0], place(chip_ref[0], core_ref[0])[i][step]
+    out_ref[span(0, h, n), :] = own_ref[...]
+    out_ref[span(0, 1 - h, n), :] = got_ref[...]
+
+
+def swap_one(i, step, sent):
+    return lax.ppermute(sent, ("chip", "core"), swaps(AXES[i][step % 3], step))
+
+
+def reduce_color(i, chip, core, kept_one, kept_two, got_one, got_two):
+    at = (chip, core)
+    name = "xyz"[i]
+    sent, kept = plain_call(
+        functools.partial(blend_kernel, i),
+        [16 * CHUNK] * 2,
+        "blend_" + name,
+        *at,
+        kept_one,
+        kept_two,
+        got_one,
+        got_two,
     )
-
-
-def blend_kernel(chip_ref, core_ref, one_ref, two_ref, *refs):
-    got_one, got_two, sent, kept_ref = refs[:3], refs[3:6], refs[6:9], refs[9]
-    places = place(chip_ref[0], core_ref[0])
-    at_one = at_two = 0
-    for i in range(3):
-        h = places[i][2]
-        for ref, got, at, m, begin in (
-            (one_ref, got_one[i], at_one, ONE[i], 0),
-            (two_ref, got_two[i], at_two, TWO[i], ONE[i]),
-        ):
-            for k in range(8):
-                for side, out, base in ((1 - h, sent[i], 0), (h, kept_ref, 704 * i)):
-                    start = pl.multiple_of(side * (8 * m) + m * k, 8)
-                    value = ref[pl.ds(at + start, m), :] + got[pl.ds(start, m), :]
-                    out[base + CHUNK * k + begin : base + CHUNK * k + begin + m, :] = value
-        at_one, at_two = at_one + 16 * ONE[i], at_two + 16 * TWO[i]
-
-
-def blend(chip, core, one, two, got_one, got_two):
-    return plain_call(
-        blend_kernel, [704] * 3 + [2112], "blend", chip, core, one, two, *got_one, *got_two
+    for step in (2,):
+        got = swap_one(i, step - 1, sent)
+        kernel = functools.partial(halve_kernel, i, step)
+        sizes = [CHUNK * 32 >> step] * 2
+        sent, kept = plain_call(kernel, sizes, "halve_%s%d" % (name, step), *at, kept, got)
+    (own,) = plain_call(
+        add_kernel, [8 * CHUNK], "close_" + name, *at, kept, swap_one(i, 2, sent)
     )
-
-
-def close_kernel(chip_ref, core_ref, keep_ref, *refs):
-    for i in range(3):
-        refs[3 + i][...] = keep_ref[CHUNK * i : CHUNK * (i + 1), :] + refs[i][...]
-
-
-def double_kernel(step, chip_ref, core_ref, *refs):
-    places = place(chip_ref[0], core_ref[0])
-    for i in range(3):
-        own, got, out = refs[i], refs[3 + i], refs[6 + i]
-        n, h = own.shape[0], places[i][step]
-        out[span(0, h, n), :] = own[...]
-        out[span(0, 1 - h, n), :] = got[...]
-
-
-def double(step, chip, core, own, got):
-    return plain_call(
-        functools.partial(double_kernel, step),
-        [2 * own[0].shape[0]] * 3,
-        "double_%d" % step,
-        chip,
-        core,
-        *own,
-        *got,
-    )
+    for step in (3, 4, 5):
+        (own,) = plain_call(
+            add_kernel, [8 * CHUNK], "pair_%s%d" % (name, step), *at, own, swap_one(i, step, own)
+        )
+    for step in (2, 1):
+        kernel = functools.partial(double_kernel, i, step)
+        sizes = [2 * own.shape[0]]
+        (own,) = plain_call(
+            kernel, sizes, "double_%s%d" % (name, step), *at, own, swap_one(i, step, own)
+        )
+    return own
 
 
 def layer_rows(layer):
@@ -873,28 +870,42 @@
 
     @pl.when(step == 0)
     def _():
-        half = 512 * core
-        acc_ref[pl.ds(pl.multiple_of(512 - half, 8), 512), :] = small_in[...]
+        acc_ref[pl.ds(pl.multiple_of(512 * (1 - core), 8), 512), :] = small_in[...]
         for at, value in small_rows():
-            acc_ref[pl.ds(pl.multiple_of(half + at, 8), value.shape[0]), :] = value
-        tower_inner[0] = acc_ref[0:256, :]
-        tower_inner[1] = acc_ref[256:512, :]
+            acc_ref[pl.ds(pl.multiple_of(512 * core + at, 8), value.shape[0]), :] = value
+
+        def early(at, count):
+            parts = []
+            if at < SHARE:
+                parts.append(acc_ref[at : min(at + count, SHARE), :])
+            if at + count > SHARE:
+                parts.append(acc_ref[512 + max(at, SHARE) - SHARE : 512 + at + count - SHARE, :])
+            return parts[0] if len(parts) == 1 else jnp.concatenate(parts, axis=0)
+
+        def late(at, count):
+            at += SHARE
+            return acc_ref[at : at + count, :] + acc_ref[512 + at : 512 + at + count, :]
+
+        tower_inner[0] = early(0, 256)
+        tower_inner[1] = early(256, 256)
         for s in range(2):
             lanes = slice(s * 128, (s + 1) * 128)
-            for at, codes, mix, back in (
-                (512, codes_one, mix_one, back_one),
-                (624, codes_two, mix_two, back_two),
+            for at, read, codes, mix, back in (
+                (0, late, codes_one, mix_one, back_one),
+                (512, early, codes_two, mix_two, back_two),
             ):
                 at += 56 * s
-                codes[:, lanes] = acc_ref[at : at + 32, :]
-                mix[:, lanes] = acc_ref[at + 32 : at + 40, :]
-                back[:, lanes] = acc_ref[at + 40 : at + 56, :]
-            bias_one[:, lanes] = acc_ref[736 + 16 * s : 752 + 16 * s, :]
-            bias_two[:, lanes] = acc_ref[768 + 16 * s : 784 + 16 * s, :]
-        tower_outer[...] = acc_ref[800:802, :]
-        tower_bias[...] = acc_ref[802:804, :]
-        lane = lax.broadcasted_iota(jnp.int32, (1, 128), 1)
-        tower_last[...] = jnp.where(lane == 0, acc_ref[804:805, :], acc_ref[805:806, :])
+                codes[:, lanes] = read(at, 32)
+                mix[:, lanes] = read(at + 32, 8)
+                back[:, lanes] = read(at + 40, 16)
+            for ref, found in ((bias_one, late(112 + 16 * s, 16)), (bias_two, early(624 + 16 * s, 16))):
+                for e in range(EXPERTS):
+                    ref[2 * e + s : 2 * e + s + 1, :] = found[e : e + 1]
+        last = early(656, 8)
+        tower_outer[...] = last[0:2]
+        tower_bias[...] = last[2:4]
+        tower_last[:, 0:1] = last[4:5, 0:1]
+        tower_last[:, 1:2] = last[5:6, 0:1]
 
 
 def lay(mine, chip, core, own, got, more):
@@ -912,14 +923,14 @@
 
     in_specs = [still(a.shape) for a in (*own, *got)]
     if mine:
-        little = [(SMALL // 2, 128)]
+        little = [(512, 128)]
         scratch, aliases = [], {}
     else:
         in_specs += [still(more[0].shape)] + [pl.BlockSpec(memory_space=pl.ANY)] * 4
         aliases = {9: 0, 10: 1, 11: 2, 12: 3}
-        little = [(32, WIDTH), (8, WIDTH), (EXPERTS, WIDTH), (EXPERTS, HID)] * 2
-        little += [(TASKS, WIDTH, TOWER), (TASKS, TOWER), (TASKS, TOWER), (1, 128)]
-        scratch = [pltpu.VMEM((SMALL, 128), F32)]
+        little = [(32, WIDTH), (8, WIDTH), (EXPERTS, WIDTH), (2 * EXPERTS, 128)] * 2
+        little += [(TASKS, WIDTH, TOWER), (TASKS, TOWER), (TASKS, TOWER), (1, TASKS)]
+        scratch = [pltpu.VMEM((1024, 128), F32)]
     shapes += little
     out_specs += [still(s) for s in little]
     return pl.pallas_call(
@@ -935,7 +946,7 @@
         input_output_aliases=aliases,
         cost_estimate=pl.CostEstimate(flops=0, bytes_accessed=16_000_000, transcendentals=0),
         compiler_params=pltpu.CompilerParams(
-            dimension_semantics=("arbitrary",), vmem_limit_bytes=32 * 1024 * 1024
+            dimension_semantics=("arbitrary",), vmem_limit_bytes=32 * MIB
         ),
         name="lay_own" if mine else "lay_other",
     )(chip, core, *own, *got, *more)
@@ -984,37 +995,30 @@
     )
     towers = (tower_inner, tower_inner_bias, tower_outer, tower_outer_bias.reshape(1, TASKS))
     towers = (labels.T, counts, lengths.reshape(1, -1), base, *towers)
-    send, keep_two, bias_two, rest_two, dy, predictions, little, grad_tower_inner = main_part(
+    send, keep_two, dy, predictions, small_send, small_keep = main_part(
         core, u_two, codes_two, mixing_two, inner_two, inner_bias_two, outer_two, outer_bias_two, towers
     )
     got_two = cross(send)
+    small_got = cross(small_send)
     send, bias_one, acc, dgate = last_part(
         True, core, u, inner_one, outer_one, state, gate, dy, ()
     )
     got_one = cross(send)
-    *sent, kept_two = open_rows(TWO, chip, core, keep_two, got_two)
+    opened = open_rows(TWO, chip, core, keep_two, got_two)
+    sent, kept_two = opened[:3], opened[3:]
     got_two = swap(0, sent)
     more = (acc, dgate, codes_one, mixing_one, outer_bias_one, code, mix)
-    more += (bias_one, bias_two, rest_two, little, grad_tower_inner)
-    keep_one, grad_tokens, small_send, small_keep = last_part(
+    more += (bias_one,)
+    keep_one, grad_tokens, small_own = last_part(
         False, core, u, inner_one, outer_one, state, gate, dy, more
     )
-    small_got = cross(small_send)
     *got_two, keep_one = lax.optimization_barrier((*got_two, keep_one))
-    *sent, kept_two = halve(1, [32 * m for m in TWO], chip, core, kept_two, got_two)
-    got_two = swap(1, sent)
-    *sent, kept_one = open_rows(ONE, chip, core, keep_one, got_one, small_keep, small_got)
-    got_one = swap(0, sent)
-    *sent, kept_one = halve(1, [32 * m for m in ONE], chip, core, kept_one, got_one)
-    got_one = swap(1, sent)
-    *sent, kept = blend(chip, core, kept_one, kept_two, got_one, got_two)
-    for step in (3, 4, 5):
-        got = swap(step - 1, sent)
-        *sent, kept = halve(step, [CHUNK * 64 >> step] * 3, chip, core, kept, got)
-    got = swap(5, sent)
-    own = plain_call(close_kernel, [CHUNK] * 3, "close", chip, core, kept, *got)
-    for step in (5, 4, 3, 2, 1):
-        own = double(step, chip, core, own, swap(step, own))
+    opened = open_rows(ONE, chip, core, keep_one, got_one, small_keep, small_got, small_own)
+    got_one = swap(0, opened[:3])
+    own = [
+        reduce_color(i, chip, core, opened[3 + i], kept_two[i], got_one[i], got_two[i])
+        for i in (2, 1, 0)
+    ][::-1]
     got = swap(0, own)
     own_other = [cross(a) for a in own]
     got_other = [cross(a) for a in got]
@@ -1041,7 +1045,7 @@
         tower_inner,
         tower_bias,
         tower_outer,
-        tower_last[0, :2],
+        tower_last.reshape(-1),
     )
 
 

time: 254 us -> 211 us (0.83)
  starting transfers between devices: 94.2 us -> 57.6 us
  waiting for transfers between devices: 70.3 us -> 62.6 us
  Pallas kernels: 71.7 us -> 75.1 us
    ppermute x9, starting transfers between devices: 37.1 us -> 9.28 us  [cross(): return lax.ppermute(a, 'core', [(0, 1), (1, 0)])]
    ppermute x42 -> x30, starting transfers between devices: 45.6 us -> 36.9 us  [the longest x21 18.4 us: swap_one(): return lax.ppermute(sent, ('chip', 'core'), swaps(AXES[i][step % 3], step))]
    ppermute x42 -> x30, waiting for transfers between devices: 67.9 us -> 62 us  [the longest x21 41.2 us: swap_one(): return lax.ppermute(sent, ('chip', 'core'), swaps(AXES[i][step % 3], step))]
  transfers between devices with their start and end apart: 52 -> 40, of which waited for: 34 -> 23; matrix products, arithmetic and copies ran while one was open for 1% -> 0% of each run, Pallas kernels for 12% -> 16%
where the time goes in v3:
time: 211 us; the launch traced here: 208 us
  Pallas kernels  75.1 us (36%)
  waiting for transfers between devices  62.6 us (30%)
  starting transfers between devices  57.6 us (27%)
  local copies, waits for them, and re-layouts  9.77 us (5%)
    ppermute x21, waiting for transfers between devices, swap_one(): return lax.ppermute(sent, ('chip', 'core'), swaps(AXES[i][step % 3], step))  41.2 us
    pallas_call x1, Pallas kernels, main_part(): pl.pallas_call(functools.partial(main_kernel, rows), grid_spec=pltpu.Pref...  35.8 us
    ppermute x9, waiting for transfers between devices, swap(): lax.ppermute(s, ('chip', 'core'), swaps(axes[step % 3], step))  20.9 us
    ppermute x21, starting transfers between devices, swap_one(): return lax.ppermute(sent, ('chip', 'core'), swaps(AXES[i][step % 3], step))  18.4 us
    ppermute x9, starting transfers between devices, swap(): lax.ppermute(s, ('chip', 'core'), swaps(axes[step % 3], step))  18.4 us
    pallas_call x2, Pallas kernels, last_part(): pl.pallas_call(functools.partial(last_kernel, sending, rows), grid_spec=p...  14.1 us
    pallas_call x1, Pallas kernels, first_part(): pl.pallas_call(functools.partial(first_kernel, rows), grid=(WAVES,), in_s...  12.3 us
    all_to_all x1, starting transfers between devices, on_device(): counts = lax.all_to_all(sent, ('chip', 'core'), 0, 0, tiled=True)  11.5 us
  transfers between devices with their start and end apart: 40, of which 23 were waited for; matrix products, arithmetic and copies ran while one was open for 0% of the time, Pallas kernels for 16%

profile of v3, /device:TPU:1, one launch (start us, length us, event | category | flops | bytes accessed | tf_op | source)
XLA Modules:
  0.0 207.5 jit_solution(2020656392998098763)
XLA Ops:
  2.1 11.5 %all-to-all-start = ((f32[128,1,128]{2,1,0:T(1,128)}), f32[128,1,128]{2,1,0:T(1,128)S(1)}, u32[]{:S(2)}, u32[]{:S(2)}) async-start(f32[128,1,128]{2,1,0:T(1,128)} %broadcast_in_dim.2), calls=%async_computation | async-start | bytes 131072 | tf_op jit(solution)/shard_map/all_to_all | solution.py:992
  13.6 12.3 %first_part.1 = (bf16[16,256,512]{2,1,0:T(8,128)(2,1)}, bf16[16,256,512]{2,1,0:T(8,128)(2,1)}, bf16[16,256,512]{2,1,0:T(8,128)(2,1)}, f32[16,1024]{1,0:T(8,128)}...) custom-call(bf16[512,256]{1,0:T(8,128)(2,1)} %tokens_ref.1, ...), custom_call_target="tpu_custom_call" | custom-call | flops 8000000000 | bytes 20000000 | tf_op jit(solution)/shard_map/first_part/pallas_call | solution.py:379
  26.6 35.8 %main_part.1 = (f32[8,1024,128]{2,1,0:T(8,128)}, f32[8,1024,128]{2,1,0:T(8,128)}, f32[256,1024]{1,0:T(8,128)}, f32[2,512]{1,0:T(2,128)}, f32[336,128]{1,0:T(8,128)}, /*index=5*/f32[336,128]{1,0:T(8,128)}) custom-call(s32[1]{0:T(128)} %bitcast.core_ref, bf16[256,1024]{1,0:T(8,128)(2,1)} %get-tuple-element.88.refs_0_, bf16[32,256]{1,0:T(8,128)(2,1)} %bitcast.36, ...), custom_call_target="tpu_custom_call" | custom-call | flops 14000000000 | bytes 40000000 | tf_op jit(solution)/shard_map/main_part/pallas_call | solution.py:483
  62.3 1.2 collective-permute-start
  63.5 1.6 copy-done.3
  65.1 2.2 %copy-done.8 = bf16[16,256,512]{2,1,0:T(8,128)(2,1)S(1)} copy-done((bf16[16,256,512]{2,1,0:T(8,128)(2,1)S(1)}, bf16[16,256,512]{2,1,0:T(8,128)(2,1)}, u32[]{:S(2)}) %copy-start.8) | copy-done | bytes 4194328
  67.3 1.2 copy-done.9
  68.5 0.9 copy-done.13
  70.3 6.2 %last_send.1 = (f32[8,1024,128]{2,1,0:T(8,128)}, f32[4,4,256]{2,1,0:T(4,128)S(1)}, f32[256,512]{1,0:T(8,128)S(1)}, f32[16,1024]{1,0:T(8,128)S(1)}) custom-call(s32[1]{0:T(128)} %bitcast.core_ref, bf16[256,512]{1,0:T(8,128)(2,1)S(1)} %copy-done.13, bf16[256,4096]{1,0:T(8,128)(2,1)S(1)} %copy-done.2, bf16[16,256,256]{2,1,0:T(8,128)(2,1)S(1)} %copy-done.3, ...), custom_call_target="tpu_custom_call" | custom-call | flops 8000000000 | bytes 20000000 | tf_op jit(solution)/shard_map/last_send/pallas_call | solution.py:633
  78.1 2.8 %collective-permute-start.3 = (f32[1536,128]{1,0:T(8,128)S(1)}, f32[1536,128]{1,0:T(8,128)S(1)}, u32[]{:S(2)}, u32[]{:S(2)}) collective-permute-start(f32[1536,128]{1,0:T(8,128)S(1)} %get-tuple-element.106), channel_id=1, source_target_pairs={{0,8},{1,25},{2,10},{3,27},{4,12},{5,29},{6,14},{7,31},{8,0},{9,17... | collective-permute-start | bytes 2359304 | tf_op jit(solution)/shard_map/ppermute | solution.py:675
  80.9 2.4 %collective-permute-start.1 = (f32[1280,128]{1,0:T(8,128)S(1)}, f32[1280,128]{1,0:T(8,128)S(1)}, u32[]{:S(2)}, u32[]{:S(2)}) collective-permute-start(f32[1280,128]{1,0:T(8,128)S(1)} %get-tuple-element.104), channel_id=1, source_target_pairs={{0,2},{1,7},{2,0},{3,5},{4,6},{5,3},{6,4},{7,1},{8,10},{9,15},{10,... | collective-permute-start | bytes 1966088 | tf_op jit(solution)/shard_map/ppermute | solution.py:675
  83.3 2.6 %collective-permute-start.2 = (f32[1280,128]{1,0:T(8,128)S(1)}, f32[1280,128]{1,0:T(8,128)S(1)}, u32[]{:S(2)}, u32[]{:S(2)}) collective-permute-start(f32[1280,128]{1,0:T(8,128)S(1)} %get-tuple-element.105), channel_id=1, source_target_pairs={{0,32},{1,97},{2,34},{3,99},{4,36},{5,101},{6,38},{7,103},{8,40},{... | collective-permute-start | bytes 1966088 | tf_op jit(solution)/shard_map/ppermute | solution.py:675
  86.8 7.9 %last_keep.1 = (f32[8,1024,128]{2,1,0:T(8,128)S(1)}, f32[512,256]{1,0:T(8,128)}, f32[144,128]{1,0:T(8,128)S(1)}) custom-call(s32[1]{0:T(128)} %bitcast.core_ref, bf16[256,512]{1,0:T(8,128)(2,1)S(1)} %copy-done.14, bf16[256,4096]{1,0:T(8,128)(2,1)S(1)} %copy-done.2, bf16[16,256,256]{2,1,0:T(8,128)(2,1)S(1)} %copy-done.4, ...), custom_call_target="tpu_custom_call" | custom-call | flops 8000000000 | bytes 20000000 | tf_op jit(solution)/shard_map/last_keep/pallas_call | solution.py:633
  94.7 2.8 %open_one.1 = (f32[1536,128]{1,0:T(8,128)S(1)}, f32[1536,128]{1,0:T(8,128)S(1)}, f32[1280,128]{1,0:T(8,128)S(1)}, f32[1536,128]{1,0:T(8,128)S(1)}, f32[1536,128]{1,0:T(8,128)S(1)}, /*index=5*/f32[1280,128]{1,0:T(8,128)S(1)}) custom-call(s32[1]{0:T(128)} %bitcast.13.chip_ref, s32[1]{0:T(128)} %bitcast.core_ref, f32[8192,128]{1,0:T(8,128)S(1)} %bitcast.27, ...), custom_call_target="tpu_custom_call" | custom-call | bytes 2000000 | tf_op jit(solution)/shard_map/open_one/pallas_call | solution.py:683
  97.5 1.9 collective-permute-start.15
  99.7 1.2 collective-permute-start.24
  100.8 9.5 %collective-permute-done.24.got_one = f32[1280,128]{1,0:T(8,128)S(1)} collective-permute-done((f32[1280,128]{1,0:T(8,128)S(1)}, f32[1280,128]{1,0:T(8,128)S(1)}, u32[]{:S(2)}, u32[]{:S(2)}) %collective-permute-start.24) | collective-permute-done | bytes 655392 | tf_op jit(solution)/shard_map/ppermute | solution.py:675
  110.5 2.5 %collective-permute-start.25 = (f32[1408,128]{1,0:T(8,128)S(1)}, f32[1408,128]{1,0:T(8,128)S(1)}, u32[]{:S(2)}, u32[]{:S(2)}) collective-permute-start(f32[1408,128]{1,0:T(8,128)S(1)} %get-tuple-element.134), channel_id=1, source_target_pairs={{0,2},{1,7},{2,0},{3,5},{4,6},{5,3},{6,4},{7,1},{8,10},{9,15},{10,... | collective-permute-start | bytes 2162696 | tf_op jit(solution)/shard_map/ppermute | solution.py:764
  113.2 1.0 collective-permute-start.16
  115.3 6.7 %collective-permute-done.25.got_ref = f32[1408,128]{1,0:T(8,128)S(1)} collective-permute-done((f32[1408,128]{1,0:T(8,128)S(1)}, f32[1408,128]{1,0:T(8,128)S(1)}, u32[]{:S(2)}, u32[]{:S(2)}) %collective-permute-start.25) | collective-permute-done | bytes 720928 | tf_op jit(solution)/shard_map/ppermute | solution.py:764
  122.9 1.7 collective-permute-done.16.got_ref
  125.9 1.8 collective-permute-start.8
  127.7 2.0 collective-permute-done.26.got_ref
  129.8 2.5 %collective-permute-done.17.got_ref = f32[704,128]{1,0:T(8,128)S(1)} collective-permute-done((f32[704,128]{1,0:T(8,128)S(1)}, f32[704,128]{1,0:T(8,128)S(1)}, u32[]{:S(2)}, u32[]{:S(2)}) %collective-permute-start.17) | collective-permute-done | bytes 360480 | tf_op jit(solution)/shard_map/ppermute | solution.py:764
  132.4 2.4 %collective-permute-done.8.got_ref = f32[704,128]{1,0:T(8,128)S(1)} collective-permute-done((f32[704,128]{1,0:T(8,128)S(1)}, f32[704,128]{1,0:T(8,128)S(1)}, u32[]{:S(2)}, u32[]{:S(2)}) %collective-permute-start.8) | collective-permute-done | bytes 360480 | tf_op jit(solution)/shard_map/ppermute | solution.py:764
  134.9 1.4 collective-permute-done.27.got_ref
  136.7 2.2 %collective-permute-done.18.got_ref = f32[704,128]{1,0:T(8,128)S(1)} collective-permute-done((f32[704,128]{1,0:T(8,128)S(1)}, f32[704,128]{1,0:T(8,128)S(1)}, u32[]{:S(2)}, u32[]{:S(2)}) %collective-permute-start.18) | collective-permute-done | bytes 360480 | tf_op jit(solution)/shard_map/ppermute | solution.py:764
  139.1 2.1 collective-permute-done.9.got_ref
  141.3 4.0 %collective-permute-done.28.got_ref = f32[704,128]{1,0:T(8,128)S(1)} collective-permute-done((f32[704,128]{1,0:T(8,128)S(1)}, f32[704,128]{1,0:T(8,128)S(1)}, u32[]{:S(2)}, u32[]{:S(2)}) %collective-permute-start.28) | collective-permute-done | bytes 360480 | tf_op jit(solution)/shard_map/ppermute | solution.py:764
  145.8 2.1 collective-permute-done.10.got_ref
  148.0 4.0 %collective-permute-done.29.got_ref = f32[704,128]{1,0:T(8,128)S(1)} collective-permute-done((f32[704,128]{1,0:T(8,128)S(1)}, f32[704,128]{1,0:T(8,128)S(1)}, u32[]{:S(2)}, u32[]{:S(2)}) %collective-permute-start.29) | collective-permute-done | bytes 360480 | tf_op jit(solution)/shard_map/ppermute | solution.py:764
  152.0 1.4 collective-permute-start.30
  154.6 2.9 %collective-permute-start.12 = (f32[704,128]{1,0:T(8,128)S(1)}, f32[704,128]{1,0:T(8,128)S(1)}, u32[]{:S(2)}, u32[]{:S(2)}) collective-permute-start(f32[704,128]{1,0:T(8,128)S(1)} %pair_x5.1.own_ref), channel_id=1, source_target_pairs={{0,8},{1,25},{2,10},{3,27},{4,12},{5,29},{6,14},{7,31},{8,0},{9,17... | collective-permute-start | bytes 1081352 | tf_op jit(solution)/shard_map/ppermute | solution.py:764
  157.4 2.5 %collective-permute-done.30.got_ref = f32[704,128]{1,0:T(8,128)S(1)} collective-permute-done((f32[704,128]{1,0:T(8,128)S(1)}, f32[704,128]{1,0:T(8,128)S(1)}, u32[]{:S(2)}, u32[]{:S(2)}) %collective-permute-start.30) | collective-permute-done | bytes 360480 | tf_op jit(solution)/shard_map/ppermute | solution.py:764
  160.0 1.0 collective-permute-start.31
  161.1 1.6 collective-permute-start.22
  163.0 2.5 %collective-permute-start.13 = (f32[1408,128]{1,0:T(8,128)S(1)}, f32[1408,128]{1,0:T(8,128)S(1)}, u32[]{:S(2)}, u32[]{:S(2)}) collective-permute-start(f32[1408,128]{1,0:T(8,128)S(1)} %double_x2.1.own_ref), channel_id=1, source_target_pairs={{0,32},{1,97},{2,34},{3,99},{4,36},{5,101},{6,38},{7,103},{8,40},{... | collective-permute-start | bytes 2162696 | tf_op jit(solution)/shard_map/ppermute | solution.py:764
  165.5 5.9 %collective-permute-done.31.got_ref = f32[1408,128]{1,0:T(8,128)S(1)} collective-permute-done((f32[1408,128]{1,0:T(8,128)S(1)}, f32[1408,128]{1,0:T(8,128)S(1)}, u32[]{:S(2)}, u32[]{:S(2)}) %collective-permute-start.31) | collective-permute-done | bytes 720928 | tf_op jit(solution)/shard_map/ppermute | solution.py:764
  171.5 2.6 %collective-permute-start.37 = (f32[2816,128]{1,0:T(8,128)S(1)}, f32[2816,128]{1,0:T(8,128)S(1)}, u32[]{:S(2)}, u32[]{:S(2)}) collective-permute-start(f32[2816,128]{1,0:T(8,128)S(1)} %double_z1.1.refs_2_), channel_id=1, source_target_pairs={{0,8},{1,25},{2,10},{3,27},{4,12},{5,29},{6,14},{7,31},{8,0},{9,17... | collective-permute-start | bytes 4325384 | tf_op jit(solution)/shard_map/ppermute | solution.py:675
  174.1 0.9 collective-permute-start.32
  175.1 1.7 collective-permute-start.35
  176.9 3.1 %collective-permute-start.33 = (f32[2816,128]{1,0:T(8,128)S(1)}, f32[2816,128]{1,0:T(8,128)S(1)}, u32[]{:S(2)}, u32[]{:S(2)}) collective-permute-start(f32[2816,128]{1,0:T(8,128)S(1)} %double_x1.1.refs_0_), channel_id=1, source_target_pairs={{0,2},{1,7},{2,0},{3,5},{4,6},{5,3},{6,4},{7,1},{8,10},{9,15},{10,... | collective-permute-start | bytes 4325384 | tf_op jit(solution)/shard_map/ppermute | solution.py:675
  180.0 10.7 %collective-permute-done.37.refs_5_ = f32[2816,128]{1,0:T(8,128)S(1)} collective-permute-done((f32[2816,128]{1,0:T(8,128)S(1)}, f32[2816,128]{1,0:T(8,128)S(1)}, u32[]{:S(2)}, u32[]{:S(2)}) %collective-permute-start.37) | collective-permute-done | bytes 1441824 | tf_op jit(solution)/shard_map/ppermute | solution.py:675
  190.6 3.3 %collective-permute-start.14 = (f32[2816,128]{1,0:T(8,128)S(1)}, f32[2816,128]{1,0:T(8,128)S(1)}, u32[]{:S(2)}, u32[]{:S(2)}) collective-permute-start(f32[2816,128]{1,0:T(8,128)S(1)} %double_x1.1.refs_0_), channel_id=1, source_target_pairs={{0,1},{1,0},{2,3},{3,2},{4,5},{5,4},{6,7},{7,6},{8,9},{9,8},{10,11... | collective-permute-start | bytes 4325384 | tf_op jit(solution)/shard_map/ppermute | solution.py:982
  194.2 1.7 collective-permute-start.36
  196.4 2.2 %collective-permute-start.34 = (f32[2816,128]{1,0:T(8,128)S(1)}, f32[2816,128]{1,0:T(8,128)S(1)}, u32[]{:S(2)}, u32[]{:S(2)}) collective-permute-start(f32[2816,128]{1,0:T(8,128)S(1)} %collective-permute-done.33.refs_3_), channel_id=1, source_target_pairs={{0,1},{1,0},{2,3},{3,2},{4,5},{5,4},{6,7},{7,6},{8,9},{9,8},{10,11... | collective-permute-start | bytes 4325384 | tf_op jit(solution)/shard_map/ppermute | solution.py:982
  198.5 3.9 %lay_own.1 = (f32[256,4096]{1,0:T(8,128)}, f32[16,256,256]{2,1,0:T(8,128)}, f32[256,4096]{1,0:T(8,128)}, f32[16,256,256]{2,1,0:T(8,128)}, f32[512,128]{1,0:T(8,128)S(1)}) custom-call(s32[1]{0:T(128)} %bitcast.13.chip_ref, s32[1]{0:T(128)} %bitcast.core_ref, f32[2816,128]{1,0:T(8,128)S(1)} %double_x1.1.refs_0_, f32[2816,128]{1,0:T(8,128)S(1)} %double_y1.1.refs_1_, ...), custom_call_target="tpu_custom_call" | custom-call | bytes 16000000 | tf_op jit(solution)/shard_map/lay_own/pallas_call | solution.py:936
  202.9 4.1 %lay_other.1 = (f32[256,4096]{1,0:T(8,128)}, f32[16,256,256]{2,1,0:T(8,128)}, f32[256,4096]{1,0:T(8,128)}, f32[16,256,256]{2,1,0:T(8,128)}, f32[32,256]{1,0:T(8,...) custom-call(s32[1]{0:T(128)} %bitcast.13.chip_ref, ...), custom_call_target="tpu_custom_call", output_to_operand_aliasing={{0}: (9, {}), {1}: (10, {}), {2}: (11, {}), {3}: (12, {})} | custom-call | bytes 16000000 | tf_op jit(solution)/shard_map/lay_other/pallas_call | solution.py:936
  (113 shorter events, 13.9 us)
Async XLA Ops:
  2.1 23.8 %all-to-all-start = ((f32[128,1,128]{2,1,0:T(1,128)}), f32[128,1,128]{2,1,0:T(1,128)S(1)}, u32[]{:S(2)}, u32[]{:S(2)}) async-start(f32[128,1,128]{2,1,0:T(1,128)} %broadcast_in_dim.2), calls=%async_computation | async-start | bytes 131072 | tf_op jit(solution)/shard_map/all_to_all | solution.py:992
  26.6 36.9 %copy-start.2 = (bf16[256,4096]{1,0:T(8,128)(2,1)S(1)}, bf16[256,4096]{1,0:T(8,128)(2,1)}, u32[]{:S(2)}) copy-start(bf16[256,4096]{1,0:T(8,128)(2,1)} %refs_1_.3) | copy-start | bytes 6291460
  62.3 15.0 %collective-permute-start = (f32[8,1024,128]{2,1,0:T(8,128)}, f32[8,1024,128]{2,1,0:T(8,128)S(1)}, u32[]{:S(2)}, u32[]{:S(2)}) collective-permute-start(f32[8,1024,128]{2,1,0:T(8,128)} %get-tuple-element.103), channel_id=1, source_target_pairs={{0,1},{1,0},{2,3},{3,2},{4,5},{5,4},{6,7},{7,6},{8,9},{9,8},{10,11... | collective-permute-start | bytes 12582920 | tf_op jit(solution)/shard_map/ppermute | solution.py:982
  77.3 17.4 %collective-permute-start.4 = (f32[8,1024,128]{2,1,0:T(8,128)}, f32[8,1024,128]{2,1,0:T(8,128)}, u32[]{:S(2)}, u32[]{:S(2)}) collective-permute-start(f32[8,1024,128]{2,1,0:T(8,128)} %get-tuple-element.109), channel_id=1, source_target_pairs={{0,1},{1,0},{2,3},{3,2},{4,5},{5,4},{6,7},{7,6},{8,9},{9,8},{10,11... | collective-permute-start | bytes 12582920 | tf_op jit(solution)/shard_map/ppermute | solution.py:982
  77.4 8.5 %copy-start.4 = (bf16[16,256,256]{2,1,0:T(8,128)(2,1)S(1)}, bf16[16,256,256]{2,1,0:T(8,128)(2,1)}, u32[]{:S(2)}) copy-start(bf16[16,256,256]{2,1,0:T(8,128)(2,1)} %refs_2_.3) | copy-start | bytes 6291460
  77.4 8.5 %copy-start.5 = (bf16[256,32]{0,1:T(8,128)(2,1)S(1)}, bf16[256,32]{0,1:T(8,128)(2,1)}, u32[]{:S(2)}) copy-start(bf16[256,32]{0,1:T(8,128)(2,1)} %param.22) | copy-start | bytes 49156
  77.4 8.5 %copy-start.6 = (bf16[16,256]{1,0:T(8,128)(2,1)S(1)}, bf16[16,256]{1,0:T(8,128)(2,1)}, u32[]{:S(2)}) copy-start(bf16[16,256]{1,0:T(8,128)(2,1)} %refs_12_.3) | copy-start | bytes 24580
  77.4 8.5 %copy-start.7 = (bf16[256,8]{0,1:T(8,128)(2,1)S(1)}, bf16[256,8]{0,1:T(8,128)(2,1)}, u32[]{:S(2)}) copy-start(bf16[256,8]{0,1:T(8,128)(2,1)} %param.23) | copy-start | bytes 12292
  77.4 8.5 %copy-start.10 = (f32[256,1024]{1,0:T(8,128)S(1)}, f32[256,1024]{1,0:T(8,128)}, u32[]{:S(2)}) copy-start(f32[256,1024]{1,0:T(8,128)} %get-tuple-element.95.refs_7_) | copy-start | bytes 3145732
  77.4 8.5 %copy-start.12 = (f32[256,512]{1,0:T(8,128)S(1)}, f32[256,512]{1,0:T(8,128)}, u32[]{:S(2)}) copy-start(f32[256,512]{1,0:T(8,128)} %copy-done.11) | copy-start | bytes 1572868
  77.4 8.5 %copy-start.14 = (bf16[256,512]{1,0:T(8,128)(2,1)S(1)}, bf16[256,512]{1,0:T(8,128)(2,1)}, u32[]{:S(2)}) copy-start(bf16[256,512]{1,0:T(8,128)(2,1)} %get-tuple-element.90.refs_0_) | copy-start | bytes 786436
  78.1 16.6 %collective-permute-start.3 = (f32[1536,128]{1,0:T(8,128)S(1)}, f32[1536,128]{1,0:T(8,128)S(1)}, u32[]{:S(2)}, u32[]{:S(2)}) collective-permute-start(f32[1536,128]{1,0:T(8,128)S(1)} %get-tuple-element.106), channel_id=1, source_target_pairs={{0,8},{1,25},{2,10},{3,27},{4,12},{5,29},{6,14},{7,31},{8,0},{9,17... | collective-permute-start | bytes 2359304 | tf_op jit(solution)/shard_map/ppermute | solution.py:675
  80.9 13.8 %collective-permute-start.5 = (f32[336,128]{1,0:T(8,128)S(1)}, f32[336,128]{1,0:T(8,128)S(1)}, u32[]{:S(2)}, u32[]{:S(2)}) collective-permute-start(f32[336,128]{1,0:T(8,128)S(1)} %copy-done.22), channel_id=1, source_target_pairs={{0,1},{1,0},{2,3},{3,2},{4,5},{5,4},{6,7},{7,6},{8,9},{9,8},{10,11... | collective-permute-start | bytes 516104 | tf_op jit(solution)/shard_map/ppermute | solution.py:982
  80.9 13.8 %collective-permute-start.1 = (f32[1280,128]{1,0:T(8,128)S(1)}, f32[1280,128]{1,0:T(8,128)S(1)}, u32[]{:S(2)}, u32[]{:S(2)}) collective-permute-start(f32[1280,128]{1,0:T(8,128)S(1)} %get-tuple-element.104), channel_id=1, source_target_pairs={{0,2},{1,7},{2,0},{3,5},{4,6},{5,3},{6,4},{7,1},{8,10},{9,15},{10,... | collective-permute-start | bytes 1966088 | tf_op jit(solution)/shard_map/ppermute | solution.py:675
  83.3 11.4 %collective-permute-start.2 = (f32[1280,128]{1,0:T(8,128)S(1)}, f32[1280,128]{1,0:T(8,128)S(1)}, u32[]{:S(2)}, u32[]{:S(2)}) collective-permute-start(f32[1280,128]{1,0:T(8,128)S(1)} %get-tuple-element.105), channel_id=1, source_target_pairs={{0,32},{1,97},{2,34},{3,99},{4,36},{5,101},{6,38},{7,103},{8,40},{... | collective-permute-start | bytes 1966088 | tf_op jit(solution)/shard_map/ppermute | solution.py:675
  97.5 15.5 %collective-permute-start.15 = (f32[1536,128]{1,0:T(8,128)S(1)}, f32[1536,128]{1,0:T(8,128)S(1)}, u32[]{:S(2)}, u32[]{:S(2)}) collective-permute-start(f32[1536,128]{1,0:T(8,128)S(1)} %get-tuple-element.123), channel_id=1, source_target_pairs={{0,32},{1,97},{2,34},{3,99},{4,36},{5,101},{6,38},{7,103},{8,40},{... | collective-permute-start | bytes 2359304 | tf_op jit(solution)/shard_map/ppermute | solution.py:675
  99.5 14.7 %collective-permute-start.6 = (f32[1536,128]{1,0:T(8,128)S(1)}, f32[1536,128]{1,0:T(8,128)S(1)}, u32[]{:S(2)}, u32[]{:S(2)}) collective-permute-start(f32[1536,128]{1,0:T(8,128)S(1)} %get-tuple-element.115), channel_id=1, source_target_pairs={{0,2},{1,7},{2,0},{3,5},{4,6},{5,3},{6,4},{7,1},{8,10},{9,15},{10,... | collective-permute-start | bytes 2359304 | tf_op jit(solution)/shard_map/ppermute | solution.py:675
  99.7 10.6 %collective-permute-start.24 = (f32[1280,128]{1,0:T(8,128)S(1)}, f32[1280,128]{1,0:T(8,128)S(1)}, u32[]{:S(2)}, u32[]{:S(2)}) collective-permute-start(f32[1280,128]{1,0:T(8,128)S(1)} %get-tuple-element.131), channel_id=1, source_target_pairs={{0,8},{1,25},{2,10},{3,27},{4,12},{5,29},{6,14},{7,31},{8,0},{9,17... | collective-permute-start | bytes 1966088 | tf_op jit(solution)/shard_map/ppermute | solution.py:675
  110.5 11.4 %collective-permute-start.25 = (f32[1408,128]{1,0:T(8,128)S(1)}, f32[1408,128]{1,0:T(8,128)S(1)}, u32[]{:S(2)}, u32[]{:S(2)}) collective-permute-start(f32[1408,128]{1,0:T(8,128)S(1)} %get-tuple-element.134), channel_id=1, source_target_pairs={{0,2},{1,7},{2,0},{3,5},{4,6},{5,3},{6,4},{7,1},{8,10},{9,15},{10,... | collective-permute-start | bytes 2162696 | tf_op jit(solution)/shard_map/ppermute | solution.py:764
  113.2 11.4 %collective-permute-start.16 = (f32[1408,128]{1,0:T(8,128)S(1)}, f32[1408,128]{1,0:T(8,128)S(1)}, u32[]{:S(2)}, u32[]{:S(2)}) collective-permute-start(f32[1408,128]{1,0:T(8,128)S(1)} %get-tuple-element.126), channel_id=1, source_target_pairs={{0,8},{1,25},{2,10},{3,27},{4,12},{5,29},{6,14},{7,31},{8,0},{9,17... | collective-permute-start | bytes 2162696 | tf_op jit(solution)/shard_map/ppermute | solution.py:764
  114.3 11.4 %collective-permute-start.7 = (f32[1408,128]{1,0:T(8,128)S(1)}, f32[1408,128]{1,0:T(8,128)S(1)}, u32[]{:S(2)}, u32[]{:S(2)}) collective-permute-start(f32[1408,128]{1,0:T(8,128)S(1)} %get-tuple-element.118), channel_id=1, source_target_pairs={{0,32},{1,97},{2,34},{3,99},{4,36},{5,101},{6,38},{7,103},{8,40},{... | collective-permute-start | bytes 2162696 | tf_op jit(solution)/shard_map/ppermute | solution.py:764
  122.0 7.6 %collective-permute-start.26 = (f32[704,128]{1,0:T(8,128)S(1)}, f32[704,128]{1,0:T(8,128)S(1)}, u32[]{:S(2)}, u32[]{:S(2)}) collective-permute-start(f32[704,128]{1,0:T(8,128)S(1)} %get-tuple-element.136), channel_id=1, source_target_pairs={{0,32},{1,97},{2,34},{3,99},{4,36},{5,101},{6,38},{7,103},{8,40},{... | collective-permute-start | bytes 1081352 | tf_op jit(solution)/shard_map/ppermute | solution.py:764
  124.7 7.6 %collective-permute-start.17 = (f32[704,128]{1,0:T(8,128)S(1)}, f32[704,128]{1,0:T(8,128)S(1)}, u32[]{:S(2)}, u32[]{:S(2)}) collective-permute-start(f32[704,128]{1,0:T(8,128)S(1)} %get-tuple-element.128), channel_id=1, source_target_pairs={{0,2},{1,7},{2,0},{3,5},{4,6},{5,3},{6,4},{7,1},{8,10},{9,15},{10,... | collective-permute-start | bytes 1081352 | tf_op jit(solution)/shard_map/ppermute | solution.py:764
  125.9 8.9 %collective-permute-start.8 = (f32[704,128]{1,0:T(8,128)S(1)}, f32[704,128]{1,0:T(8,128)S(1)}, u32[]{:S(2)}, u32[]{:S(2)}) collective-permute-start(f32[704,128]{1,0:T(8,128)S(1)} %get-tuple-element.120), channel_id=1, source_target_pairs={{0,8},{1,25},{2,10},{3,27},{4,12},{5,29},{6,14},{7,31},{8,0},{9,17... | collective-permute-start | bytes 1081352 | tf_op jit(solution)/shard_map/ppermute | solution.py:764
  129.7 6.7 %collective-permute-start.27 = (f32[704,128]{1,0:T(8,128)S(1)}, f32[704,128]{1,0:T(8,128)S(1)}, u32[]{:S(2)}, u32[]{:S(2)}) collective-permute-start(f32[704,128]{1,0:T(8,128)S(1)} %close_z.1.own_ref), channel_id=1, source_target_pairs={{0,24},{1,9},{2,26},{3,11},{4,28},{5,13},{6,30},{7,15},{8,16},{9,1... | collective-permute-start | bytes 1081352 | tf_op jit(solution)/shard_map/ppermute | solution.py:764
  132.3 6.7 %collective-permute-start.18 = (f32[704,128]{1,0:T(8,128)S(1)}, f32[704,128]{1,0:T(8,128)S(1)}, u32[]{:S(2)}, u32[]{:S(2)}) collective-permute-start(f32[704,128]{1,0:T(8,128)S(1)} %close_y.1.own_ref), channel_id=1, source_target_pairs={{0,96},{1,33},{2,98},{3,35},{4,100},{5,37},{6,102},{7,39},{8,104},... | collective-permute-start | bytes 1081352 | tf_op jit(solution)/shard_map/ppermute | solution.py:764
  134.8 6.4 %collective-permute-start.9 = (f32[704,128]{1,0:T(8,128)S(1)}, f32[704,128]{1,0:T(8,128)S(1)}, u32[]{:S(2)}, u32[]{:S(2)}) collective-permute-start(f32[704,128]{1,0:T(8,128)S(1)} %close_x.1.own_ref), channel_id=1, source_target_pairs={{0,6},{1,3},{2,4},{3,1},{4,2},{5,7},{6,0},{7,5},{8,14},{9,11},{10,... | collective-permute-start | bytes 1081352 | tf_op jit(solution)/shard_map/ppermute | solution.py:764
  136.4 8.9 %collective-permute-start.28 = (f32[704,128]{1,0:T(8,128)S(1)}, f32[704,128]{1,0:T(8,128)S(1)}, u32[]{:S(2)}, u32[]{:S(2)}) collective-permute-start(f32[704,128]{1,0:T(8,128)S(1)} %pair_z3.1.own_ref), channel_id=1, source_target_pairs={{0,6},{1,3},{2,4},{3,1},{4,2},{5,7},{6,0},{7,5},{8,14},{9,11},{10,... | collective-permute-start | bytes 1081352 | tf_op jit(solution)/shard_map/ppermute | solution.py:764
  139.0 6.7 %collective-permute-start.19 = (f32[704,128]{1,0:T(8,128)S(1)}, f32[704,128]{1,0:T(8,128)S(1)}, u32[]{:S(2)}, u32[]{:S(2)}) collective-permute-start(f32[704,128]{1,0:T(8,128)S(1)} %pair_y3.1.own_ref), channel_id=1, source_target_pairs={{0,24},{1,9},{2,26},{3,11},{4,28},{5,13},{6,30},{7,15},{8,16},{9,1... | collective-permute-start | bytes 1081352 | tf_op jit(solution)/shard_map/ppermute | solution.py:764
  141.2 6.7 %collective-permute-start.10 = (f32[704,128]{1,0:T(8,128)S(1)}, f32[704,128]{1,0:T(8,128)S(1)}, u32[]{:S(2)}, u32[]{:S(2)}) collective-permute-start(f32[704,128]{1,0:T(8,128)S(1)} %pair_x3.1.own_ref), channel_id=1, source_target_pairs={{0,96},{1,33},{2,98},{3,35},{4,100},{5,37},{6,102},{7,39},{8,104},... | collective-permute-start | bytes 1081352 | tf_op jit(solution)/shard_map/ppermute | solution.py:764
  145.3 6.7 %collective-permute-start.29 = (f32[704,128]{1,0:T(8,128)S(1)}, f32[704,128]{1,0:T(8,128)S(1)}, u32[]{:S(2)}, u32[]{:S(2)}) collective-permute-start(f32[704,128]{1,0:T(8,128)S(1)} %pair_z4.1.own_ref), channel_id=1, source_target_pairs={{0,96},{1,33},{2,98},{3,35},{4,100},{5,37},{6,102},{7,39},{8,104},... | collective-permute-start | bytes 1081352 | tf_op jit(solution)/shard_map/ppermute | solution.py:764
  145.7 7.8 %collective-permute-start.20 = (f32[704,128]{1,0:T(8,128)S(1)}, f32[704,128]{1,0:T(8,128)S(1)}, u32[]{:S(2)}, u32[]{:S(2)}) collective-permute-start(f32[704,128]{1,0:T(8,128)S(1)} %pair_y4.1.own_ref), channel_id=1, source_target_pairs={{0,6},{1,3},{2,4},{3,1},{4,2},{5,7},{6,0},{7,5},{8,14},{9,11},{10,... | collective-permute-start | bytes 1081352 | tf_op jit(solution)/shard_map/ppermute | solution.py:764
  147.9 6.7 %collective-permute-start.11 = (f32[704,128]{1,0:T(8,128)S(1)}, f32[704,128]{1,0:T(8,128)S(1)}, u32[]{:S(2)}, u32[]{:S(2)}) collective-permute-start(f32[704,128]{1,0:T(8,128)S(1)} %pair_x4.1.own_ref), channel_id=1, source_target_pairs={{0,24},{1,9},{2,26},{3,11},{4,28},{5,13},{6,30},{7,15},{8,16},{9,1... | collective-permute-start | bytes 1081352 | tf_op jit(solution)/shard_map/ppermute | solution.py:764
  152.0 7.9 %collective-permute-start.30 = (f32[704,128]{1,0:T(8,128)S(1)}, f32[704,128]{1,0:T(8,128)S(1)}, u32[]{:S(2)}, u32[]{:S(2)}) collective-permute-start(f32[704,128]{1,0:T(8,128)S(1)} %pair_z5.1.own_ref), channel_id=1, source_target_pairs={{0,32},{1,97},{2,34},{3,99},{4,36},{5,101},{6,38},{7,103},{8,40},{... | collective-permute-start | bytes 1081352 | tf_op jit(solution)/shard_map/ppermute | solution.py:764
  153.5 7.6 %collective-permute-start.21 = (f32[704,128]{1,0:T(8,128)S(1)}, f32[704,128]{1,0:T(8,128)S(1)}, u32[]{:S(2)}, u32[]{:S(2)}) collective-permute-start(f32[704,128]{1,0:T(8,128)S(1)} %pair_y5.1.own_ref), channel_id=1, source_target_pairs={{0,2},{1,7},{2,0},{3,5},{4,6},{5,3},{6,4},{7,1},{8,10},{9,15},{10,... | collective-permute-start | bytes 1081352 | tf_op jit(solution)/shard_map/ppermute | solution.py:764
  154.6 8.3 %collective-permute-start.12 = (f32[704,128]{1,0:T(8,128)S(1)}, f32[704,128]{1,0:T(8,128)S(1)}, u32[]{:S(2)}, u32[]{:S(2)}) collective-permute-start(f32[704,128]{1,0:T(8,128)S(1)} %pair_x5.1.own_ref), channel_id=1, source_target_pairs={{0,8},{1,25},{2,10},{3,27},{4,12},{5,29},{6,14},{7,31},{8,0},{9,17... | collective-permute-start | bytes 1081352 | tf_op jit(solution)/shard_map/ppermute | solution.py:764
  160.0 11.4 %collective-permute-start.31 = (f32[1408,128]{1,0:T(8,128)S(1)}, f32[1408,128]{1,0:T(8,128)S(1)}, u32[]{:S(2)}, u32[]{:S(2)}) collective-permute-start(f32[1408,128]{1,0:T(8,128)S(1)} %double_z2.1.own_ref), channel_id=1, source_target_pairs={{0,2},{1,7},{2,0},{3,5},{4,6},{5,3},{6,4},{7,1},{8,10},{9,15},{10,... | collective-permute-start | bytes 2162696 | tf_op jit(solution)/shard_map/ppermute | solution.py:764
  161.1 13.9 %collective-permute-start.22 = (f32[1408,128]{1,0:T(8,128)S(1)}, f32[1408,128]{1,0:T(8,128)S(1)}, u32[]{:S(2)}, u32[]{:S(2)}) collective-permute-start(f32[1408,128]{1,0:T(8,128)S(1)} %double_y2.1.own_ref), channel_id=1, source_target_pairs={{0,8},{1,25},{2,10},{3,27},{4,12},{5,29},{6,14},{7,31},{8,0},{9,17... | collective-permute-start | bytes 2162696 | tf_op jit(solution)/shard_map/ppermute | solution.py:764
  163.0 13.8 %collective-permute-start.13 = (f32[1408,128]{1,0:T(8,128)S(1)}, f32[1408,128]{1,0:T(8,128)S(1)}, u32[]{:S(2)}, u32[]{:S(2)}) collective-permute-start(f32[1408,128]{1,0:T(8,128)S(1)} %double_x2.1.own_ref), channel_id=1, source_target_pairs={{0,32},{1,97},{2,34},{3,99},{4,36},{5,101},{6,38},{7,103},{8,40},{... | collective-permute-start | bytes 2162696 | tf_op jit(solution)/shard_map/ppermute | solution.py:764
  171.5 19.2 %collective-permute-start.37 = (f32[2816,128]{1,0:T(8,128)S(1)}, f32[2816,128]{1,0:T(8,128)S(1)}, u32[]{:S(2)}, u32[]{:S(2)}) collective-permute-start(f32[2816,128]{1,0:T(8,128)S(1)} %double_z1.1.refs_2_), channel_id=1, source_target_pairs={{0,8},{1,25},{2,10},{3,27},{4,12},{5,29},{6,14},{7,31},{8,0},{9,17... | collective-permute-start | bytes 4325384 | tf_op jit(solution)/shard_map/ppermute | solution.py:675
  174.1 19.9 %collective-permute-start.32 = (f32[2816,128]{1,0:T(8,128)S(1)}, f32[2816,128]{1,0:T(8,128)S(1)}, u32[]{:S(2)}, u32[]{:S(2)}) collective-permute-start(f32[2816,128]{1,0:T(8,128)S(1)} %double_z1.1.refs_2_), channel_id=1, source_target_pairs={{0,1},{1,0},{2,3},{3,2},{4,5},{5,4},{6,7},{7,6},{8,9},{9,8},{10,11... | collective-permute-start | bytes 4325384 | tf_op jit(solution)/shard_map/ppermute | solution.py:982
  175.1 19.2 %collective-permute-start.35 = (f32[2816,128]{1,0:T(8,128)S(1)}, f32[2816,128]{1,0:T(8,128)S(1)}, u32[]{:S(2)}, u32[]{:S(2)}) collective-permute-start(f32[2816,128]{1,0:T(8,128)S(1)} %double_y1.1.refs_1_), channel_id=1, source_target_pairs={{0,32},{1,97},{2,34},{3,99},{4,36},{5,101},{6,38},{7,103},{8,40},{... | collective-permute-start | bytes 4325384 | tf_op jit(solution)/shard_map/ppermute | solution.py:675
  176.9 19.5 %collective-permute-start.33 = (f32[2816,128]{1,0:T(8,128)S(1)}, f32[2816,128]{1,0:T(8,128)S(1)}, u32[]{:S(2)}, u32[]{:S(2)}) collective-permute-start(f32[2816,128]{1,0:T(8,128)S(1)} %double_x1.1.refs_0_), channel_id=1, source_target_pairs={{0,2},{1,7},{2,0},{3,5},{4,6},{5,3},{6,4},{7,1},{8,10},{9,15},{10,... | collective-permute-start | bytes 4325384 | tf_op jit(solution)/shard_map/ppermute | solution.py:675
  180.0 22.4 %collective-permute-start.23 = (f32[2816,128]{1,0:T(8,128)S(1)}, f32[2816,128]{1,0:T(8,128)S(1)}, u32[]{:S(2)}, u32[]{:S(2)}) collective-permute-start(f32[2816,128]{1,0:T(8,128)S(1)} %double_y1.1.refs_1_), channel_id=1, source_target_pairs={{0,1},{1,0},{2,3},{3,2},{4,5},{5,4},{6,7},{7,6},{8,9},{9,8},{10,11... | collective-permute-start | bytes 4325384 | tf_op jit(solution)/shard_map/ppermute | solution.py:982
  190.6 11.7 %collective-permute-start.14 = (f32[2816,128]{1,0:T(8,128)S(1)}, f32[2816,128]{1,0:T(8,128)S(1)}, u32[]{:S(2)}, u32[]{:S(2)}) collective-permute-start(f32[2816,128]{1,0:T(8,128)S(1)} %double_x1.1.refs_0_), channel_id=1, source_target_pairs={{0,1},{1,0},{2,3},{3,2},{4,5},{5,4},{6,7},{7,6},{8,9},{9,8},{10,11... | collective-permute-start | bytes 4325384 | tf_op jit(solution)/shard_map/ppermute | solution.py:982
  193.9 8.5 %collective-permute-start.38 = (f32[2816,128]{1,0:T(8,128)S(1)}, f32[2816,128]{1,0:T(8,128)S(1)}, u32[]{:S(2)}, u32[]{:S(2)}) collective-permute-start(f32[2816,128]{1,0:T(8,128)S(1)} %collective-permute-done.37.refs_5_), channel_id=1, source_target_pairs={{0,1},{1,0},{2,3},{3,2},{4,5},{5,4},{6,7},{7,6},{8,9},{9,8},{10,11... | collective-permute-start | bytes 4325384 | tf_op jit(solution)/shard_map/ppermute | solution.py:982
  194.2 8.1 %collective-permute-start.36 = (f32[2816,128]{1,0:T(8,128)S(1)}, f32[2816,128]{1,0:T(8,128)S(1)}, u32[]{:S(2)}, u32[]{:S(2)}) collective-permute-start(f32[2816,128]{1,0:T(8,128)S(1)} %collective-permute-done.35.refs_4_), channel_id=1, source_target_pairs={{0,1},{1,0},{2,3},{3,2},{4,5},{5,4},{6,7},{7,6},{8,9},{9,8},{10,11... | collective-permute-start | bytes 4325384 | tf_op jit(solution)/shard_map/ppermute | solution.py:982
  196.4 6.6 %collective-permute-start.34 = (f32[2816,128]{1,0:T(8,128)S(1)}, f32[2816,128]{1,0:T(8,128)S(1)}, u32[]{:S(2)}, u32[]{:S(2)}) collective-permute-start(f32[2816,128]{1,0:T(8,128)S(1)} %collective-permute-done.33.refs_3_), channel_id=1, source_target_pairs={{0,1},{1,0},{2,3},{3,2},{4,5},{5,4},{6,7},{7,6},{8,9},{9,8},{10,11... | collective-permute-start | bytes 4325384 | tf_op jit(solution)/shard_map/ppermute | solution.py:982
  (15 other events, 53.7 us)

commit v4 on v3

--- a/solution.py
+++ b/solution.py
@@ -19,6 +19,8 @@
 HALF = STEPS // 2
 GROUP = 4
 WAVES = EXPERTS // GROUP
+AHEAD = 4
+ROUNDS = EXPERTS // AHEAD
 SLAB = 1024
 SMALL = 672
 SHARE = SMALL // 2
@@ -126,7 +128,7 @@
 
 
 def whole(shape):
-    return pl.BlockSpec(shape, lambda *_: (0,) * len(shape))
+    return pl.BlockSpec(shape, lambda *_: (0,) * len(shape), pipeline_mode=pl.Buffered(1))
 
 
 def tower(
@@ -212,7 +214,7 @@
         acc_ref[:, span] = tn(outer_bias, hi) + tn(outer_bias, mid) + tn(outer_bias, low)
 
 
-def forward_wave(shared, rows, wave, u_ref, inner_ref, bias_ref, outer_ref, state, gate_ref, acc_ref, work):
+def forward_wave(shared, rows, wave, u_ref, inner_ref, bias_ref, outer_ref, state, gate_ref, acc_ref, work, ready=None):
     bias = bias_ref[...].astype(F32).T
     lanes = rows if shared else rows * TASKS
     tiles = lanes // 256
@@ -236,6 +238,9 @@
             hid, slope = gelu_both(pre_refs[p % 2][here, :lanes] + column)
             hid_ref[here, :] = hid.astype(BF16)
             slope_ref[here, :] = slope.astype(BF16)
+        if ready and q == tiles - 1:
+            ready(p, 0)
+            ready(p, 1)
 
     def start_out(p, q):
         if q == 0:
@@ -245,7 +250,7 @@
 
     def combine(p, q):
         if q == 0:
-            kept["gate", p] = gate_ref[pl.ds(wave * GROUP + p, 1), :]
+            kept["gate", p] = gate_ref[pl.ds(wave * AHEAD + p, 1), :]
         gate = kept["gate", p]
         for at in range(q * part, (q + 1) * part, tall):
             here = slice(at, at + tall)
@@ -254,8 +259,10 @@
             for t in range(TASKS if shared else 1):
                 span = slice(t * rows, (t + 1) * rows) if shared else slice(0, lanes)
                 acc_ref[here, span] += gate[:, span] * out
-
-    pipeline(GROUP, tiles, (start_pre, bend, start_out, combine))
+        if ready and q == tiles - 1:
+            ready(p, 2)
+
+    pipeline(AHEAD, tiles, (start_pre, bend, start_out, combine))
 
 
 def backward_wave(shared, rows, wave, aug_ref, inner_ref, outer_ref, state, gate_ref, dy_ref, acc_ref, dgate_ref, slab_ref, bias_ref, dout_ref, dpre_ref, work):
@@ -318,11 +325,12 @@
     dcode_ref[...] = jnp.zeros_like(dcode_ref)
     dmix_ref[...] = jnp.zeros_like(dmix_ref)
     outer_bias = outer_bias_ref[...]
+    y_hi, y_mid = pieces(dy_ref[...])[:2]
+    bias_share = nn(outer_bias, y_hi) + nn(outer_bias, y_mid)
     for t in range(TASKS):
         span = slice(t * rows, (t + 1) * rows)
         here = task_lanes(t, rows, shared)
-        hi, mid, low = pieces(dy_ref[:, span])
-        upto = nn(outer_bias, hi) + nn(outer_bias, mid) + nn(outer_bias, low)
+        upto = bias_share[:, span]
         code, mix = task_rows(code_ref, mix_ref, t, here)
         grad_code, grad_mix = gate_back(code, mix, dgate_ref[:, span] + upto)
         for k in range(16):
@@ -333,8 +341,7 @@
     dmix = dmix_ref[...].astype(BF16)
     rest_ref[:32, :] = nt(dcode, u)
     rest_ref[32:40, :] = nt(dmix, u)
-    g_hi, g_mid, _ = pieces(gate_ref[...])
-    y_hi, y_mid, _ = pieces(dy_ref[...])
+    g_hi, g_mid = pieces(gate_ref[...])[:2]
     rest_ref[40:56, :] = nt(g_hi, y_hi) + nt(g_hi, y_mid) + nt(g_mid, y_hi)
     return acc_ref[...] + tn(codes_ref[...], dcode) + tn(mixing_ref[...], dmix)
 
@@ -346,7 +353,8 @@
 
 
 def first_kernel(rows, tokens_ref, codes_ref, mixing_ref, inner_ref, bias_ref, outer_ref, outer_bias_ref, *refs):
-    (hid_ref, slope_ref, out_ref, gate_ref, code_ref, mix_ref, turned, next_ref, acc_ref), work = refs[:9], refs[9:]
+    far, (gate_ref, code_ref, mix_ref, turned, next_ref), refs = refs[:3], refs[3:8], refs[8:]
+    near, (sems, acc_ref), work = refs[:3], refs[3:5], refs[5:]
     step = pl.program_id(0)
 
     @pl.when(step == 0)
@@ -354,92 +362,131 @@
         turned[...] = tokens_ref[...].astype(F32).T.astype(BF16)
         prepare(True, rows, turned[...], codes_ref, mixing_ref, outer_bias_ref, code_ref, mix_ref, gate_ref, acc_ref)
 
+    slot = step % 2
+
     def state(p):
-        return hid_ref.at[p], slope_ref.at[p], out_ref.at[p]
-
-    forward_wave(True, rows, step, turned, inner_ref, bias_ref, outer_ref, state, gate_ref, acc_ref, work)
-
-    @pl.when(step == WAVES - 1)
+        return tuple(r.at[slot, p] for r in near)
+
+    def copy(wave, p, k):
+        to = far[k].at[wave * AHEAD + p]
+        return pltpu.make_async_copy(near[k].at[wave % 2, p], to, sems.at[k, wave % 2, p])
+
+    def settle(wave):
+        for p in range(AHEAD):
+            for k in range(3):
+                copy(wave, p, k).wait()
+
+    @pl.when(step >= 2)
+    def _():
+        settle(step - 2)
+
+    def ready(p, k):
+        copy(step, p, k).start()
+
+    forward_wave(True, rows, step, turned, inner_ref, bias_ref, outer_ref, state, gate_ref, acc_ref, work, ready)
+
+    @pl.when(step == ROUNDS - 1)
     def _():
         next_ref[...] = acc_ref[...].astype(BF16)
+        settle(step - 1)
+        settle(step)
 
 
 def first_part(tokens, codes, mixing, inner, inner_bias, outer, outer_bias):
     rows = tokens.shape[0]
     wide = rows * TASKS
-    state = jax.ShapeDtypeStruct((EXPERTS, HID, rows), BF16)
+    arrays = (tokens, codes, mixing, inner, inner_bias.reshape(2 * EXPERTS, 128), outer, outer_bias)
+    arrays = [pltpu.with_memory_space_constraint(a, pltpu.HBM) for a in arrays]
+    state = pltpu.HBM((EXPERTS, HID, rows), BF16)
     plain = [
-        jax.ShapeDtypeStruct((EXPERTS, wide), F32),
-        jax.ShapeDtypeStruct((32, rows), F32),
-        jax.ShapeDtypeStruct((8, rows), F32),
-        jax.ShapeDtypeStruct((WIDTH, rows), BF16),
+        pltpu.HBM((EXPERTS, wide), F32),
+        pltpu.HBM((32, rows), F32),
+        pltpu.HBM((8, rows), F32),
+        pltpu.HBM((WIDTH, rows), BF16),
         jax.ShapeDtypeStruct((WIDTH, wide), BF16),
     ]
-    state_spec = pl.BlockSpec((GROUP, HID, rows), lambda i: (i, 0, 0))
     return pl.pallas_call(
         functools.partial(first_kernel, rows),
-        grid=(WAVES,),
+        grid=(ROUNDS,),
         in_specs=[
             whole(tokens.shape),
             whole(codes.shape),
             whole(mixing.shape),
-            pl.BlockSpec((WIDTH, GROUP * HID), lambda i: (0, i)),
-            pl.BlockSpec((2 * GROUP, 128), lambda i: (i, 0)),
-            pl.BlockSpec((GROUP, HID, WIDTH), lambda i: (i, 0, 0)),
+            pl.BlockSpec((WIDTH, AHEAD * HID), lambda i: (0, i)),
+            pl.BlockSpec((2 * AHEAD, 128), lambda i: (i, 0)),
+            pl.BlockSpec((AHEAD, HID, WIDTH), lambda i: (i, 0, 0)),
             whole(outer_bias.shape),
         ],
-        out_specs=[state_spec] * 3 + [whole(s.shape) for s in plain],
+        out_specs=[pl.BlockSpec(memory_space=pl.ANY)] * 3 + [whole(s.shape) for s in plain],
         out_shape=[state] * 3 + plain,
-        scratch_shapes=[pltpu.VMEM((WIDTH, wide), F32)] + [pltpu.VMEM((HID, rows), F32)] * 4,
+        scratch_shapes=[
+            *[pltpu.VMEM((2, AHEAD, HID, rows), BF16)] * 3,
+            pltpu.SemaphoreType.DMA((3, 2, AHEAD)),
+            pltpu.VMEM((WIDTH, wide), F32),
+        ]
+        + [pltpu.VMEM((HID, rows), F32)] * 4,
         cost_estimate=pl.CostEstimate(flops=8_000_000_000, bytes_accessed=20_000_000, transcendentals=0),
         compiler_params=pltpu.CompilerParams(
-            dimension_semantics=("arbitrary",), vmem_limit_bytes=61 * MIB
+            dimension_semantics=("arbitrary",), vmem_limit_bytes=26 * MIB
         ),
         name="first_part",
-    )(tokens, codes, mixing, inner, inner_bias.reshape(2 * EXPERTS, 128), outer, outer_bias)
+    )(*arrays)
 
 
 def main_kernel(rows, core_ref, *refs):
     (u_ref, codes_two, mixing_two, inner_two, bias_two, outer_two, outer_bias_two), refs = refs[:7], refs[7:]
+    (inner_back, outer_back), refs = refs[:2], refs[2:]
     tower_in, refs = refs[:8], refs[8:]
     (send_ref, keep_ref, dy_one, predictions, small_send, small_keep), refs = refs[:6], refs[6:]
     (grad_bias, rest_ref, little, tower_inner, small_ref), refs = refs[:5], refs[5:]
     tower_out = (predictions, little, tower_inner)
+    (slab_ref, sems), refs = refs[:2], refs[2:]
     (hid_two, slope_two, out_two, gate_two, code_two, mix_two, aug, v_ref), refs = refs[:8], refs[8:]
     (acc_ref, dy_two, dgate_ref, dcode_ref, dmix_ref, dout_ref, dpre_ref), work = refs[:7], refs[7:]
     step = pl.program_id(0)
 
-    def state_two(wave):
-        return lambda p: tuple(r.at[wave * GROUP + p] for r in (hid_two, slope_two, out_two))
+    def state_two(base):
+        return lambda p: tuple(r.at[base + p] for r in (hid_two, slope_two, out_two))
 
     @pl.when(step == 0)
     def _():
         extend(aug, u_ref[...])
         prepare(False, rows, u_ref[...], codes_two, mixing_two, outer_bias_two, code_two, mix_two, gate_two, acc_ref)
 
-    @pl.when(step < WAVES)
+    @pl.when(step < ROUNDS)
     def _():
-        forward_wave(False, rows, step, aug, inner_two, bias_two, outer_two, state_two(step), gate_two, acc_ref, work)
-
-    @pl.when(step == WAVES)
+        forward_wave(False, rows, step, aug, inner_two, bias_two, outer_two, state_two(step * AHEAD), gate_two, acc_ref, work)
+
+    @pl.when(step == ROUNDS)
     def _():
         v_ref[...] = acc_ref[...].astype(BF16)
         tower(rows, v_ref, *tower_in, *tower_out, dy_two)
         acc_ref[...] = jnp.zeros_like(acc_ref)
 
-    def back(slab_ref):
-        wave = (step + 2 * (1 - core_ref[0])) % WAVES
-        backward_wave(False, rows, wave, aug, inner_two, outer_two, state_two(wave), gate_two, dy_two, acc_ref, dgate_ref, slab_ref, grad_bias.at[pl.ds(wave, 1)], dout_ref, dpre_ref, work)
-
-    @pl.when((step >= WAVES) & (step < WAVES + 2))
+    def carry(j):
+        out_ref = send_ref if j < 2 else keep_ref
+        at = pl.ds(GROUP * (j % 2), GROUP)
+        return pltpu.make_async_copy(slab_ref.at[j % 2], out_ref.at[at], sems.at[j])
+
+    for j in range(WAVES):
+
+        @pl.when(step == ROUNDS + j)
+        def _():
+            if j >= 2:
+                carry(j - 2).wait()
+
+    @pl.when(step >= ROUNDS)
     def _():
-        back(send_ref)
-
-    @pl.when(step >= WAVES + 2)
-    def _():
-        back(keep_ref)
-
-    @pl.when(step == 2 * WAVES - 1)
+        wave = (step - ROUNDS + 2 * (1 - core_ref[0])) % WAVES
+        backward_wave(False, rows, wave, aug, inner_back, outer_back, state_two(wave * GROUP), gate_two, dy_two, acc_ref, dgate_ref, slab_ref.at[(step - ROUNDS) % 2], grad_bias.at[pl.ds(wave, 1)], dout_ref, dpre_ref, work)
+
+    for j in range(WAVES):
+
+        @pl.when(step == ROUNDS + j)
+        def _():
+            carry(j).start()
+
+    @pl.when(step == ROUNDS + WAVES - 1)
     def _():
         dy_one[...] = finish(False, rows, u_ref[...], codes_two, mixing_two, outer_bias_two, code_two, mix_two, gate_two, dy_two, dgate_ref, acc_ref, dcode_ref, dmix_ref, rest_ref)
         small_ref[0:256, :] = tower_inner[0]
@@ -454,10 +501,11 @@
         core = core_ref[0]
         small_send[...] = small_ref[pl.ds(pl.multiple_of((1 - core) * SHARE, 8), SHARE), :]
         small_keep[...] = small_ref[pl.ds(pl.multiple_of(core * SHARE, 8), SHARE), :]
-
-
-def fixed(shape):
-    return pl.BlockSpec(shape, lambda i, core: (0,) * len(shape))
+        carry(2).wait()
+        carry(3).wait()
+
+
+fixed = whole
 
 
 def main_part(core, u, codes, mixing, inner, inner_bias, outer, outer_bias, tower_in):
@@ -465,12 +513,12 @@
     rows = wide // TASKS
 
     def order(i, core):
-        return jnp.where(i < WAVES, i, (i + 2 * (1 - core[0])) % WAVES)
+        return jnp.minimum(i, ROUNDS - 1)
+
+    def back(i, core):
+        return (jnp.maximum(i - ROUNDS, 0) + 2 * (1 - core[0])) % WAVES
 
     slab = jax.ShapeDtypeStruct((EXPERTS // 2, SLAB, 128), F32)
-
-    def slab_spec(begin):
-        return pl.BlockSpec((GROUP, SLAB, 128), lambda i, core: (jnp.clip(i - begin, 0, 1), 0, 0))
 
     rest = [
         jax.ShapeDtypeStruct((WIDTH, wide), F32),
@@ -478,24 +526,27 @@
         jax.ShapeDtypeStruct((SHARE, 128), F32),
         jax.ShapeDtypeStruct((SHARE, 128), F32),
     ]
+    inner, outer = [pltpu.with_memory_space_constraint(a, pltpu.HBM) for a in (inner, outer)]
     tower_specs = [fixed(a.shape) for a in tower_in]
     tower_specs[3] = pl.BlockSpec(memory_space=pltpu.SMEM)
     return pl.pallas_call(
         functools.partial(main_kernel, rows),
         grid_spec=pltpu.PrefetchScalarGridSpec(
             num_scalar_prefetch=1,
-            grid=(2 * WAVES,),
+            grid=(ROUNDS + WAVES,),
             in_specs=[
                 fixed(u.shape),
                 fixed(codes.shape),
                 fixed(mixing.shape),
-                pl.BlockSpec((WIDTH, GROUP * HID), lambda i, core: (0, order(i, core))),
-                pl.BlockSpec((2 * GROUP, 128), lambda i, core: (order(i, core), 0)),
-                pl.BlockSpec((GROUP, HID, WIDTH), lambda i, core: (order(i, core), 0, 0)),
+                pl.BlockSpec((WIDTH, AHEAD * HID), lambda i, core: (0, order(i, core))),
+                pl.BlockSpec((2 * AHEAD, 128), lambda i, core: (order(i, core), 0)),
+                pl.BlockSpec((AHEAD, HID, WIDTH), lambda i, core: (order(i, core), 0, 0)),
                 fixed(outer_bias.shape),
+                pl.BlockSpec((WIDTH, GROUP * HID), lambda i, core: (0, back(i, core))),
+                pl.BlockSpec((GROUP, HID, WIDTH), lambda i, core: (back(i, core), 0, 0)),
             ]
             + tower_specs,
-            out_specs=[slab_spec(WAVES), slab_spec(WAVES + 2)]
+            out_specs=[pl.BlockSpec(memory_space=pl.ANY)] * 2
             + [fixed(s.shape) for s in rest],
             scratch_shapes=[
                 pltpu.VMEM((WAVES, GROUP, HID), F32),
@@ -503,6 +554,8 @@
                 pltpu.VMEM((8, TOWER), F32),
                 pltpu.VMEM((TASKS, WIDTH, TOWER), F32),
                 pltpu.VMEM((SMALL, 128), F32),
+                pltpu.VMEM((2, GROUP, SLAB, 128), F32),
+                pltpu.SemaphoreType.DMA((WAVES,)),
                 *[pltpu.VMEM((EXPERTS, HID, wide), BF16)] * 3,
                 pltpu.VMEM((EXPERTS, wide), F32),
                 pltpu.VMEM((32, wide), F32),
@@ -522,7 +575,7 @@
         out_shape=[slab, slab] + rest,
         cost_estimate=pl.CostEstimate(flops=14_000_000_000, bytes_accessed=40_000_000, transcendentals=0),
         compiler_params=pltpu.CompilerParams(
-            dimension_semantics=("arbitrary",), vmem_limit_bytes=61 * MIB
+            dimension_semantics=("arbitrary",), vmem_limit_bytes=46 * MIB
         ),
         name="main_part",
     )(
@@ -534,12 +587,16 @@
         inner_bias.reshape(2 * EXPERTS, 128),
         outer,
         outer_bias,
+        inner,
+        outer,
         *tower_in,
     )
 
 
 def last_kernel(sending, rows, core_ref, *refs):
-    (u_ref, inner_ref, outer_ref, hid_ref, slope_ref, out_ref, gate_ref, dy_ref), refs = refs[:8], refs[8:]
+    far, (u_ref, gate_ref, dy_ref), refs = refs[:5], refs[5:8], refs[8:]
+    near, sems, refs = refs[-6:-1], refs[-1], refs[:-6]
+    inner_ref, outer_ref, hid_ref, slope_ref, out_ref = near
     step = pl.program_id(0)
     if sending:
         (slab_ref, bias_ref, acc_ref, dgate_ref), refs = refs[:4], refs[4:]
@@ -553,8 +610,21 @@
         wave = step + 2 * core_ref[0]
         bias_at = bias_ref.at[pl.ds(step, 1)]
 
+    def fetch(j):
+        e = wave - step + j
+        at = pl.ds(pl.multiple_of(e * GROUP, GROUP), GROUP)
+        columns = pl.ds(pl.multiple_of(e * GROUP * HID, GROUP * HID), GROUP * HID)
+        sources = [far[0].at[:, columns]] + [r.at[at] for r in far[1:]]
+        return [
+            pltpu.make_async_copy(a, b.at[j], sems.at[k, j])
+            for k, (a, b) in enumerate(zip(sources, near))
+        ]
+
     @pl.when(step == 0)
     def _():
+        for j in range(2):
+            for copy in fetch(j):
+                copy.start()
         extend(aug, u_ref[...])
         if sending:
             acc_ref[...] = jnp.zeros_like(acc_ref)
@@ -563,10 +633,13 @@
             acc_ref[...] = acc_in[...]
             dgate_ref[...] = dgate_in[...]
 
+    for copy in fetch(step):
+        copy.wait()
+
     def state(p):
-        return hid_ref.at[p], slope_ref.at[p], out_ref.at[p]
-
-    backward_wave(True, rows, wave, aug, inner_ref, outer_ref, state, gate_ref, dy_ref, acc_ref, dgate_ref, slab_ref, bias_at, dout_ref, dpre_ref, work)
+        return hid_ref.at[step, p], slope_ref.at[step, p], out_ref.at[step, p]
+
+    backward_wave(True, rows, wave, aug, inner_ref.at[step], outer_ref.at[step], state, gate_ref, dy_ref, acc_ref, dgate_ref, slab_ref, bias_at, dout_ref, dpre_ref, work)
     if sending:
         return
 
@@ -589,17 +662,11 @@
     def wave(i, core):
         return i + 2 * (1 - core[0] if sending else core[0])
 
-    state_spec = pl.BlockSpec((GROUP, HID, rows), lambda i, core: (wave(i, core), 0, 0))
-    arrays = [u, inner, outer, *state, gate, dy, *more]
-    in_specs = [
-        fixed(u.shape),
-        pl.BlockSpec((WIDTH, GROUP * HID), lambda i, core: (0, wave(i, core))),
-        pl.BlockSpec((GROUP, HID, WIDTH), lambda i, core: (wave(i, core), 0, 0)),
-        state_spec,
-        state_spec,
-        state_spec,
-    ]
-    in_specs += [fixed(a.shape) for a in arrays[6:]]
+    inner, outer = [pltpu.with_memory_space_constraint(a, pltpu.HBM) for a in (inner, outer)]
+    state = [pltpu.with_memory_space_constraint(a, pltpu.HBM) for a in state]
+    arrays = [inner, outer, *state, u, gate, dy, *more]
+    in_specs = [pl.BlockSpec(memory_space=pl.ANY)] * 5
+    in_specs += [fixed(a.shape) for a in arrays[5:]]
     out_shape = [jax.ShapeDtypeStruct((EXPERTS // 2, SLAB, 128), F32)]
     out_specs = [pl.BlockSpec((GROUP, SLAB, 128), lambda i, core: (i, 0, 0))]
     scratch = [
@@ -628,6 +695,12 @@
             pltpu.VMEM((56, WIDTH), F32),
         ]
     scratch += [pltpu.VMEM((HID, rows), F32)] * 2
+    scratch += [
+        pltpu.VMEM((2, WIDTH, GROUP * HID), BF16),
+        pltpu.VMEM((2, GROUP, HID, WIDTH), BF16),
+        *[pltpu.VMEM((2, GROUP, HID, rows), BF16)] * 3,
+        pltpu.SemaphoreType.DMA((5, 2)),
+    ]
     out_shape += added
     out_specs += [fixed(s.shape) for s in added]
     return pl.pallas_call(
@@ -642,7 +715,7 @@
         out_shape=out_shape,
         cost_estimate=pl.CostEstimate(flops=8_000_000_000, bytes_accessed=20_000_000, transcendentals=0),
         compiler_params=pltpu.CompilerParams(
-            dimension_semantics=("arbitrary",), vmem_limit_bytes=40 * MIB
+            dimension_semantics=("arbitrary",), vmem_limit_bytes=(24 if sending else 24) * MIB
         ),
         name="last_send" if sending else "last_keep",
     )(core, *arrays)
@@ -952,6 +1025,13 @@
     )(chip, core, *own, *got, *more)
 
 
+def count_kernel(labels_ref, out_ref):
+    count = jnp.sum(labels_ref[...].astype(F32), axis=1, keepdims=True)
+    lane = lax.broadcasted_iota(jnp.int32, (1, 128), 1)
+    row = jnp.where(lane == 0, count[0:1], jnp.where(lane == 1, count[1:2], 0.0))
+    out_ref[...] = jnp.broadcast_to(row, (128, 128))
+
+
 def on_device(
     tokens,
     labels,
@@ -987,14 +1067,16 @@
         codes_two.T,
         mixing_two.T,
     )
-    count = jnp.sum(labels.astype(F32), axis=0)
-    sent = jnp.broadcast_to(jnp.pad(count, (0, 126))[None, :], (128, 128))
+    labels = labels.T
+    sent = pl.pallas_call(
+        count_kernel, out_shape=jax.ShapeDtypeStruct((128, 128), F32), name="count"
+    )(labels)
     counts = lax.all_to_all(sent, ("chip", "core"), 0, 0, tiled=True)
     *state, gate, code, mix, u, u_two = first_part(
         tokens, codes_one, mixing_one, inner_one, inner_bias_one, outer_one, outer_bias_one
     )
     towers = (tower_inner, tower_inner_bias, tower_outer, tower_outer_bias.reshape(1, TASKS))
-    towers = (labels.T, counts, lengths.reshape(1, -1), base, *towers)
+    towers = (labels, counts, lengths.reshape(1, -1), base, *towers)
     send, keep_two, dy, predictions, small_send, small_keep = main_part(
         core, u_two, codes_two, mixing_two, inner_two, inner_bias_two, outer_two, outer_bias_two, towers
     )

time: 211 us -> 193 us (0.915); the launches traced: 208 us -> 193 us
  local copies, waits for them, and re-layouts: 9.77 us -> 0.1 us
  Pallas kernels: 75.1 us -> 69.8 us
    unnamed x46 -> x36, local copies, waits for them, and re-layouts: 9.1 us -> 0.1 us
    pallas_call x1, Pallas kernels: 35.8 us -> 31.9 us  [main_part(): pl.pallas_call(functools.partial(main_kernel, rows), grid_spec=pltpu.Pref...]
    ppermute x9, starting transfers between devices: 18.4 us -> 20.9 us  [swap(): lax.ppermute(s, ('chip', 'core'), swaps(axes[step % 3], step))]
    pallas_call x26, Pallas kernels: 5 us -> 2.63 us  [plain_call(): pl.pallas_call(kernel, in_specs=[smem, smem] + [vmem] * len(arrays), out_...]
    pallas_call x1 -> x2, Pallas kernels: 12.3 us -> 13.5 us  [the longest x1 12.1 us: first_part(): pl.pallas_call(functools.partial(first_kernel, rows), grid=(ROUNDS,), in_...]
  transfers between devices with their start and end apart: 40 -> 40, of which waited for: 23 -> 23; matrix products, arithmetic and copies ran while one was open for 0% -> 0% of each run, Pallas kernels for 16% -> 17%
where the time goes in v4:
time: 193 us
  Pallas kernels  69.8 us (36%)
  waiting for transfers between devices  63.4 us (33%)
  starting transfers between devices  58.3 us (30%)
    ppermute x21, waiting for transfers between devices, swap_one(): return lax.ppermute(sent, ('chip', 'core'), swaps(AXES[i][step % 3], step))  40.4 us
    pallas_call x1, Pallas kernels, main_part(): pl.pallas_call(functools.partial(main_kernel, rows), grid_spec=pltpu.Pref...  31.9 us
    ppermute x9, waiting for transfers between devices, swap(): lax.ppermute(s, ('chip', 'core'), swaps(axes[step % 3], step))  21 us
    ppermute x9, starting transfers between devices, swap(): lax.ppermute(s, ('chip', 'core'), swaps(axes[step % 3], step))  20.9 us
    ppermute x21, starting transfers between devices, swap_one(): return lax.ppermute(sent, ('chip', 'core'), swaps(AXES[i][step % 3], step))  18.5 us
    pallas_call x2, Pallas kernels, last_part(): pl.pallas_call(functools.partial(last_kernel, sending, rows), grid_spec=p...  13.9 us
    pallas_call x1, Pallas kernels, first_part(): pl.pallas_call(functools.partial(first_kernel, rows), grid=(ROUNDS,), in_...  12.1 us
    all_to_all x1, starting transfers between devices, on_device(): counts = lax.all_to_all(sent, ('chip', 'core'), 0, 0, tiled=True)  11.5 us
  transfers between devices with their start and end apart: 40, of which 23 were waited for; matrix products, arithmetic and copies ran while one was open for 0% of the time, Pallas kernels for 17%

profile of v4, /device:TPU:1, one launch (start us, length us, event | category | flops | bytes accessed | tf_op | source)
XLA Modules:
  0.0 193.0 jit_solution(9676795642227846469)
XLA Ops:
  0.7 1.4 count.1
  2.1 11.5 %all-to-all-start = ((f32[128,1,128]{2,1,0:T(1,128)}), f32[128,1,128]{2,1,0:T(1,128)S(1)}, u32[]{:S(2)}, u32[]{:S(2)}) async-start(f32[128,1,128]{2,1,0:T(1,128)} %bitcast.44), calls=%async_computation | async-start | bytes 131072 | tf_op jit(solution)/shard_map/all_to_all | solution.py:1074
  13.7 12.1 %first_part.1 = (bf16[16,256,512]{2,1,0:T(8,128)(2,1)}, bf16[16,256,512]{2,1,0:T(8,128)(2,1)}, bf16[16,256,512]{2,1,0:T(8,128)(2,1)}, f32[16,1024]{1,0:T(8,128)}...) custom-call(bf16[512,256]{1,0:T(8,128)(2,1)} %tokens_ref.1, ...), custom_call_target="tpu_custom_call" | custom-call | flops 8000000000 | bytes 20000000 | tf_op jit(solution)/shard_map/first_part/pallas_call | solution.py:408
  25.9 31.9 %main_part.1 = (f32[8,1024,128]{2,1,0:T(8,128)}, f32[8,1024,128]{2,1,0:T(8,128)}, f32[256,1024]{1,0:T(8,128)S(1)}, f32[2,512]{1,0:T(2,128)}, f32[336,128]{1,0:T(8,128)S(1)}, /*index=5*/f32[336,128]{1,0:T(8,128)S(1)}) custom-call(s32[1]{0:T(128)} %bitcast.core_ref, bf16[256,1024]{1,0:T(8,128)(2,1)S(1)} %get-tuple-element.88.refs_0_, ...), custom_call_target="tpu_custom_call" | custom-call | flops 14000000000 | bytes 40000000 | tf_op jit(solution)/shard_map/main_part/pallas_call | solution.py:532
  57.8 0.8 collective-permute-start
  58.6 5.8 %last_send.1 = (f32[8,1024,128]{2,1,0:T(8,128)S(1)}, f32[4,4,256]{2,1,0:T(4,128)S(1)}, f32[256,512]{1,0:T(8,128)S(1)}, f32[16,1024]{1,0:T(8,128)S(1)}) custom-call(s32[1]{0:T(128)} %bitcast.core_ref, bf16[256,4096]{1,0:T(8,128)(2,1)} %refs_0_.3, bf16[16,256,256]{2,1,0:T(8,128)(2,1)} %refs_1_.3, bf16[16,256,512]{2,1,0:T(8,128)(2,1)} %get-tuple-element.90.refs_2_, ...), custom_call_target="tpu_custom_call" | custom-call | flops 8000000000 | bytes 20000000 | tf_op jit(solution)/shard_map/last_send/pallas_call | solution.py:706
  64.6 1.0 collective-permute-done
  66.1 3.2 %collective-permute-start.3 = (f32[1536,128]{1,0:T(8,128)S(1)}, f32[1536,128]{1,0:T(8,128)S(1)}, u32[]{:S(2)}, u32[]{:S(2)}) collective-permute-start(f32[1536,128]{1,0:T(8,128)S(1)} %get-tuple-element.106), channel_id=1, source_target_pairs={{0,8},{1,25},{2,10},{3,27},{4,12},{5,29},{6,14},{7,31},{8,0},{9,17... | collective-permute-start | bytes 2359304 | tf_op jit(solution)/shard_map/ppermute | solution.py:748
  69.3 2.4 %collective-permute-start.1 = (f32[1280,128]{1,0:T(8,128)S(1)}, f32[1280,128]{1,0:T(8,128)S(1)}, u32[]{:S(2)}, u32[]{:S(2)}) collective-permute-start(f32[1280,128]{1,0:T(8,128)S(1)} %get-tuple-element.104), channel_id=1, source_target_pairs={{0,2},{1,7},{2,0},{3,5},{4,6},{5,3},{6,4},{7,1},{8,10},{9,15},{10,... | collective-permute-start | bytes 1966088 | tf_op jit(solution)/shard_map/ppermute | solution.py:748
  71.8 2.6 %collective-permute-start.2 = (f32[1280,128]{1,0:T(8,128)S(1)}, f32[1280,128]{1,0:T(8,128)S(1)}, u32[]{:S(2)}, u32[]{:S(2)}) collective-permute-start(f32[1280,128]{1,0:T(8,128)S(1)} %get-tuple-element.105), channel_id=1, source_target_pairs={{0,32},{1,97},{2,34},{3,99},{4,36},{5,101},{6,38},{7,103},{8,40},{... | collective-permute-start | bytes 1966088 | tf_op jit(solution)/shard_map/ppermute | solution.py:748
  74.4 8.0 %last_keep.1 = (f32[8,1024,128]{2,1,0:T(8,128)S(1)}, f32[512,256]{1,0:T(8,128)}, f32[144,128]{1,0:T(8,128)S(1)}) custom-call(s32[1]{0:T(128)} %bitcast.core_ref, bf16[256,4096]{1,0:T(8,128)(2,1)} %refs_0_.3, bf16[16,256,256]{2,1,0:T(8,128)(2,1)} %refs_1_.3, bf16[16,256,512]{2,1,0:T(8,128)(2,1)} %get-tuple-element.90.refs_2_, ...), custom_call_target="tpu_custom_call" | custom-call | flops 8000000000 | bytes 20000000 | tf_op jit(solution)/shard_map/last_keep/pallas_call | solution.py:706
  83.0 2.6 %collective-permute-start.15 = (f32[1536,128]{1,0:T(8,128)S(1)}, f32[1536,128]{1,0:T(8,128)S(1)}, u32[]{:S(2)}, u32[]{:S(2)}) collective-permute-start(f32[1536,128]{1,0:T(8,128)S(1)} %get-tuple-element.123), channel_id=1, source_target_pairs={{0,32},{1,97},{2,34},{3,99},{4,36},{5,101},{6,38},{7,103},{8,40},{... | collective-permute-start | bytes 2359304 | tf_op jit(solution)/shard_map/ppermute | solution.py:748
  85.9 1.2 collective-permute-start.24
  87.0 9.5 %collective-permute-done.24.got_one = f32[1280,128]{1,0:T(8,128)S(1)} collective-permute-done((f32[1280,128]{1,0:T(8,128)S(1)}, f32[1280,128]{1,0:T(8,128)S(1)}, u32[]{:S(2)}, u32[]{:S(2)}) %collective-permute-start.24) | collective-permute-done | bytes 655392 | tf_op jit(solution)/shard_map/ppermute | solution.py:748
  96.7 2.5 %collective-permute-start.25 = (f32[1408,128]{1,0:T(8,128)S(1)}, f32[1408,128]{1,0:T(8,128)S(1)}, u32[]{:S(2)}, u32[]{:S(2)}) collective-permute-start(f32[1408,128]{1,0:T(8,128)S(1)} %get-tuple-element.134), channel_id=1, source_target_pairs={{0,2},{1,7},{2,0},{3,5},{4,6},{5,3},{6,4},{7,1},{8,10},{9,15},{10,... | collective-permute-start | bytes 2162696 | tf_op jit(solution)/shard_map/ppermute | solution.py:837
  99.4 0.8 collective-permute-start.16
  100.6 7.5 %collective-permute-done.25.got_ref = f32[1408,128]{1,0:T(8,128)S(1)} collective-permute-done((f32[1408,128]{1,0:T(8,128)S(1)}, f32[1408,128]{1,0:T(8,128)S(1)}, u32[]{:S(2)}, u32[]{:S(2)}) %collective-permute-start.25) | collective-permute-done | bytes 720928 | tf_op jit(solution)/shard_map/ppermute | solution.py:837
  108.4 2.4 %collective-permute-done.16.got_ref = f32[1408,128]{1,0:T(8,128)S(1)} collective-permute-done((f32[1408,128]{1,0:T(8,128)S(1)}, f32[1408,128]{1,0:T(8,128)S(1)}, u32[]{:S(2)}, u32[]{:S(2)}) %collective-permute-start.16) | collective-permute-done | bytes 720928 | tf_op jit(solution)/shard_map/ppermute | solution.py:837
  111.2 0.6 collective-permute-done.7.got_ref
  111.9 2.0 %collective-permute-start.8 = (f32[704,128]{1,0:T(8,128)S(1)}, f32[704,128]{1,0:T(8,128)S(1)}, u32[]{:S(2)}, u32[]{:S(2)}) collective-permute-start(f32[704,128]{1,0:T(8,128)S(1)} %get-tuple-element.120), channel_id=1, source_target_pairs={{0,8},{1,25},{2,10},{3,27},{4,12},{5,29},{6,14},{7,31},{8,0},{9,17... | collective-permute-start | bytes 1081352 | tf_op jit(solution)/shard_map/ppermute | solution.py:837
  113.9 1.9 collective-permute-done.26.got_ref
  115.9 2.6 %collective-permute-done.17.got_ref = f32[704,128]{1,0:T(8,128)S(1)} collective-permute-done((f32[704,128]{1,0:T(8,128)S(1)}, f32[704,128]{1,0:T(8,128)S(1)}, u32[]{:S(2)}, u32[]{:S(2)}) %collective-permute-start.17) | collective-permute-done | bytes 360480 | tf_op jit(solution)/shard_map/ppermute | solution.py:837
  118.6 2.0 %collective-permute-done.8.got_ref = f32[704,128]{1,0:T(8,128)S(1)} collective-permute-done((f32[704,128]{1,0:T(8,128)S(1)}, f32[704,128]{1,0:T(8,128)S(1)}, u32[]{:S(2)}, u32[]{:S(2)}) %collective-permute-start.8) | collective-permute-done | bytes 360480 | tf_op jit(solution)/shard_map/ppermute | solution.py:837
  120.8 1.7 collective-permute-done.27.got_ref
  122.6 2.6 %collective-permute-done.18.got_ref = f32[704,128]{1,0:T(8,128)S(1)} collective-permute-done((f32[704,128]{1,0:T(8,128)S(1)}, f32[704,128]{1,0:T(8,128)S(1)}, u32[]{:S(2)}, u32[]{:S(2)}) %collective-permute-start.18) | collective-permute-done | bytes 360480 | tf_op jit(solution)/shard_map/ppermute | solution.py:837
  125.3 1.7 collective-permute-done.9.got_ref
  127.2 4.0 %collective-permute-done.28.got_ref = f32[704,128]{1,0:T(8,128)S(1)} collective-permute-done((f32[704,128]{1,0:T(8,128)S(1)}, f32[704,128]{1,0:T(8,128)S(1)}, u32[]{:S(2)}, u32[]{:S(2)}) %collective-permute-start.28) | collective-permute-done | bytes 360480 | tf_op jit(solution)/shard_map/ppermute | solution.py:837
  132.0 1.7 collective-permute-done.10.got_ref
  133.8 4.0 %collective-permute-done.29.got_ref = f32[704,128]{1,0:T(8,128)S(1)} collective-permute-done((f32[704,128]{1,0:T(8,128)S(1)}, f32[704,128]{1,0:T(8,128)S(1)}, u32[]{:S(2)}, u32[]{:S(2)}) %collective-permute-start.29) | collective-permute-done | bytes 360480 | tf_op jit(solution)/shard_map/ppermute | solution.py:837
  137.9 1.8 collective-permute-start.30
  139.8 0.6 collective-permute-done.11.got_ref
  140.4 3.8 %collective-permute-start.12 = (f32[704,128]{1,0:T(8,128)S(1)}, f32[704,128]{1,0:T(8,128)S(1)}, u32[]{:S(2)}, u32[]{:S(2)}) collective-permute-start(f32[704,128]{1,0:T(8,128)S(1)} %pair_x5.1.own_ref), channel_id=1, source_target_pairs={{0,8},{1,25},{2,10},{3,27},{4,12},{5,29},{6,14},{7,31},{8,0},{9,17... | collective-permute-start | bytes 1081352 | tf_op jit(solution)/shard_map/ppermute | solution.py:837
  144.2 1.2 collective-permute-done.30.got_ref
  145.5 1.2 collective-permute-start.31
  146.7 0.6 collective-permute-done.21.got_ref
  147.3 2.1 %collective-permute-start.22 = (f32[1408,128]{1,0:T(8,128)S(1)}, f32[1408,128]{1,0:T(8,128)S(1)}, u32[]{:S(2)}, u32[]{:S(2)}) collective-permute-start(f32[1408,128]{1,0:T(8,128)S(1)} %double_y2.1.own_ref), channel_id=1, source_target_pairs={{0,8},{1,25},{2,10},{3,27},{4,12},{5,29},{6,14},{7,31},{8,0},{9,17... | collective-permute-start | bytes 2162696 | tf_op jit(solution)/shard_map/ppermute | solution.py:837
  149.5 2.7 %collective-permute-start.13 = (f32[1408,128]{1,0:T(8,128)S(1)}, f32[1408,128]{1,0:T(8,128)S(1)}, u32[]{:S(2)}, u32[]{:S(2)}) collective-permute-start(f32[1408,128]{1,0:T(8,128)S(1)} %double_x2.1.own_ref), channel_id=1, source_target_pairs={{0,32},{1,97},{2,34},{3,99},{4,36},{5,101},{6,38},{7,103},{8,40},{... | collective-permute-start | bytes 2162696 | tf_op jit(solution)/shard_map/ppermute | solution.py:837
  152.2 4.7 %collective-permute-done.31.got_ref = f32[1408,128]{1,0:T(8,128)S(1)} collective-permute-done((f32[1408,128]{1,0:T(8,128)S(1)}, f32[1408,128]{1,0:T(8,128)S(1)}, u32[]{:S(2)}, u32[]{:S(2)}) %collective-permute-start.31) | collective-permute-done | bytes 720928 | tf_op jit(solution)/shard_map/ppermute | solution.py:837
  157.1 3.5 %collective-permute-start.37 = (f32[2816,128]{1,0:T(8,128)S(1)}, f32[2816,128]{1,0:T(8,128)S(1)}, u32[]{:S(2)}, u32[]{:S(2)}) collective-permute-start(f32[2816,128]{1,0:T(8,128)S(1)} %double_z1.1.refs_2_), channel_id=1, source_target_pairs={{0,8},{1,25},{2,10},{3,27},{4,12},{5,29},{6,14},{7,31},{8,0},{9,17... | collective-permute-start | bytes 4325384 | tf_op jit(solution)/shard_map/ppermute | solution.py:748
  160.9 2.2 %collective-permute-start.35 = (f32[2816,128]{1,0:T(8,128)S(1)}, f32[2816,128]{1,0:T(8,128)S(1)}, u32[]{:S(2)}, u32[]{:S(2)}) collective-permute-start(f32[2816,128]{1,0:T(8,128)S(1)} %double_y1.1.refs_1_), channel_id=1, source_target_pairs={{0,32},{1,97},{2,34},{3,99},{4,36},{5,101},{6,38},{7,103},{8,40},{... | collective-permute-start | bytes 4325384 | tf_op jit(solution)/shard_map/ppermute | solution.py:748
  163.2 2.9 %collective-permute-start.33 = (f32[2816,128]{1,0:T(8,128)S(1)}, f32[2816,128]{1,0:T(8,128)S(1)}, u32[]{:S(2)}, u32[]{:S(2)}) collective-permute-start(f32[2816,128]{1,0:T(8,128)S(1)} %double_x1.1.refs_0_), channel_id=1, source_target_pairs={{0,2},{1,7},{2,0},{3,5},{4,6},{5,3},{6,4},{7,1},{8,10},{9,15},{10,... | collective-permute-start | bytes 4325384 | tf_op jit(solution)/shard_map/ppermute | solution.py:748
  166.1 10.9 %collective-permute-done.37.refs_5_ = f32[2816,128]{1,0:T(8,128)S(1)} collective-permute-done((f32[2816,128]{1,0:T(8,128)S(1)}, f32[2816,128]{1,0:T(8,128)S(1)}, u32[]{:S(2)}, u32[]{:S(2)}) %collective-permute-start.37) | collective-permute-done | bytes 1441824 | tf_op jit(solution)/shard_map/ppermute | solution.py:748
  177.0 2.7 %collective-permute-start.14 = (f32[2816,128]{1,0:T(8,128)S(1)}, f32[2816,128]{1,0:T(8,128)S(1)}, u32[]{:S(2)}, u32[]{:S(2)}) collective-permute-start(f32[2816,128]{1,0:T(8,128)S(1)} %double_x1.1.refs_0_), channel_id=1, source_target_pairs={{0,1},{1,0},{2,3},{3,2},{4,5},{5,4},{6,7},{7,6},{8,9},{9,8},{10,11... | collective-permute-start | bytes 4325384 | tf_op jit(solution)/shard_map/ppermute | solution.py:1062
  180.0 2.2 %collective-permute-start.36 = (f32[2816,128]{1,0:T(8,128)S(1)}, f32[2816,128]{1,0:T(8,128)S(1)}, u32[]{:S(2)}, u32[]{:S(2)}) collective-permute-start(f32[2816,128]{1,0:T(8,128)S(1)} %collective-permute-done.35.refs_4_), channel_id=1, source_target_pairs={{0,1},{1,0},{2,3},{3,2},{4,5},{5,4},{6,7},{7,6},{8,9},{9,8},{10,11... | collective-permute-start | bytes 4325384 | tf_op jit(solution)/shard_map/ppermute | solution.py:1062
  182.5 1.4 collective-permute-start.34
  183.9 3.9 %lay_own.1 = (f32[256,4096]{1,0:T(8,128)}, f32[16,256,256]{2,1,0:T(8,128)}, f32[256,4096]{1,0:T(8,128)}, f32[16,256,256]{2,1,0:T(8,128)}, f32[512,128]{1,0:T(8,128)S(1)}) custom-call(s32[1]{0:T(128)} %bitcast.15.chip_ref, s32[1]{0:T(128)} %bitcast.core_ref, f32[2816,128]{1,0:T(8,128)S(1)} %double_x1.1.refs_0_, f32[2816,128]{1,0:T(8,128)S(1)} %double_y1.1.refs_1_, ...), custom_call_target="tpu_custom_call" | custom-call | bytes 16000000 | tf_op jit(solution)/shard_map/lay_own/pallas_call | solution.py:1009
  187.8 0.9 collective-permute-done.34.refs_3_
  188.7 4.1 %lay_other.1 = (f32[256,4096]{1,0:T(8,128)}, f32[16,256,256]{2,1,0:T(8,128)}, f32[256,4096]{1,0:T(8,128)}, f32[16,256,256]{2,1,0:T(8,128)}, f32[32,256]{1,0:T(8,...) custom-call(s32[1]{0:T(128)} %bitcast.15.chip_ref, ...), custom_call_target="tpu_custom_call", output_to_operand_aliasing={{0}: (9, {}), {1}: (10, {}), {2}: (11, {}), {3}: (12, {})} | custom-call | bytes 16000000 | tf_op jit(solution)/shard_map/lay_other/pallas_call | solution.py:1009
  (101 shorter events, 6.1 us)
Async XLA Ops:
  2.1 23.7 %all-to-all-start = ((f32[128,1,128]{2,1,0:T(1,128)}), f32[128,1,128]{2,1,0:T(1,128)S(1)}, u32[]{:S(2)}, u32[]{:S(2)}) async-start(f32[128,1,128]{2,1,0:T(1,128)} %bitcast.44), calls=%async_computation | async-start | bytes 131072 | tf_op jit(solution)/shard_map/all_to_all | solution.py:1074
  13.6 12.2 %copy-start.1 = (s32[512,2]{0,1:T(2,128)S(1)}, s32[512,2]{0,1:T(2,128)}, u32[]{:S(2)}) copy-start(s32[512,2]{0,1:T(2,128)} %param.20) | copy-start | bytes 12292
  13.6 12.2 %copy-start.2 = (bf16[2,256,128]{2,1,0:T(8,128)(2,1)S(1)}, bf16[2,256,128]{2,1,0:T(8,128)(2,1)}, u32[]{:S(2)}) copy-start(bf16[2,256,128]{2,1,0:T(8,128)(2,1)} %refs_13_.1) | copy-start | bytes 393220
  13.6 12.2 %copy-start.3 = (bf16[256,32]{0,1:T(8,128)(2,1)S(1)}, bf16[256,32]{0,1:T(8,128)(2,1)}, u32[]{:S(2)}) copy-start(bf16[256,32]{0,1:T(8,128)(2,1)} %param.28) | copy-start | bytes 49156
  13.6 12.2 %copy-start.5 = (bf16[4096]{0:T(1024)(128)(2,1)S(1)}, bf16[4096]{0:T(1024)(128)(2,1)}, u32[]{:S(2)}) copy-start(bf16[4096]{0:T(1024)(128)(2,1)} %param.31) | copy-start | bytes 24580
  13.6 12.2 %copy-start.6 = (bf16[16,256]{1,0:T(8,128)(2,1)S(1)}, bf16[16,256]{1,0:T(8,128)(2,1)}, u32[]{:S(2)}) copy-start(bf16[16,256]{1,0:T(8,128)(2,1)} %refs_6_.1) | copy-start | bytes 24580
  13.6 12.2 %copy-start.8 = (bf16[256,8]{0,1:T(8,128)(2,1)S(1)}, bf16[256,8]{0,1:T(8,128)(2,1)}, u32[]{:S(2)}) copy-start(bf16[256,8]{0,1:T(8,128)(2,1)} %param.29) | copy-start | bytes 12292
  25.9 32.8 %copy-start.14 = (bf16[256,512]{1,0:T(8,128)(2,1)S(1)}, bf16[256,512]{1,0:T(8,128)(2,1)}, u32[]{:S(2)}) copy-start(bf16[256,512]{1,0:T(8,128)(2,1)} %get-tuple-element.93.refs_5_) | copy-start | bytes 786436
  25.9 32.7 %copy-start.15 = (f32[16,1024]{1,0:T(8,128)S(1)}, f32[16,1024]{1,0:T(8,128)}, u32[]{:S(2)}) copy-start(f32[16,1024]{1,0:T(8,128)} %get-tuple-element.94.refs_6_) | copy-start | bytes 196612
  57.8 7.8 %collective-permute-start = (f32[8,1024,128]{2,1,0:T(8,128)}, f32[8,1024,128]{2,1,0:T(8,128)S(1)}, u32[]{:S(2)}, u32[]{:S(2)}) collective-permute-start(f32[8,1024,128]{2,1,0:T(8,128)} %get-tuple-element.103), channel_id=1, source_target_pairs={{0,1},{1,0},{2,3},{3,2},{4,5},{5,4},{6,7},{7,6},{8,9},{9,8},{10,11... | collective-permute-start | bytes 12582920 | tf_op jit(solution)/shard_map/ppermute | solution.py:1062
  64.5 18.0 %collective-permute-start.4 = (f32[8,1024,128]{2,1,0:T(8,128)S(1)}, f32[8,1024,128]{2,1,0:T(8,128)S(1)}, u32[]{:S(2)}, u32[]{:S(2)}) collective-permute-start(f32[8,1024,128]{2,1,0:T(8,128)S(1)} %get-tuple-element.109), channel_id=1, source_target_pairs={{0,1},{1,0},{2,3},{3,2},{4,5},{5,4},{6,7},{7,6},{8,9},{9,8},{10,11... | collective-permute-start | bytes 12582920 | tf_op jit(solution)/shard_map/ppermute | solution.py:1062
  66.1 16.4 %collective-permute-start.3 = (f32[1536,128]{1,0:T(8,128)S(1)}, f32[1536,128]{1,0:T(8,128)S(1)}, u32[]{:S(2)}, u32[]{:S(2)}) collective-permute-start(f32[1536,128]{1,0:T(8,128)S(1)} %get-tuple-element.106), channel_id=1, source_target_pairs={{0,8},{1,25},{2,10},{3,27},{4,12},{5,29},{6,14},{7,31},{8,0},{9,17... | collective-permute-start | bytes 2359304 | tf_op jit(solution)/shard_map/ppermute | solution.py:748
  69.3 13.2 %collective-permute-start.5 = (f32[336,128]{1,0:T(8,128)S(1)}, f32[336,128]{1,0:T(8,128)S(1)}, u32[]{:S(2)}, u32[]{:S(2)}) collective-permute-start(f32[336,128]{1,0:T(8,128)S(1)} %get-tuple-element.111), channel_id=1, source_target_pairs={{0,1},{1,0},{2,3},{3,2},{4,5},{5,4},{6,7},{7,6},{8,9},{9,8},{10,11... | collective-permute-start | bytes 516104 | tf_op jit(solution)/shard_map/ppermute | solution.py:1062
  69.3 13.1 %collective-permute-start.1 = (f32[1280,128]{1,0:T(8,128)S(1)}, f32[1280,128]{1,0:T(8,128)S(1)}, u32[]{:S(2)}, u32[]{:S(2)}) collective-permute-start(f32[1280,128]{1,0:T(8,128)S(1)} %get-tuple-element.104), channel_id=1, source_target_pairs={{0,2},{1,7},{2,0},{3,5},{4,6},{5,3},{6,4},{7,1},{8,10},{9,15},{10,... | collective-permute-start | bytes 1966088 | tf_op jit(solution)/shard_map/ppermute | solution.py:748
  71.8 10.7 %collective-permute-start.2 = (f32[1280,128]{1,0:T(8,128)S(1)}, f32[1280,128]{1,0:T(8,128)S(1)}, u32[]{:S(2)}, u32[]{:S(2)}) collective-permute-start(f32[1280,128]{1,0:T(8,128)S(1)} %get-tuple-element.105), channel_id=1, source_target_pairs={{0,32},{1,97},{2,34},{3,99},{4,36},{5,101},{6,38},{7,103},{8,40},{... | collective-permute-start | bytes 1966088 | tf_op jit(solution)/shard_map/ppermute | solution.py:748
  83.0 16.2 %collective-permute-start.15 = (f32[1536,128]{1,0:T(8,128)S(1)}, f32[1536,128]{1,0:T(8,128)S(1)}, u32[]{:S(2)}, u32[]{:S(2)}) collective-permute-start(f32[1536,128]{1,0:T(8,128)S(1)} %get-tuple-element.123), channel_id=1, source_target_pairs={{0,32},{1,97},{2,34},{3,99},{4,36},{5,101},{6,38},{7,103},{8,40},{... | collective-permute-start | bytes 2359304 | tf_op jit(solution)/shard_map/ppermute | solution.py:748
  85.6 14.6 %collective-permute-start.6 = (f32[1536,128]{1,0:T(8,128)S(1)}, f32[1536,128]{1,0:T(8,128)S(1)}, u32[]{:S(2)}, u32[]{:S(2)}) collective-permute-start(f32[1536,128]{1,0:T(8,128)S(1)} %get-tuple-element.115), channel_id=1, source_target_pairs={{0,2},{1,7},{2,0},{3,5},{4,6},{5,3},{6,4},{7,1},{8,10},{9,15},{10,... | collective-permute-start | bytes 2359304 | tf_op jit(solution)/shard_map/ppermute | solution.py:748
  85.9 10.6 %collective-permute-start.24 = (f32[1280,128]{1,0:T(8,128)S(1)}, f32[1280,128]{1,0:T(8,128)S(1)}, u32[]{:S(2)}, u32[]{:S(2)}) collective-permute-start(f32[1280,128]{1,0:T(8,128)S(1)} %get-tuple-element.131), channel_id=1, source_target_pairs={{0,8},{1,25},{2,10},{3,27},{4,12},{5,29},{6,14},{7,31},{8,0},{9,17... | collective-permute-start | bytes 1966088 | tf_op jit(solution)/shard_map/ppermute | solution.py:748
  96.7 11.4 %collective-permute-start.25 = (f32[1408,128]{1,0:T(8,128)S(1)}, f32[1408,128]{1,0:T(8,128)S(1)}, u32[]{:S(2)}, u32[]{:S(2)}) collective-permute-start(f32[1408,128]{1,0:T(8,128)S(1)} %get-tuple-element.134), channel_id=1, source_target_pairs={{0,2},{1,7},{2,0},{3,5},{4,6},{5,3},{6,4},{7,1},{8,10},{9,15},{10,... | collective-permute-start | bytes 2162696 | tf_op jit(solution)/shard_map/ppermute | solution.py:837
  99.4 11.4 %collective-permute-start.16 = (f32[1408,128]{1,0:T(8,128)S(1)}, f32[1408,128]{1,0:T(8,128)S(1)}, u32[]{:S(2)}, u32[]{:S(2)}) collective-permute-start(f32[1408,128]{1,0:T(8,128)S(1)} %get-tuple-element.126), channel_id=1, source_target_pairs={{0,8},{1,25},{2,10},{3,27},{4,12},{5,29},{6,14},{7,31},{8,0},{9,17... | collective-permute-start | bytes 2162696 | tf_op jit(solution)/shard_map/ppermute | solution.py:837
  100.4 11.4 %collective-permute-start.7 = (f32[1408,128]{1,0:T(8,128)S(1)}, f32[1408,128]{1,0:T(8,128)S(1)}, u32[]{:S(2)}, u32[]{:S(2)}) collective-permute-start(f32[1408,128]{1,0:T(8,128)S(1)} %get-tuple-element.118), channel_id=1, source_target_pairs={{0,32},{1,97},{2,34},{3,99},{4,36},{5,101},{6,38},{7,103},{8,40},{... | collective-permute-start | bytes 2162696 | tf_op jit(solution)/shard_map/ppermute | solution.py:837
  108.2 7.6 %collective-permute-start.26 = (f32[704,128]{1,0:T(8,128)S(1)}, f32[704,128]{1,0:T(8,128)S(1)}, u32[]{:S(2)}, u32[]{:S(2)}) collective-permute-start(f32[704,128]{1,0:T(8,128)S(1)} %get-tuple-element.136), channel_id=1, source_target_pairs={{0,32},{1,97},{2,34},{3,99},{4,36},{5,101},{6,38},{7,103},{8,40},{... | collective-permute-start | bytes 1081352 | tf_op jit(solution)/shard_map/ppermute | solution.py:837
  110.9 7.6 %collective-permute-start.17 = (f32[704,128]{1,0:T(8,128)S(1)}, f32[704,128]{1,0:T(8,128)S(1)}, u32[]{:S(2)}, u32[]{:S(2)}) collective-permute-start(f32[704,128]{1,0:T(8,128)S(1)} %get-tuple-element.128), channel_id=1, source_target_pairs={{0,2},{1,7},{2,0},{3,5},{4,6},{5,3},{6,4},{7,1},{8,10},{9,15},{10,... | collective-permute-start | bytes 1081352 | tf_op jit(solution)/shard_map/ppermute | solution.py:837
  111.9 8.8 %collective-permute-start.8 = (f32[704,128]{1,0:T(8,128)S(1)}, f32[704,128]{1,0:T(8,128)S(1)}, u32[]{:S(2)}, u32[]{:S(2)}) collective-permute-start(f32[704,128]{1,0:T(8,128)S(1)} %get-tuple-element.120), channel_id=1, source_target_pairs={{0,8},{1,25},{2,10},{3,27},{4,12},{5,29},{6,14},{7,31},{8,0},{9,17... | collective-permute-start | bytes 1081352 | tf_op jit(solution)/shard_map/ppermute | solution.py:837
  115.8 6.7 %collective-permute-start.27 = (f32[704,128]{1,0:T(8,128)S(1)}, f32[704,128]{1,0:T(8,128)S(1)}, u32[]{:S(2)}, u32[]{:S(2)}) collective-permute-start(f32[704,128]{1,0:T(8,128)S(1)} %close_z.1.own_ref), channel_id=1, source_target_pairs={{0,24},{1,9},{2,26},{3,11},{4,28},{5,13},{6,30},{7,15},{8,16},{9,1... | collective-permute-start | bytes 1081352 | tf_op jit(solution)/shard_map/ppermute | solution.py:837
  118.5 6.7 %collective-permute-start.18 = (f32[704,128]{1,0:T(8,128)S(1)}, f32[704,128]{1,0:T(8,128)S(1)}, u32[]{:S(2)}, u32[]{:S(2)}) collective-permute-start(f32[704,128]{1,0:T(8,128)S(1)} %close_y.1.own_ref), channel_id=1, source_target_pairs={{0,96},{1,33},{2,98},{3,35},{4,100},{5,37},{6,102},{7,39},{8,104},... | collective-permute-start | bytes 1081352 | tf_op jit(solution)/shard_map/ppermute | solution.py:837
  120.7 6.4 %collective-permute-start.9 = (f32[704,128]{1,0:T(8,128)S(1)}, f32[704,128]{1,0:T(8,128)S(1)}, u32[]{:S(2)}, u32[]{:S(2)}) collective-permute-start(f32[704,128]{1,0:T(8,128)S(1)} %close_x.1.own_ref), channel_id=1, source_target_pairs={{0,6},{1,3},{2,4},{3,1},{4,2},{5,7},{6,0},{7,5},{8,14},{9,11},{10,... | collective-permute-start | bytes 1081352 | tf_op jit(solution)/shard_map/ppermute | solution.py:837
  122.5 8.7 %collective-permute-start.28 = (f32[704,128]{1,0:T(8,128)S(1)}, f32[704,128]{1,0:T(8,128)S(1)}, u32[]{:S(2)}, u32[]{:S(2)}) collective-permute-start(f32[704,128]{1,0:T(8,128)S(1)} %pair_z3.1.own_ref), channel_id=1, source_target_pairs={{0,6},{1,3},{2,4},{3,1},{4,2},{5,7},{6,0},{7,5},{8,14},{9,11},{10,... | collective-permute-start | bytes 1081352 | tf_op jit(solution)/shard_map/ppermute | solution.py:837
  125.2 6.7 %collective-permute-start.19 = (f32[704,128]{1,0:T(8,128)S(1)}, f32[704,128]{1,0:T(8,128)S(1)}, u32[]{:S(2)}, u32[]{:S(2)}) collective-permute-start(f32[704,128]{1,0:T(8,128)S(1)} %pair_y3.1.own_ref), channel_id=1, source_target_pairs={{0,24},{1,9},{2,26},{3,11},{4,28},{5,13},{6,30},{7,15},{8,16},{9,1... | collective-permute-start | bytes 1081352 | tf_op jit(solution)/shard_map/ppermute | solution.py:837
  127.1 6.7 %collective-permute-start.10 = (f32[704,128]{1,0:T(8,128)S(1)}, f32[704,128]{1,0:T(8,128)S(1)}, u32[]{:S(2)}, u32[]{:S(2)}) collective-permute-start(f32[704,128]{1,0:T(8,128)S(1)} %pair_x3.1.own_ref), channel_id=1, source_target_pairs={{0,96},{1,33},{2,98},{3,35},{4,100},{5,37},{6,102},{7,39},{8,104},... | collective-permute-start | bytes 1081352 | tf_op jit(solution)/shard_map/ppermute | solution.py:837
  131.2 6.7 %collective-permute-start.29 = (f32[704,128]{1,0:T(8,128)S(1)}, f32[704,128]{1,0:T(8,128)S(1)}, u32[]{:S(2)}, u32[]{:S(2)}) collective-permute-start(f32[704,128]{1,0:T(8,128)S(1)} %pair_z4.1.own_ref), channel_id=1, source_target_pairs={{0,96},{1,33},{2,98},{3,35},{4,100},{5,37},{6,102},{7,39},{8,104},... | collective-permute-start | bytes 1081352 | tf_op jit(solution)/shard_map/ppermute | solution.py:837
  131.9 7.8 %collective-permute-start.20 = (f32[704,128]{1,0:T(8,128)S(1)}, f32[704,128]{1,0:T(8,128)S(1)}, u32[]{:S(2)}, u32[]{:S(2)}) collective-permute-start(f32[704,128]{1,0:T(8,128)S(1)} %pair_y4.1.own_ref), channel_id=1, source_target_pairs={{0,6},{1,3},{2,4},{3,1},{4,2},{5,7},{6,0},{7,5},{8,14},{9,11},{10,... | collective-permute-start | bytes 1081352 | tf_op jit(solution)/shard_map/ppermute | solution.py:837
  133.8 6.7 %collective-permute-start.11 = (f32[704,128]{1,0:T(8,128)S(1)}, f32[704,128]{1,0:T(8,128)S(1)}, u32[]{:S(2)}, u32[]{:S(2)}) collective-permute-start(f32[704,128]{1,0:T(8,128)S(1)} %pair_x4.1.own_ref), channel_id=1, source_target_pairs={{0,24},{1,9},{2,26},{3,11},{4,28},{5,13},{6,30},{7,15},{8,16},{9,1... | collective-permute-start | bytes 1081352 | tf_op jit(solution)/shard_map/ppermute | solution.py:837
  137.9 7.6 %collective-permute-start.30 = (f32[704,128]{1,0:T(8,128)S(1)}, f32[704,128]{1,0:T(8,128)S(1)}, u32[]{:S(2)}, u32[]{:S(2)}) collective-permute-start(f32[704,128]{1,0:T(8,128)S(1)} %pair_z5.1.own_ref), channel_id=1, source_target_pairs={{0,32},{1,97},{2,34},{3,99},{4,36},{5,101},{6,38},{7,103},{8,40},{... | collective-permute-start | bytes 1081352 | tf_op jit(solution)/shard_map/ppermute | solution.py:837
  139.7 7.6 %collective-permute-start.21 = (f32[704,128]{1,0:T(8,128)S(1)}, f32[704,128]{1,0:T(8,128)S(1)}, u32[]{:S(2)}, u32[]{:S(2)}) collective-permute-start(f32[704,128]{1,0:T(8,128)S(1)} %pair_y5.1.own_ref), channel_id=1, source_target_pairs={{0,2},{1,7},{2,0},{3,5},{4,6},{5,3},{6,4},{7,1},{8,10},{9,15},{10,... | collective-permute-start | bytes 1081352 | tf_op jit(solution)/shard_map/ppermute | solution.py:837
  140.4 9.0 %collective-permute-start.12 = (f32[704,128]{1,0:T(8,128)S(1)}, f32[704,128]{1,0:T(8,128)S(1)}, u32[]{:S(2)}, u32[]{:S(2)}) collective-permute-start(f32[704,128]{1,0:T(8,128)S(1)} %pair_x5.1.own_ref), channel_id=1, source_target_pairs={{0,8},{1,25},{2,10},{3,27},{4,12},{5,29},{6,14},{7,31},{8,0},{9,17... | collective-permute-start | bytes 1081352 | tf_op jit(solution)/shard_map/ppermute | solution.py:837
  145.5 11.4 %collective-permute-start.31 = (f32[1408,128]{1,0:T(8,128)S(1)}, f32[1408,128]{1,0:T(8,128)S(1)}, u32[]{:S(2)}, u32[]{:S(2)}) collective-permute-start(f32[1408,128]{1,0:T(8,128)S(1)} %double_z2.1.own_ref), channel_id=1, source_target_pairs={{0,2},{1,7},{2,0},{3,5},{4,6},{5,3},{6,4},{7,1},{8,10},{9,15},{10,... | collective-permute-start | bytes 2162696 | tf_op jit(solution)/shard_map/ppermute | solution.py:837
  147.3 13.4 %collective-permute-start.22 = (f32[1408,128]{1,0:T(8,128)S(1)}, f32[1408,128]{1,0:T(8,128)S(1)}, u32[]{:S(2)}, u32[]{:S(2)}) collective-permute-start(f32[1408,128]{1,0:T(8,128)S(1)} %double_y2.1.own_ref), channel_id=1, source_target_pairs={{0,8},{1,25},{2,10},{3,27},{4,12},{5,29},{6,14},{7,31},{8,0},{9,17... | collective-permute-start | bytes 2162696 | tf_op jit(solution)/shard_map/ppermute | solution.py:837
  149.5 13.6 %collective-permute-start.13 = (f32[1408,128]{1,0:T(8,128)S(1)}, f32[1408,128]{1,0:T(8,128)S(1)}, u32[]{:S(2)}, u32[]{:S(2)}) collective-permute-start(f32[1408,128]{1,0:T(8,128)S(1)} %double_x2.1.own_ref), channel_id=1, source_target_pairs={{0,32},{1,97},{2,34},{3,99},{4,36},{5,101},{6,38},{7,103},{8,40},{... | collective-permute-start | bytes 2162696 | tf_op jit(solution)/shard_map/ppermute | solution.py:837
  157.1 19.9 %collective-permute-start.37 = (f32[2816,128]{1,0:T(8,128)S(1)}, f32[2816,128]{1,0:T(8,128)S(1)}, u32[]{:S(2)}, u32[]{:S(2)}) collective-permute-start(f32[2816,128]{1,0:T(8,128)S(1)} %double_z1.1.refs_2_), channel_id=1, source_target_pairs={{0,8},{1,25},{2,10},{3,27},{4,12},{5,29},{6,14},{7,31},{8,0},{9,17... | collective-permute-start | bytes 4325384 | tf_op jit(solution)/shard_map/ppermute | solution.py:748
  160.6 19.1 %collective-permute-start.32 = (f32[2816,128]{1,0:T(8,128)S(1)}, f32[2816,128]{1,0:T(8,128)S(1)}, u32[]{:S(2)}, u32[]{:S(2)}) collective-permute-start(f32[2816,128]{1,0:T(8,128)S(1)} %double_z1.1.refs_2_), channel_id=1, source_target_pairs={{0,1},{1,0},{2,3},{3,2},{4,5},{5,4},{6,7},{7,6},{8,9},{9,8},{10,11... | collective-permute-start | bytes 4325384 | tf_op jit(solution)/shard_map/ppermute | solution.py:1062
  160.9 19.2 %collective-permute-start.35 = (f32[2816,128]{1,0:T(8,128)S(1)}, f32[2816,128]{1,0:T(8,128)S(1)}, u32[]{:S(2)}, u32[]{:S(2)}) collective-permute-start(f32[2816,128]{1,0:T(8,128)S(1)} %double_y1.1.refs_1_), channel_id=1, source_target_pairs={{0,32},{1,97},{2,34},{3,99},{4,36},{5,101},{6,38},{7,103},{8,40},{... | collective-permute-start | bytes 4325384 | tf_op jit(solution)/shard_map/ppermute | solution.py:748
  163.2 19.3 %collective-permute-start.33 = (f32[2816,128]{1,0:T(8,128)S(1)}, f32[2816,128]{1,0:T(8,128)S(1)}, u32[]{:S(2)}, u32[]{:S(2)}) collective-permute-start(f32[2816,128]{1,0:T(8,128)S(1)} %double_x1.1.refs_0_), channel_id=1, source_target_pairs={{0,2},{1,7},{2,0},{3,5},{4,6},{5,3},{6,4},{7,1},{8,10},{9,15},{10,... | collective-permute-start | bytes 4325384 | tf_op jit(solution)/shard_map/ppermute | solution.py:748
  166.1 21.6 %collective-permute-start.23 = (f32[2816,128]{1,0:T(8,128)S(1)}, f32[2816,128]{1,0:T(8,128)S(1)}, u32[]{:S(2)}, u32[]{:S(2)}) collective-permute-start(f32[2816,128]{1,0:T(8,128)S(1)} %double_y1.1.refs_1_), channel_id=1, source_target_pairs={{0,1},{1,0},{2,3},{3,2},{4,5},{5,4},{6,7},{7,6},{8,9},{9,8},{10,11... | collective-permute-start | bytes 4325384 | tf_op jit(solution)/shard_map/ppermute | solution.py:1062
  177.0 10.8 %collective-permute-start.14 = (f32[2816,128]{1,0:T(8,128)S(1)}, f32[2816,128]{1,0:T(8,128)S(1)}, u32[]{:S(2)}, u32[]{:S(2)}) collective-permute-start(f32[2816,128]{1,0:T(8,128)S(1)} %double_x1.1.refs_0_), channel_id=1, source_target_pairs={{0,1},{1,0},{2,3},{3,2},{4,5},{5,4},{6,7},{7,6},{8,9},{9,8},{10,11... | collective-permute-start | bytes 4325384 | tf_op jit(solution)/shard_map/ppermute | solution.py:1062
  179.7 8.1 %collective-permute-start.38 = (f32[2816,128]{1,0:T(8,128)S(1)}, f32[2816,128]{1,0:T(8,128)S(1)}, u32[]{:S(2)}, u32[]{:S(2)}) collective-permute-start(f32[2816,128]{1,0:T(8,128)S(1)} %collective-permute-done.37.refs_5_), channel_id=1, source_target_pairs={{0,1},{1,0},{2,3},{3,2},{4,5},{5,4},{6,7},{7,6},{8,9},{9,8},{10,11... | collective-permute-start | bytes 4325384 | tf_op jit(solution)/shard_map/ppermute | solution.py:1062
  180.0 7.8 %collective-permute-start.36 = (f32[2816,128]{1,0:T(8,128)S(1)}, f32[2816,128]{1,0:T(8,128)S(1)}, u32[]{:S(2)}, u32[]{:S(2)}) collective-permute-start(f32[2816,128]{1,0:T(8,128)S(1)} %collective-permute-done.35.refs_4_), channel_id=1, source_target_pairs={{0,1},{1,0},{2,3},{3,2},{4,5},{5,4},{6,7},{7,6},{8,9},{9,8},{10,11... | collective-permute-start | bytes 4325384 | tf_op jit(solution)/shard_map/ppermute | solution.py:1062
  182.5 6.2 %collective-permute-start.34 = (f32[2816,128]{1,0:T(8,128)S(1)}, f32[2816,128]{1,0:T(8,128)S(1)}, u32[]{:S(2)}, u32[]{:S(2)}) collective-permute-start(f32[2816,128]{1,0:T(8,128)S(1)} %collective-permute-done.33.refs_3_), channel_id=1, source_target_pairs={{0,1},{1,0},{2,3},{3,2},{4,5},{5,4},{6,7},{7,6},{8,9},{9,8},{10,11... | collective-permute-start | bytes 4325384 | tf_op jit(solution)/shard_map/ppermute | solution.py:1062
  (10 other events, 99.5 us)
